TPU v7x, 128 devices: a whole 4x4x4 slice. The times are simulated.
128 devices in a mesh: dp: 4 (over x), shard: 32 (over y, z, core).
Axes of the slice: x: 4, y: 4, z: 4, core: 2. Of those that a mesh axis runs over, the one named last changes fastest.
Arguments:
- grads: bfloat16 [4, 192, 512, 512], P('dp', None, 'shard'), may hold values from -0.59765625 to 0.59765625
- owner_table: int32 [4, 48, 1], replicated, may hold values from 0 to 31; in each aligned block of 48 rows (0 to 47, 48 to 95, ..., all dimensions but the last counted through in order) at most 3 rows name the same one
- momentum: float32 [384, 512, 512], P(('dp', 'shard')), may hold values from -1.2 to 1.2
- variance: float32 [384, 512, 512], P(('dp', 'shard')), may hold values from 0.01 to 0.1
- left_factor: bfloat16 [384, 512, 512], P(('dp', 'shard')), may hold values from -6 to 6
- right_factor: bfloat16 [384, 512, 512], P(('dp', 'shard')), may hold values from -6 to 6
- left_basis: bfloat16 [384, 512, 512], P(('dp', 'shard')), may hold values from -0.25 to 0.25
- right_basis: bfloat16 [384, 512, 512], P(('dp', 'shard')), may hold values from -0.25 to 0.25
Outputs:
- update: bfloat16 [192, 512, 512], P('dp', 'shard')
- new_momentum: float32 [384, 512, 512], P(('dp', 'shard'))
- new_variance: float32 [384, 512, 512], P(('dp', 'shard'))
- new_left_factor: bfloat16 [384, 512, 512], P(('dp', 'shard'))
- new_right_factor: bfloat16 [384, 512, 512], P(('dp', 'shard'))
Inputs may be any that keep to these rules, and one draw needn't show every extreme that they name: `owner_table`: within the 48 blocks of one group no owner is named by more than 3 blocks, and in some group an owner is named by exactly 3.
All inputs are finite; a program needn't handle non-finite values.
Results may differ from a plain program's by a relative error of at most 0.013.
Values may be sent and summed in bfloat16 or wider, within the bound.
No kernel may reach another device: no remote copies, remote signals or barrier semaphores. Data moves between devices by JAX's collectives and lax.ppermute only.
A program may use at most 128 MiB of HBM per device.

v0:
```python
import jax
import jax.numpy as jnp
from jax import lax
from jax.sharding import PartitionSpec as P

beta_moment = 0.95
beta_second = 0.95
beta_factor = 0.95
epsilon = 1e-08


def owner_ranks(owners, owner_count):
    ident = jnp.arange(owner_count, dtype=jnp.int32)
    onehot = (owners[:, None] == ident[None, :]).astype(jnp.int32)
    before = jnp.cumsum(onehot, axis=0) - onehot
    return jnp.sum(before * onehot, axis=1)


def pick_table(owners, ranks, owner_count, capacity):
    block_count = owners.shape[0]
    blocks = jnp.arange(block_count, dtype=jnp.int32)
    slot_ids = jnp.arange(capacity, dtype=jnp.int32)
    owner_ids = jnp.arange(owner_count, dtype=jnp.int32)
    match = (ranks[None, None, :] == slot_ids[:, None, None]) & (
        owners[None, None, :] == owner_ids[None, :, None]
    )
    picked = jnp.sum(jnp.where(match, blocks[None, None, :], 0), axis=2)
    present = jnp.any(match, axis=2)
    return jnp.where(present, picked, block_count)


def owner_work(gathered, momentum, variance, left_basis, right_basis):
    moment = beta_moment * momentum + (1.0 - beta_moment) * gathered.astype(jnp.float32)
    paired = jnp.stack([gathered, moment.astype(jnp.bfloat16)])
    turned = jnp.einsum(
        "cki,sckj->scij", left_basis, paired, preferred_element_type=jnp.float32
    ).astype(jnp.bfloat16)
    rotated = jnp.einsum("scij,cjk->scik", turned, right_basis, preferred_element_type=jnp.float32)
    second = beta_second * variance + (1.0 - beta_second) * rotated[0] * rotated[0]
    direction = (rotated[1] / (jnp.sqrt(second) + epsilon)).astype(jnp.bfloat16)
    back_half = jnp.einsum(
        "cij,cjk->cik", left_basis, direction, preferred_element_type=jnp.float32
    ).astype(jnp.bfloat16)
    update = jnp.einsum(
        "cij,ckj->cik", back_half, right_basis, preferred_element_type=jnp.float32
    ).astype(jnp.bfloat16)
    return (moment, second, update)


def factor_work(gathered, left_factor, right_factor):
    outer_left = jnp.einsum("cik,cjk->cij", gathered, gathered, preferred_element_type=jnp.float32)
    outer_right = jnp.einsum("cki,ckj->cij", gathered, gathered, preferred_element_type=jnp.float32)
    new_left = (
        beta_factor * left_factor.astype(jnp.float32) + (1.0 - beta_factor) * outer_left
    ).astype(jnp.bfloat16)
    new_right = (
        beta_factor * right_factor.astype(jnp.float32) + (1.0 - beta_factor) * outer_right
    ).astype(jnp.bfloat16)
    return (new_left, new_right)


def send_back(update):
    return lax.all_to_all(update, "shard", split_axis=1, concat_axis=1, tiled=True)


def body(
    grads, owner_table, momentum, variance, left_factor, right_factor, left_basis, right_basis
):
    owner_count = lax.axis_size("shard")
    group_index = lax.axis_index("dp")
    own_index = lax.axis_index("shard")
    capacity = momentum.shape[0]
    owners_all = owner_table[:, :, 0]
    ranks_all = jax.vmap(lambda row: owner_ranks(row, owner_count))(owners_all)
    owners = lax.dynamic_index_in_dim(owners_all, group_index, 0, keepdims=False)
    ranks = lax.dynamic_index_in_dim(ranks_all, group_index, 0, keepdims=False)
    local = grads[0]
    slab_rows = local.shape[1]
    width = local.shape[2]
    reduced = lax.psum_scatter(
        local.astype(jnp.float32).astype(jnp.bfloat16), "dp", scatter_dimension=0, tiled=True
    )
    picks = pick_table(owners, ranks, owner_count, capacity)
    padded = jnp.concatenate([reduced, jnp.zeros((1, slab_rows, width), reduced.dtype)], axis=0)
    outgoing = jnp.take(padded, picks.reshape(-1), axis=0).reshape(
        capacity, owner_count * slab_rows, width
    )
    gathered = lax.all_to_all(outgoing, "shard", split_axis=1, concat_axis=1, tiled=True)
    load = jnp.sum((owners == own_index).astype(jnp.int32))
    live = (jnp.arange(capacity, dtype=jnp.int32) < load)[:, None, None]
    new_left, new_right = factor_work(gathered, left_factor, right_factor)
    moment, second, update = owner_work(gathered, momentum, variance, left_basis, right_basis)
    returned = send_back(update)
    flat = returned.reshape(capacity * owner_count, slab_rows, width)
    update_rows = jnp.take(flat, ranks * owner_count + owners, axis=0)
    new_momentum = jnp.where(live, moment, momentum)
    new_variance = jnp.where(live, second, variance)
    new_left_factor = jnp.where(live, new_left, left_factor)
    new_right_factor = jnp.where(live, new_right, right_factor)
    return (update_rows, new_momentum, new_variance, new_left_factor, new_right_factor)


def solution(mesh):
    return jax.shard_map(
        body,
        mesh=mesh,
        in_specs=(
            P("dp", None, "shard", None),
            P(),
            P(("dp", "shard"), None, None),
            P(("dp", "shard"), None, None),
            P(("dp", "shard"), None, None),
            P(("dp", "shard"), None, None),
            P(("dp", "shard"), None, None),
            P(("dp", "shard"), None, None),
        ),
        out_specs=(
            P("dp", "shard", None),
            P(("dp", "shard"), None, None),
            P(("dp", "shard"), None, None),
            P(("dp", "shard"), None, None),
            P(("dp", "shard"), None, None),
        ),
        check_vma=False,
    )
```

profile of v0, /device:TPU:1, one launch (start us, length us, event | category | flops | bytes accessed | tf_op | source)
XLA Modules:
  0.0 170.6 jit_solution(7947792548060409607)
XLA Ops:
  7.2 0.0 copy-start
  7.2 0.0 copy-start.3
  7.2 0.0 reduce-scatter.2.cloned.1.call-start
  7.2 0.7 reduce-scatter.2.cloned.1.call-update
  7.9 0.1 copy-done.3
  8.0 0.1 fusion.27
  8.1 0.1 reduce_window_sum.11
  8.2 0.6 fusion.29
  8.8 0.2 select_reduce_fusion
  9.1 0.1 and_reduce_fusion
  9.2 0.2 fusion.28
  9.4 0.1 select_n.88
  9.5 0.1 broadcast_in_dim.72
  9.6 0.1 broadcast_in_dim.73
  9.7 42.2 %reduce-scatter.2.cloned.1.call-done = bf16[48,16,512]{2,1,0:T(8,128)(2,1)} async-done(((bf16[192,16,512]{2,1,0:T(8,128)(2,1)}), bf16[48,16,512]{2,1,0:T(8,128)(2,1)}) %reduce-scatter.2.cloned.1.call-update) | async-done | bytes 786448 | tf_op jit(solution)/shard_map/reduce_scatter | solution.py:80
  51.9 1.2 concatenate.3
  53.1 1.9 %gather_fusion = bf16[96,16,512]{2,1,0:T(8,128)(2,1)} fusion(bf16[49,16,512]{2,1,0:T(8,128)(2,1)S(1)} %concatenate.3, s32[1024]{0:T(1024)S(1)} %pad_clamp_fusion.1), kind=kCustom, calls=%fused_computation | custom fusion | bytes 3146112 | tf_op jit(solution)/shard_map/jit(_take)/gather | solution.py:85
  55.0 1.7 bitcast_select_fusion
  56.7 2.7 %copy.69 = bf16[3,512,512]{2,0,1:T(4,128)(2,1)} copy(bf16[3,512,512]{2,1,0:T(8,128)(2,1)S(1)} %bitcast_select_fusion) | data formatting | bytes 3145728 | tf_op jit(solution)/shard_map/jit(_take)/select_n | solution.py:85
  59.4 7.7 %all-to-all-start = ((bf16[3,512,512]{2,0,1:T(4,128)(2,1)}), bf16[3,512,512]{2,0,1:T(4,128)(2,1)}, u32[]{:S(2)}, u32[]{:S(2)}) async-start(bf16[3,512,512]{2,0,1:T(4,128)(2,1)} %copy.69), calls=%async_computation.1 | async-start | bytes 4194304 | tf_op jit(solution)/shard_map/all_to_all | solution.py:88
  67.1 3.6 %copy.75 = f32[3,512,512]{1,2,0:T(8,128)} copy(f32[3,512,512]{2,1,0:T(8,128)} %param.11) | data formatting | bytes 6291456 | tf_op args[3]
  70.7 3.5 %copy.71 = f32[3,512,512]{1,2,0:T(8,128)} copy(f32[3,512,512]{2,1,0:T(8,128)} %param.10) | data formatting | bytes 6291456 | tf_op args[2]
  74.2 0.6 iota_compare_fusion.3
  74.9 20.6 %all-to-all-done = bf16[3,512,512]{2,0,1:T(4,128)(2,1)} async-done(((bf16[3,512,512]{2,0,1:T(4,128)(2,1)}), bf16[3,512,512]{2,0,1:T(4,128)(2,1)}, u32[]{:S(2)}, u32[]{:S(2)}) %all-to-all-start) | async-done | bytes 1572896 | tf_op jit(solution)/shard_map/all_to_all | solution.py:88
  95.4 2.9 %copy.70 = bf16[3,512,512]{1,2,0:T(8,128)(2,1)S(1)} copy(bf16[3,512,512]{2,0,1:T(4,128)(2,1)} %all-to-all-done) | data formatting | bytes 3145728 | tf_op jit(solution)/shard_map/all_to_all | solution.py:88
  98.3 0.0 copy-start.4
  98.3 4.5 %fusion.9 = (f32[3,512,512]{1,2,0:T(8,128)}, bf16[1,3,512,512]{2,3,0,1:T(8,128)(2,1)S(1)}) fusion(f32[3,512,512]{1,2,0:T(8,128)} %copy.71, bf16[3,512,512]{1,2,0:T(8,128)(2,1)S(1)} %copy.70, pred[3]{0:T(512)(128)(4,1)S(1)} %iota_compare_fusion.3), kind=kLoop, calls=%fused_computation.18 | loop fusion | flops 4718592 | bytes 9437187 | tf_op jit(solution)/shard_map/jit(_where)/select_n | solution.py:96
  102.8 0.0 copy-done.4
  102.8 1.8 %convert_bitcast_fusion = bf16[2,3,512,512]{2,3,0,1:T(8,128)(2,1)S(1)} fusion(bf16[1,3,512,512]{2,3,0,1:T(8,128)(2,1)S(1)} %get-tuple-element.27, bf16[1,3,512,512]{2,3,0,1:T(8,128)(2,1)S(1)} %bitcast.60, bf16[3,512,512]{2,1,0:T(8,128)(2,1)S(1)} %copy-done.4), kind=kOutput, calls=%fused_computation.16 | convolution fusion | flops 1613758464 | bytes 7864320 | tf_op jit(solution)/shard_map/cki,sckj->scij/dot_general | solution.py:35
  104.6 0.0 copy-done
  104.6 4.5 %fusion.11 = f32[2,3,512,512]{2,3,1,0:T(8,128)} fusion(bf16[2,3,512,512]{2,3,0,1:T(8,128)(2,1)S(1)} %convert_bitcast_fusion, bf16[3,512,512]{2,1,0:T(8,128)(2,1)S(1)} %copy-done), kind=kOutput, calls=%fused_computation.20 | convolution fusion | flops 1610612736 | bytes 11010048 | tf_op jit(solution)/shard_map/scij,cjk->scik/dot_general | solution.py:38
  109.1 8.0 %convolution_convert_fusion = bf16[3,512,512]{2,1,0:T(8,128)(2,1)} fusion(bf16[3,512,512]{2,1,0:T(8,128)(2,1)S(1)} %copy-done, bf16[3,512,512]{2,1,0:T(8,128)(2,1)} %param.14, f32[2,3,512,512]{2,3,1,0:T(8,128)} %fusion.11, f32[3,512,512]{1,2,0:T(8,128)} %copy.75), kind=kOutput, calls=%fused_computation.24 | convolution fusion | flops 1617690624 | bytes 14155776 | tf_op jit(solution)/shard_map/cij,ckj->cik/dot_general | solution.py:44
  117.1 4.3 %copy.77 = bf16[3,512,512]{2,0,1:T(4,128)(2,1)} copy(bf16[3,512,512]{2,1,0:T(8,128)(2,1)} %convolution_convert_fusion) | data formatting | bytes 3145728 | tf_op jit(solution)/shard_map/convert_element_type | solution.py:46
  121.4 5.2 %all-to-all-start.1 = ((bf16[3,512,512]{2,0,1:T(4,128)(2,1)}), bf16[3,512,512]{2,0,1:T(4,128)(2,1)}, u32[]{:S(2)}, u32[]{:S(2)}) async-start(bf16[3,512,512]{2,0,1:T(4,128)(2,1)} %copy.77), calls=%async_computation.2 | async-start | bytes 4194304 | tf_op jit(solution)/shard_map/all_to_all | solution.py:63
  126.7 0.0 copy-done.2
  126.7 1.6 copy.81
  128.2 1.7 %copy.86 = bf16[3,512,512]{1,2,0:T(8,128)(2,1)S(1)} copy(bf16[3,512,512]{2,1,0:T(8,128)(2,1)} %param.13) | data formatting | bytes 3145728 | tf_op args[5]
  130.0 5.8 %fusion.14 = bf16[3,512,512]{1,2,0:T(8,128)(2,1)} fusion(bf16[3,512,512]{1,2,0:T(8,128)(2,1)} %copy.81, pred[3]{0:T(512)(128)(4,1)S(1)} %iota_compare_fusion.3, bf16[3,512,512]{2,0,1:T(4,128)(2,1)} %all-to-all-done), kind=kOutput, calls=%fused_computation.21 | convolution fusion | flops 810024960 | bytes 4718595 | tf_op jit(solution)/shard_map/cik,cjk->cij/dot_general | solution.py:51
  135.8 2.6 %copy.93 = bf16[3,512,512]{2,1,0:T(8,128)(2,1)} copy(bf16[3,512,512]{1,2,0:T(8,128)(2,1)} %fusion.14) | data formatting | bytes 3145728
  138.4 4.4 %fusion.15 = bf16[3,512,512]{1,2,0:T(8,128)(2,1)} fusion(bf16[3,512,512]{1,2,0:T(8,128)(2,1)S(1)} %copy.86, bf16[3,512,512]{1,2,0:T(8,128)(2,1)S(1)} %copy.70, pred[3]{0:T(512)(128)(4,1)S(1)} %iota_compare_fusion.3, bf16[3,512,512]{2,0,1:T(4,128)(2,1)} %all-to-all-done), kind=kOutput, calls=%fused_computation.22 | convolution fusion | flops 810024960 | bytes 6291459 | tf_op jit(solution)/shard_map/cki,ckj->cij/dot_general | solution.py:52
  142.7 2.6 %copy.94 = bf16[3,512,512]{2,1,0:T(8,128)(2,1)} copy(bf16[3,512,512]{1,2,0:T(8,128)(2,1)} %fusion.15) | data formatting | bytes 3145728
  145.3 3.5 %copy.91 = f32[3,512,512]{2,1,0:T(8,128)} copy(f32[3,512,512]{1,2,0:T(8,128)} %get-tuple-element.26) | data formatting | bytes 6291456
  148.9 5.5 %fusion.18 = f32[3,512,512]{1,2,0:T(8,128)} fusion(f32[3,512,512]{1,2,0:T(8,128)} %copy.75, f32[2,3,512,512]{2,3,1,0:T(8,128)} %fusion.11, pred[3]{0:T(512)(128)(4,1)S(1)} %iota_compare_fusion.3), kind=kLoop, calls=%fused_computation.23 | loop fusion | flops 3932160 | bytes 9437187 | tf_op jit(solution)/shard_map/jit(_where)/select_n | solution.py:97
  154.4 3.7 %copy.92 = f32[3,512,512]{2,1,0:T(8,128)} copy(f32[3,512,512]{1,2,0:T(8,128)} %fusion.18) | data formatting | bytes 6291456
  158.1 0.0 all-to-all-done.1
  158.1 2.0 %copy.78 = bf16[3,512,512]{2,1,0:T(8,128)(2,1)S(1)} copy(bf16[3,512,512]{2,0,1:T(4,128)(2,1)} %all-to-all-done.1) | data formatting | bytes 3145728 | tf_op jit(solution)/shard_map/all_to_all | solution.py:63
  160.0 1.5 gather_fusion.1
  161.6 2.2 %broadcast_select_fusion = bf16[48,16,512]{2,1,0:T(8,128)(2,1)} fusion(bf16[48,16,512]{2,1,0:T(8,128)(2,1)} %gather_fusion.1, pred[48]{0:T(512)(128)(4,1)S(1)} %get-tuple-element.22), kind=kLoop, calls=%fused_computation.32 | loop fusion | flops 393216 | bytes 1572912 | tf_op jit(solution)/shard_map/jit(_take)/select_n | solution.py:95
  (11 shorter events, 0.1 us)
Async XLA Ops:
  7.2 97.5 %copy-start = (bf16[3,512,512]{2,1,0:T(8,128)(2,1)S(1)}, bf16[3,512,512]{2,1,0:T(8,128)(2,1)}, u32[]{:S(2)}) copy-start(bf16[3,512,512]{2,1,0:T(8,128)(2,1)} %param.15) | copy-start | bytes 4718596
  7.2 0.8 copy-start.3
  7.2 44.7 %reduce-scatter.2.cloned.1.call-start = ((), (), s32[]{:S(2)}) async-start(), calls=%async_computation.3 | async-start | bytes 3932160 | tf_op jit(solution)/shard_map/reduce_scatter | solution.py:80
  59.4 36.1 %all-to-all-start = ((bf16[3,512,512]{2,0,1:T(4,128)(2,1)}), bf16[3,512,512]{2,0,1:T(4,128)(2,1)}, u32[]{:S(2)}, u32[]{:S(2)}) async-start(bf16[3,512,512]{2,0,1:T(4,128)(2,1)} %copy.69), calls=%async_computation.1 | async-start | bytes 4194304 | tf_op jit(solution)/shard_map/all_to_all | solution.py:88
  98.3 4.5 %copy-start.4 = (bf16[3,512,512]{2,1,0:T(8,128)(2,1)S(1)}, bf16[3,512,512]{2,1,0:T(8,128)(2,1)}, u32[]{:S(2)}) copy-start(bf16[3,512,512]{2,1,0:T(8,128)(2,1)} %param.14) | copy-start | bytes 4718596
  117.1 9.5 %copy-start.2 = (bf16[3,512,512]{2,1,0:T(8,128)(2,1)S(1)}, bf16[3,512,512]{2,1,0:T(8,128)(2,1)}, u32[]{:S(2)}) copy-start(bf16[3,512,512]{2,1,0:T(8,128)(2,1)} %param.12) | copy-start | bytes 4718596
  121.4 36.6 %all-to-all-start.1 = ((bf16[3,512,512]{2,0,1:T(4,128)(2,1)}), bf16[3,512,512]{2,0,1:T(4,128)(2,1)}, u32[]{:S(2)}, u32[]{:S(2)}) async-start(bf16[3,512,512]{2,0,1:T(4,128)(2,1)} %copy.77), calls=%async_computation.2 | async-start | bytes 4194304 | tf_op jit(solution)/shard_map/all_to_all | solution.py:63
  154.4 9.3 %copy-start.1 = (bf16[3,512,512]{2,1,0:T(8,128)(2,1)S(1)}, bf16[3,512,512]{2,1,0:T(8,128)(2,1)}, u32[]{:S(2)}) copy-start(bf16[3,512,512]{2,1,0:T(8,128)(2,1)} %param.15) | copy-start | bytes 4718596
Sparse Core Ops, SparseCore 0:
  10.4 41.4 reduce-scatter.1
where the time goes:
time: 171 us
  waiting for transfers between devices  63.5 us (37%)
  local copies, waits for them, and re-layouts  39.5 us (23%)
  matrix products  24.5 us (14%)
  other arithmetic  15.9 us (9%)
  between operations  14.2 us (8%)
  starting transfers between devices  13 us (8%)
    reduce_scatter x1, waiting for transfers between devices, body(): lax.psum_scatter(local.astype(jnp.float32).astype(jnp.bfloat16), 'dp', sc...  42.2 us
    unnamed x18, local copies, waits for them, and re-layouts  22.8 us
    all_to_all x1, waiting for transfers between devices, body(): lax.all_to_all(outgoing, 'shard', split_axis=1, concat_axis=1, tiled=True)  20.6 us
    dot_general x1, matrix products, owner_work(): jnp.einsum('cij,ckj->cik', back_half, right_basis, preferred_element_type...  8 us
    all_to_all x1, starting transfers between devices, body(): lax.all_to_all(outgoing, 'shard', split_axis=1, concat_axis=1, tiled=True)  7.72 us
    dot_general x1, matrix products, factor_work(): jnp.einsum('cik,cjk->cij', gathered, gathered, preferred_element_type=jnp...  5.8 us
    select_n x1, other arithmetic, body(): new_variance = jnp.where(live, second, variance)  5.53 us
    all_to_all x1, starting transfers between devices, send_back(): lax.all_to_all(update, 'shard', split_axis=1, concat_axis=1, tiled=True)  5.22 us
  transfers between devices with their start and end apart: 3, of which 2 were waited for; matrix products, arithmetic and copies ran while one was open for 24% of the time, Pallas kernels for 0%

commit v1 on v0

v1 whole, which is shorter than its diff:
```python
import functools

import jax
import jax.numpy as jnp
from jax import lax
from jax.experimental import pallas as pl
from jax.experimental.pallas import tpu as pltpu
from jax.sharding import PartitionSpec as P

beta_moment = 0.95
beta_second = 0.95
beta_factor = 0.95
epsilon = 1e-08

F32 = jnp.float32
BF16 = jnp.bfloat16
VMEM_LIMIT = 40 * 1024 * 1024


def dot_nn(a, b):
    return lax.dot_general(a, b, (((1,), (0,)), ((), ())), preferred_element_type=F32)


def dot_tn(a, b):
    return lax.dot_general(a, b, (((0,), (0,)), ((), ())), preferred_element_type=F32)


def dot_nt(a, b):
    return lax.dot_general(a, b, (((1,), (1,)), ((), ())), preferred_element_type=F32)


def owner_ranks(owners):
    count = owners.shape[0]
    places = jnp.arange(count, dtype=jnp.int32)
    same = (owners[:, None] == owners[None, :]) & (places[None, :] < places[:, None])
    return jnp.sum(same.astype(jnp.int32), axis=1)


def place_kernel(place_ref, group_ref, own_ref, a_ref, b_ref, c_ref, out_ref):
    del group_ref

    def step(j, carry):
        total = own_ref[j].astype(F32) + a_ref[j].astype(F32)
        total = total + (b_ref[j].astype(F32) + c_ref[j].astype(F32))
        out_ref[place_ref[j]] = total.astype(BF16)
        return carry

    lax.fori_loop(0, a_ref.shape[0], step, 0, unroll=4)


def sum_and_place(local, parts, place, group, slots):
    count, rows, width = parts[0].shape
    block = (count, rows, width)
    whole = pl.BlockSpec(block, lambda i, place, group: (0, 0, 0))
    return pl.pallas_call(
        place_kernel,
        out_shape=jax.ShapeDtypeStruct((slots, rows, width), BF16),
        grid_spec=pltpu.PrefetchScalarGridSpec(
            num_scalar_prefetch=2,
            grid=(1,),
            in_specs=[
                pl.BlockSpec(block, lambda i, place, group: (group[0], 0, 0)),
                whole,
                whole,
                whole,
            ],
            out_specs=pl.BlockSpec((slots, rows, width), lambda i, place, group: (0, 0, 0)),
        ),
        compiler_params=pltpu.CompilerParams(vmem_limit_bytes=VMEM_LIMIT),
        cost_estimate=pl.CostEstimate(
            flops=4 * count * rows * width, bytes_accessed=14 * count * rows * width, transcendentals=0
        ),
        name="sum_and_place",
    )(place, group, local, *parts)


def step_kernel(
    load_ref, grad_ref, mom_ref, var_ref, left_ref, right_ref, mom_out, var_out, upd_out
):
    slot = pl.program_id(0)
    live = slot < load_ref[0]
    size = left_ref.shape[1]

    @pl.when(live)
    def _():
        grad = grad_ref[...].reshape(size, size)
        left = left_ref[0]
        right = right_ref[0]
        moment = beta_moment * mom_ref[0] + (1.0 - beta_moment) * grad.astype(F32)
        mom_out[0] = moment
        turned_grad = dot_tn(left, grad).astype(BF16)
        turned_moment = dot_tn(left, moment.astype(BF16)).astype(BF16)
        rotated = dot_nn(turned_grad, right)
        second = beta_second * var_ref[0] + (1.0 - beta_second) * rotated * rotated
        var_out[0] = second
        rotated_moment = dot_nn(turned_moment, right)
        direction = (rotated_moment / (jnp.sqrt(second) + epsilon)).astype(BF16)
        back_half = dot_nn(left, direction).astype(BF16)
        update = dot_nt(back_half, right).astype(BF16)
        upd_out[...] = update.reshape(upd_out.shape)

    @pl.when(jnp.logical_not(live))
    def _():
        mom_out[...] = mom_ref[...]
        var_out[...] = var_ref[...]


def owner_step(load, grad, momentum, variance, left_basis, right_basis):
    slots, size, _ = momentum.shape
    owners, _, rows, _ = grad.shape
    square = pl.BlockSpec((1, size, size), lambda s, load: (s, 0, 0))
    slab = pl.BlockSpec((owners, 1, rows, size), lambda s, load: (0, s, 0, 0))
    return pl.pallas_call(
        step_kernel,
        out_shape=(
            jax.ShapeDtypeStruct(momentum.shape, F32),
            jax.ShapeDtypeStruct(variance.shape, F32),
            jax.ShapeDtypeStruct(grad.shape, BF16),
        ),
        grid_spec=pltpu.PrefetchScalarGridSpec(
            num_scalar_prefetch=1,
            grid=(slots,),
            in_specs=[slab, square, square, square, square],
            out_specs=[square, square, slab],
        ),
        compiler_params=pltpu.CompilerParams(vmem_limit_bytes=VMEM_LIMIT),
        cost_estimate=pl.CostEstimate(
            flops=12 * slots * size**3, bytes_accessed=20 * slots * size**2, transcendentals=slots * size**2
        ),
        name="owner_step",
    )(load, grad, momentum, variance, left_basis, right_basis)


def factor_kernel(load_ref, grad_ref, left_ref, right_ref, left_out, right_out):
    slot = pl.program_id(0)
    live = slot < load_ref[0]
    size = left_ref.shape[1]

    @pl.when(live)
    def _():
        grad = grad_ref[...].reshape(size, size)
        left_out[0] = (
            beta_factor * left_ref[0].astype(F32) + (1.0 - beta_factor) * dot_nt(grad, grad)
        ).astype(BF16)
        right_out[0] = (
            beta_factor * right_ref[0].astype(F32) + (1.0 - beta_factor) * dot_tn(grad, grad)
        ).astype(BF16)

    @pl.when(jnp.logical_not(live))
    def _():
        left_out[...] = left_ref[...]
        right_out[...] = right_ref[...]


def factor_step(load, grad, left_factor, right_factor):
    slots, size, _ = left_factor.shape
    owners, _, rows, _ = grad.shape
    square = pl.BlockSpec((1, size, size), lambda s, load: (s, 0, 0))
    slab = pl.BlockSpec((owners, 1, rows, size), lambda s, load: (0, s, 0, 0))
    return pl.pallas_call(
        factor_kernel,
        out_shape=(
            jax.ShapeDtypeStruct(left_factor.shape, BF16),
            jax.ShapeDtypeStruct(right_factor.shape, BF16),
        ),
        grid_spec=pltpu.PrefetchScalarGridSpec(
            num_scalar_prefetch=1,
            grid=(slots,),
            in_specs=[slab, square, square],
            out_specs=[square, square],
        ),
        compiler_params=pltpu.CompilerParams(vmem_limit_bytes=VMEM_LIMIT),
        cost_estimate=pl.CostEstimate(
            flops=4 * slots * size**3, bytes_accessed=10 * slots * size**2, transcendentals=0
        ),
        name="factor_step",
    )(load, grad, left_factor, right_factor)


def body(
    grads, owner_table, momentum, variance, left_factor, right_factor, left_basis, right_basis
):
    owner_count = lax.axis_size("shard")
    replicas = lax.axis_size("dp")
    group_index = lax.axis_index("dp")
    own_index = lax.axis_index("shard")
    capacity = momentum.shape[0]
    local = grads[0]
    blocks, rows, width = local.shape
    per_group = blocks // replicas

    owners = lax.dynamic_index_in_dim(owner_table[:, :, 0], group_index, 0, keepdims=False)
    place = owners * capacity + owner_ranks(owners)
    load = jnp.sum((owners == own_index).astype(jnp.int32)).reshape(1)

    parts = []
    for hop in (2, 1, 3):
        target = lax.rem(group_index + hop, replicas)
        chunk = lax.dynamic_slice_in_dim(local, target * per_group, per_group, 0)
        parts.append(
            lax.ppermute(chunk, "dp", [(i, (i + hop) % replicas) for i in range(replicas)])
        )
    outgoing = sum_and_place(
        local, parts, place, group_index.reshape(1), owner_count * capacity
    ).reshape(owner_count, capacity, rows, width)
    gathered = lax.all_to_all(outgoing, "shard", split_axis=0, concat_axis=0, tiled=True)
    new_momentum, new_variance, update = owner_step(
        load, gathered, momentum, variance, left_basis, right_basis
    )
    returned = lax.all_to_all(update, "shard", split_axis=0, concat_axis=0, tiled=True)
    new_left, new_right = factor_step(load, gathered, left_factor, right_factor)
    flat = returned.reshape(owner_count * capacity, rows, width)
    update_rows = jnp.take(flat, place, axis=0, mode="clip")
    return (update_rows, new_momentum, new_variance, new_left, new_right)


def solution(mesh):
    state = P(("dp", "shard"), None, None)
    return jax.shard_map(
        body,
        mesh=mesh,
        in_specs=(P("dp", None, "shard", None), P(), state, state, state, state, state, state),
        out_specs=(P("dp", "shard", None), state, state, state, state),
        check_vma=False,
    )
```

time: 171 us -> 115 us (0.67)
  local copies, waits for them, and re-layouts: 39.5 us -> 7.58 us
  blocking collectives: 0 us -> 31.8 us
  matrix products: 24.5 us -> 0 us
  waiting for transfers between devices: 63.5 us -> 46.7 us
  Pallas kernels: 0 us -> 15.5 us
  other arithmetic: 15.9 us -> 0.9 us
  between operations: 14.2 us -> 0.77 us
  starting transfers between devices: 13 us -> 10.9 us
    reduce_scatter x1 -> x0, waiting for transfers between devices: 42.2 us -> none  [body(): lax.psum_scatter(local.astype(jnp.float32).astype(jnp.bfloat16), 'dp', sc...]
    all_to_all x0 -> x1, blocking collectives: none -> 31.8 us  [body(): lax.all_to_all(outgoing, 'shard', split_axis=0, concat_axis=0, tiled=True)]
    ppermute x0 -> x3, waiting for transfers between devices: none -> 31.6 us  [body(): lax.ppermute(chunk, 'dp', [(i, (i + hop) % replicas) for i in range(repli...]
    dot_general x5 -> x0, matrix products: 24.5 us -> none  [the longest x1 8 us: owner_work(): jnp.einsum('cij,ckj->cik', back_half, right_basis, preferred_element_type...]
    unnamed x18 -> x16, local copies, waits for them, and re-layouts: 22.8 us -> 1.44 us
    pallas_call x0 -> x3, Pallas kernels: none -> 15.5 us  [the longest x1 8.47 us: owner_step(): pl.pallas_call(step_kernel, out_shape=(jax.ShapeDtypeStruct(momentum.shap...]
    select_n x6 -> x0, other arithmetic: 13.9 us -> none  [the longest x1 5.53 us: body(): new_variance = jnp.where(live, second, variance)]
    all_to_all x2 -> x1, starting transfers between devices: 12.9 us -> 4.62 us  [body(): lax.all_to_all(update, 'shard', split_axis=0, concat_axis=0, tiled=True)]
  transfers between devices with their start and end apart: 3 -> 4, of which waited for: 2 -> 3; matrix products, arithmetic and copies ran while one was open for 24% -> 1% of each run, Pallas kernels for 0% -> 4%
where the time goes in v1:
time: 115 us; the launch traced here: 114 us
  waiting for transfers between devices  46.7 us (41%)
  blocking collectives  31.8 us (28%)
  Pallas kernels  15.5 us (13%)
  starting transfers between devices  10.9 us (9%)
  local copies, waits for them, and re-layouts  7.58 us (7%)
    all_to_all x1, blocking collectives, body(): lax.all_to_all(outgoing, 'shard', split_axis=0, concat_axis=0, tiled=True)  31.8 us
    ppermute x3, waiting for transfers between devices, body(): lax.ppermute(chunk, 'dp', [(i, (i + hop) % replicas) for i in range(repli...  31.6 us
    all_to_all x1, waiting for transfers between devices, body(): lax.all_to_all(update, 'shard', split_axis=0, concat_axis=0, tiled=True)  15.1 us
    pallas_call x1, Pallas kernels, owner_step(): pl.pallas_call(step_kernel, out_shape=(jax.ShapeDtypeStruct(momentum.shap...  8.47 us
    ppermute x3, starting transfers between devices, body(): lax.ppermute(chunk, 'dp', [(i, (i + hop) % replicas) for i in range(repli...  6.25 us
    all_to_all x1, starting transfers between devices, body(): lax.all_to_all(update, 'shard', split_axis=0, concat_axis=0, tiled=True)  4.62 us
    pallas_call x1, Pallas kernels, factor_step(): pl.pallas_call(factor_kernel, out_shape=(jax.ShapeDtypeStruct(left_factor...  4.21 us
    dynamic_slice x1, local copies, waits for them, and re-layouts, body(): chunk = lax.dynamic_slice_in_dim(local, target * per_group, per_group, 0)  3.21 us
  transfers between devices with their start and end apart: 4, of which 3 were waited for; matrix products, arithmetic and copies ran while one was open for 1% of the time, Pallas kernels for 4%

profile of v1, /device:TPU:1, one launch (start us, length us, event | category | flops | bytes accessed | tf_op | source)
XLA Modules:
  0.0 114.1 jit_solution(6827678500162793807)
XLA Ops:
  0.7 0.0 copy-start.7
  0.7 0.0 copy-start
  0.7 3.2 %dynamic-slice_bitcast_fusion = (bf16[48,16,512]{2,1,0:T(8,128)(2,1)}, bf16[48,16,512]{2,1,0:T(8,128)(2,1)}, bf16[48,16,512]{2,1,0:T(8,128)(2,1)}) fusion(bf16[1,192,16,512]{3,2,1,0:T(8,128)(2,1)} %param.8, s32[]{:T(128)S(6)} %select_n.16, s32[]{:T(128)S(6)} %select_n.14, s32[]{:T(128)S(6)} %select_n.15), kind=kLoop, calls=%fused_computation.1 | loop fusion | bytes 4718604 | tf_op jit(solution)/shard_map/dynamic_slice | solution.py:199
  3.9 3.6 %collective-permute-start = (bf16[48,16,512]{2,1,0:T(8,128)(2,1)}, bf16[48,16,512]{2,1,0:T(8,128)(2,1)}, u32[]{:S(2)}, u32[]{:S(2)}) collective-permute-start(bf16[48,16,512]{2,1,0:T(8,128)(2,1)} %get-tuple-element.18), channel_id=1, source_target_pairs={{0,64},{32,96},{64,0},{96,32},{1,65},{33,97},{65,1},{97,33},{2,66}... | collective-permute-start | bytes 2359304 | tf_op jit(solution)/shard_map/ppermute | solution.py:201
  7.5 0.3 collective-permute-start.1
  7.8 2.4 %collective-permute-start.2 = (bf16[48,16,512]{2,1,0:T(8,128)(2,1)}, bf16[48,16,512]{2,1,0:T(8,128)(2,1)}, u32[]{:S(2)}, u32[]{:S(2)}) collective-permute-start(bf16[48,16,512]{2,1,0:T(8,128)(2,1)} %get-tuple-element.17), channel_id=1, source_target_pairs={{0,96},{32,0},{64,32},{96,64},{1,97},{33,1},{65,33},{97,65},{2,98}... | collective-permute-start | bytes 2359304 | tf_op jit(solution)/shard_map/ppermute | solution.py:201
  10.1 0.0 copy-done.7
  10.1 0.7 fusion.1
  10.8 0.2 convert_reduce_fusion
  11.0 13.6 %collective-permute-done.a_ref = bf16[48,16,512]{2,1,0:T(8,128)(2,1)} collective-permute-done((bf16[48,16,512]{2,1,0:T(8,128)(2,1)}, bf16[48,16,512]{2,1,0:T(8,128)(2,1)}, u32[]{:S(2)}, u32[]{:S(2)}) %collective-permute-start) | collective-permute-done | bytes 786464 | tf_op jit(solution)/shard_map/ppermute | solution.py:201
  24.6 18.0 %collective-permute-done.1.b_ref = bf16[48,16,512]{2,1,0:T(8,128)(2,1)} collective-permute-done((bf16[48,16,512]{2,1,0:T(8,128)(2,1)}, bf16[48,16,512]{2,1,0:T(8,128)(2,1)}, u32[]{:S(2)}, u32[]{:S(2)}) %collective-permute-start.1) | collective-permute-done | bytes 786464 | tf_op jit(solution)/shard_map/ppermute | solution.py:201
  42.6 0.0 collective-permute-done.2.c_ref
  42.6 0.0 copy-done
  42.6 0.0 copy-start.2
  42.6 0.0 copy-start.3
  42.7 0.0 copy-start.4
  42.7 2.9 %sum_and_place.1 = bf16[96,16,512]{2,1,0:T(8,128)(2,1)S(1)} custom-call(s32[48]{0:T(128)S(1)} %multiply_add_fusion.place_ref, s32[1]{0:T(128)} %bitcast.2.group_ref, bf16[192,16,512]{2,1,0:T(8,128)(2,1)S(1)} %bitcast.22, bf16[48,16,512]{2,1,0:T(8,128)(2,1)} %collective-permute-done.a_ref, bf16[48,16,512]{2,1,0:T(8,128)(2,1)} %collective-permute-done.1.b_ref, ...), custom_call_target="tpu_custom_call" | custom-call | flops 1572864 | bytes 5505024 | tf_op jit(solution)/shard_map/sum_and_place/pallas_call | solution.py:55
  45.5 0.0 copy-start.1
  45.5 31.8 %all_to_all.10.grad_ref = bf16[32,3,16,512]{3,2,1,0:T(8,128)(2,1)S(1)} all-to-all(bf16[32,3,16,512]{3,2,1,0:T(8,128)(2,1)S(1)} %bitcast.23), channel_id=1, replica_groups=mesh['dp'=4,'shard'=32] {'shard'}, dimensions={0} | all-to-all | bytes 3145728 | tf_op jit(solution)/shard_map/all_to_all | solution.py:206
  77.4 0.0 copy-done.2
  77.4 0.0 copy-done.3
  77.4 0.0 copy-done.4
  77.4 0.0 copy-done.1
  77.4 8.5 %owner_step.1 = (f32[3,512,512]{2,1,0:T(8,128)}, f32[3,512,512]{2,1,0:T(8,128)}, bf16[32,3,16,512]{3,2,1,0:T(8,128)(2,1)}) custom-call(s32[1]{0:T(128)} %bitcast.1.load_ref, bf16[32,3,16,512]{3,2,1,0:T(8,128)(2,1)S(1)} %all_to_all.10.grad_ref, f32[3,512,512]{2,1,0:T(8,128)S(1)} %copy-done.1, f32[3,512,512]{2,1,0:T(8,128)S(1)} %copy-done.2, ...), custom_call_target="tpu_custom_call" | custom-call | flops 4831838208 | bytes 15728640 | tf_op jit(solution)/shard_map/owner_step/pallas_call | solution.py:113
  85.9 0.0 copy-start.5
  85.9 4.6 %all-to-all-start.1 = ((bf16[32,3,16,512]{3,2,1,0:T(8,128)(2,1)}), bf16[32,3,16,512]{3,2,1,0:T(8,128)(2,1)}, u32[]{:S(2)}, u32[]{:S(2)}) async-start(bf16[32,3,16,512]{3,2,1,0:T(8,128)(2,1)} %get-tuple-element.10), calls=%async_computation.1 | async-start | bytes 3145728 | tf_op jit(solution)/shard_map/all_to_all | solution.py:210
  90.5 0.0 copy-done.5
  90.5 0.0 copy-start.6
  90.6 1.4 %copy-done.6 = bf16[3,512,512]{2,1,0:T(8,128)(2,1)S(1)} copy-done((bf16[3,512,512]{2,1,0:T(8,128)(2,1)S(1)}, bf16[3,512,512]{2,1,0:T(8,128)(2,1)}, u32[]{:S(2)}) %copy-start.6) | copy-done | bytes 1572888
  92.0 4.2 %factor_step.1 = (bf16[3,512,512]{2,1,0:T(8,128)(2,1)}, bf16[3,512,512]{2,1,0:T(8,128)(2,1)}) custom-call(s32[1]{0:T(128)} %bitcast.1.load_ref, bf16[32,3,16,512]{3,2,1,0:T(8,128)(2,1)S(1)} %all_to_all.10.grad_ref, bf16[3,512,512]{2,1,0:T(8,128)(2,1)S(1)} %copy-done.5, bf16[3,512,512]{2,1,0:T(8,128)(2,1)S(1)} %copy-done.6), custom_call_target="tpu_custom_call" | custom-call | flops 1610612736 | bytes 7864320 | tf_op jit(solution)/shard_map/factor_step/pallas_call | solution.py:160
  96.2 15.1 %all-to-all-done.1 = bf16[32,3,16,512]{3,2,1,0:T(8,128)(2,1)} async-done(((bf16[32,3,16,512]{3,2,1,0:T(8,128)(2,1)}), bf16[32,3,16,512]{3,2,1,0:T(8,128)(2,1)}, u32[]{:S(2)}, u32[]{:S(2)}) %all-to-all-start.1) | async-done | bytes 1572896 | tf_op jit(solution)/shard_map/all_to_all | solution.py:210
  111.2 2.9 %gather_fusion = bf16[48,16,512]{2,1,0:T(8,128)(2,1)} fusion(bf16[96,16,512]{2,1,0:T(8,128)(2,1)} %bitcast.8, s32[1024]{0:T(1024)S(1)} %pad_clamp_fusion), kind=kCustom, calls=%fused_computation | custom fusion | bytes 1573056 | tf_op jit(solution)/shard_map/jit(_take)/gather | solution.py:213
  (3 shorter events, 0.0 us)
Async XLA Ops:
  0.7 9.5 %copy-start.7 = (s32[4,48,1]{1,2,0:T(1,128)S(1)}, s32[4,48,1]{1,2,0:T(1,128)}, u32[]{:S(2)}) copy-start(s32[4,48,1]{1,2,0:T(1,128)} %param.9) | copy-start | bytes 2308
  0.7 42.0 %copy-start = (bf16[1,192,16,512]{3,2,1,0:T(8,128)(2,1)S(1)}, bf16[1,192,16,512]{3,2,1,0:T(8,128)(2,1)}, u32[]{:S(2)}) copy-start(bf16[1,192,16,512]{3,2,1,0:T(8,128)(2,1)} %param.8) | copy-start | bytes 9437188
  3.9 20.7 %collective-permute-start = (bf16[48,16,512]{2,1,0:T(8,128)(2,1)}, bf16[48,16,512]{2,1,0:T(8,128)(2,1)}, u32[]{:S(2)}, u32[]{:S(2)}) collective-permute-start(bf16[48,16,512]{2,1,0:T(8,128)(2,1)} %get-tuple-element.18), channel_id=1, source_target_pairs={{0,64},{32,96},{64,0},{96,32},{1,65},{33,97},{65,1},{97,33},{2,66}... | collective-permute-start | bytes 2359304 | tf_op jit(solution)/shard_map/ppermute | solution.py:201
  7.5 35.2 %collective-permute-start.1 = (bf16[48,16,512]{2,1,0:T(8,128)(2,1)}, bf16[48,16,512]{2,1,0:T(8,128)(2,1)}, u32[]{:S(2)}, u32[]{:S(2)}) collective-permute-start(bf16[48,16,512]{2,1,0:T(8,128)(2,1)} %get-tuple-element.19), channel_id=1, source_target_pairs={{0,32},{32,64},{64,96},{96,0},{1,33},{33,65},{65,97},{97,1},{2,34}... | collective-permute-start | bytes 2359304 | tf_op jit(solution)/shard_map/ppermute | solution.py:201
  7.8 34.9 %collective-permute-start.2 = (bf16[48,16,512]{2,1,0:T(8,128)(2,1)}, bf16[48,16,512]{2,1,0:T(8,128)(2,1)}, u32[]{:S(2)}, u32[]{:S(2)}) collective-permute-start(bf16[48,16,512]{2,1,0:T(8,128)(2,1)} %get-tuple-element.17), channel_id=1, source_target_pairs={{0,96},{32,0},{64,32},{96,64},{1,97},{33,1},{65,33},{97,65},{2,98}... | collective-permute-start | bytes 2359304 | tf_op jit(solution)/shard_map/ppermute | solution.py:201
  42.6 34.7 %copy-start.2 = (f32[3,512,512]{2,1,0:T(8,128)S(1)}, f32[3,512,512]{2,1,0:T(8,128)}, u32[]{:S(2)}) copy-start(f32[3,512,512]{2,1,0:T(8,128)} %var_ref.1) | copy-start | bytes 9437188
  42.6 34.7 %copy-start.3 = (bf16[3,512,512]{2,1,0:T(8,128)(2,1)S(1)}, bf16[3,512,512]{2,1,0:T(8,128)(2,1)}, u32[]{:S(2)}) copy-start(bf16[3,512,512]{2,1,0:T(8,128)(2,1)} %left_ref.2) | copy-start | bytes 4718596
  42.7 34.7 %copy-start.4 = (bf16[3,512,512]{2,1,0:T(8,128)(2,1)S(1)}, bf16[3,512,512]{2,1,0:T(8,128)(2,1)}, u32[]{:S(2)}) copy-start(bf16[3,512,512]{2,1,0:T(8,128)(2,1)} %right_ref.2) | copy-start | bytes 4718596
  45.5 31.9 %copy-start.1 = (f32[3,512,512]{2,1,0:T(8,128)S(1)}, f32[3,512,512]{2,1,0:T(8,128)}, u32[]{:S(2)}) copy-start(f32[3,512,512]{2,1,0:T(8,128)} %mom_ref.1) | copy-start | bytes 9437188
  85.9 4.7 %copy-start.5 = (bf16[3,512,512]{2,1,0:T(8,128)(2,1)S(1)}, bf16[3,512,512]{2,1,0:T(8,128)(2,1)}, u32[]{:S(2)}) copy-start(bf16[3,512,512]{2,1,0:T(8,128)(2,1)} %left_ref.3) | copy-start | bytes 4718596
  85.9 25.3 %all-to-all-start.1 = ((bf16[32,3,16,512]{3,2,1,0:T(8,128)(2,1)}), bf16[32,3,16,512]{3,2,1,0:T(8,128)(2,1)}, u32[]{:S(2)}, u32[]{:S(2)}) async-start(bf16[32,3,16,512]{3,2,1,0:T(8,128)(2,1)} %get-tuple-element.10), calls=%async_computation.1 | async-start | bytes 3145728 | tf_op jit(solution)/shard_map/all_to_all | solution.py:210
  90.5 1.4 %copy-start.6 = (bf16[3,512,512]{2,1,0:T(8,128)(2,1)S(1)}, bf16[3,512,512]{2,1,0:T(8,128)(2,1)}, u32[]{:S(2)}) copy-start(bf16[3,512,512]{2,1,0:T(8,128)(2,1)} %right_ref.3) | copy-start | bytes 4718596

commit v2 on v0

v2 whole, which is shorter than its diff:
```python
import functools

import jax
import jax.numpy as jnp
from jax import lax
from jax.experimental import pallas as pl
from jax.experimental.pallas import tpu as pltpu
from jax.sharding import PartitionSpec as P

beta_moment = 0.95
beta_second = 0.95
beta_factor = 0.95
epsilon = 1e-08

F32 = jnp.float32
BF16 = jnp.bfloat16
VMEM_LIMIT = 32 * 1024 * 1024


def dot_nn(a, b):
    return lax.dot_general(a, b, (((1,), (0,)), ((), ())), preferred_element_type=F32)


def dot_tn(a, b):
    return lax.dot_general(a, b, (((0,), (0,)), ((), ())), preferred_element_type=F32)


def dot_nt(a, b):
    return lax.dot_general(a, b, (((1,), (1,)), ((), ())), preferred_element_type=F32)


def owner_ranks(owners):
    count = owners.shape[0]
    places = jnp.arange(count, dtype=jnp.int32)
    same = (owners[:, None] == owners[None, :]) & (places[None, :] < places[:, None])
    return jnp.sum(same.astype(jnp.int32), axis=1)


ANYWHERE = pl.BlockSpec(memory_space=pl.ANY)
IN_VMEM = pl.BlockSpec(memory_space=pltpu.VMEM)
DMA = pltpu.SemaphoreType.DMA
REPLICAS = 4
CUTS = 2


def call(kernel, name, scalars, operands, outs, scratch, flops, accessed):
    def place(array, where):
        return array if where is pl.ANY else pltpu.with_memory_space_constraint(array, where)

    spaces = [where for _, where in operands]
    spec = lambda where: IN_VMEM if where is pltpu.VMEM else ANYWHERE
    return pl.pallas_call(
        kernel,
        out_shape=[
            pltpu.VMEM(shape, dtype)
            if where is pltpu.VMEM
            else jax.ShapeDtypeStruct(shape, dtype)
            for shape, dtype, where in outs
        ],
        grid_spec=pltpu.PrefetchScalarGridSpec(
            num_scalar_prefetch=len(scalars),
            grid=(1,),
            in_specs=[spec(where) for where in spaces],
            out_specs=[spec(where) for _, _, where in outs],
            scratch_shapes=scratch,
        ),
        compiler_params=pltpu.CompilerParams(vmem_limit_bytes=VMEM_LIMIT),
        cost_estimate=pl.CostEstimate(flops=flops, bytes_accessed=accessed, transcendentals=0),
        name=name,
    )(*scalars, *[place(array, where) for array, where in operands])


def ahead_of(group, hops):
    return lax.rem(group + hops, REPLICAS)


def copy_kernel(halves, group_ref, local_ref, *refs):
    outs, sem = refs[:-1], refs[-1]
    group = group_ref[0]
    count = outs[0].shape[0]
    step = count // CUTS
    reads = []
    for k, (hops, half) in enumerate(halves):
        first = (2 * ahead_of(group, hops) + half) * count
        for i in range(CUTS):
            reads.append(
                pltpu.make_async_copy(
                    local_ref.at[pl.ds(first + i * step, step)],
                    outs[k].at[pl.ds(i * step, step)],
                    sem.at[k, i],
                )
            )
            reads[-1].start()
    for read in reads:
        read.wait()


def copy_halves(local, group, halves, name):
    blocks, rows, width = local.shape
    count = blocks // REPLICAS // 2
    return call(
        functools.partial(copy_kernel, halves),
        name,
        (group,),
        [(local, pltpu.HBM)],
        [((count, rows, width), BF16, pltpu.VMEM)] * len(halves),
        [DMA((len(halves), CUTS))],
        0,
        2 * len(halves) * count * rows * width,
    )


def add_kernel(up_ref, down_ref, a_ref, b_ref, up_out, down_out):
    def step(j, carry):
        up_out[j] = (up_ref[j].astype(F32) + a_ref[j].astype(F32)).astype(BF16)
        down_out[j] = (down_ref[j].astype(F32) + b_ref[j].astype(F32)).astype(BF16)
        return carry

    lax.fori_loop(0, up_ref.shape[0], step, 0, unroll=4)


def add_relayed(own_up, own_down, up, down):
    count, rows, width = up.shape
    return call(
        add_kernel,
        "add_relayed",
        (),
        [(array, pltpu.VMEM) for array in (own_up, own_down, up, down)],
        [((count, rows, width), BF16, pltpu.VMEM)] * 2,
        [],
        2 * count * rows * width,
        12 * count * rows * width,
    )


def place_kernel(place_ref, own_a, own_b, a1, a2, b1, b2, out_ref, held, sem):
    count = a1.shape[0]
    for own, left, right, base in ((own_a, a1, a2, 0), (own_b, b1, b2, count)):

        def step(j, carry, own=own, left=left, right=right, base=base):
            total = own[j].astype(F32) + (left[j].astype(F32) + right[j].astype(F32))
            held[base + j] = total.astype(BF16)
            pltpu.make_async_copy(
                held.at[base + j], out_ref.at[place_ref[base + j]], sem
            ).start()
            return carry

        lax.fori_loop(0, count, step, 0, unroll=4)
    pltpu.make_async_copy(held, held, sem).wait()


def sum_and_place(own, a, b, place, slots):
    count, rows, width = a[0].shape
    return call(
        place_kernel,
        "sum_and_place",
        (place,),
        [(array, pltpu.VMEM) for array in (*own, *a, *b)],
        [((slots, rows, width), BF16, pltpu.HBM)],
        [pltpu.VMEM((2 * count, rows, width), BF16), DMA(())],
        4 * count * rows * width,
        16 * count * rows * width,
    )[0]


def take_kernel(place_ref, source_ref, out_ref, held, into, out_of):
    cuts = into.shape[0]
    part = out_ref.shape[0] // cuts
    for i in range(cuts):

        def step(j, carry, i=i):
            pltpu.make_async_copy(source_ref.at[place_ref[j]], held.at[j], into.at[i]).start()
            return carry

        lax.fori_loop(i * part, (i + 1) * part, step, 0, unroll=4)
    writes = []
    for i in range(cuts):
        rows = pl.ds(i * part, part)
        pltpu.make_async_copy(held.at[rows], held.at[rows], into.at[i]).wait()
        writes.append(pltpu.make_async_copy(held.at[rows], out_ref.at[rows], out_of.at[i]))
        writes[-1].start()
    for write in writes:
        write.wait()


def take_blocks(source, place):
    _, rows, width = source.shape
    count = place.shape[0]
    return call(
        take_kernel,
        "take_blocks",
        (place,),
        [(source, pl.ANY)],
        [((count, rows, width), BF16, pltpu.HBM)],
        [pltpu.VMEM((count, rows, width), BF16), DMA((3,)), DMA((3,))],
        0,
        4 * count * rows * width,
    )[0]


def turn_kernel(
    mom_ref,
    var_ref,
    left_ref,
    right_ref,
    turned_first,
    var_first,
    left_first,
    right_first,
    turned_out,
    mom,
    left,
    right,
    turned,
    into,
    out_of,
):
    slots = mom.shape[0]
    reads = [
        [
            pltpu.make_async_copy(a.at[s], b, into.at[s, k])
            for k, (a, b) in enumerate(
                (
                    (mom_ref, mom.at[s]),
                    (left_ref, left.at[s - 1] if s else left_first),
                    (right_ref, right.at[s - 1] if s else right_first),
                )
            )
        ]
        for s in range(slots)
    ]
    reads[0].append(pltpu.make_async_copy(var_ref.at[0], var_first, into.at[0, 3]))
    writes = [
        pltpu.make_async_copy(turned.at[s], turned_out.at[s], out_of.at[s])
        for s in range(slots - 1)
    ]
    for row in reads:
        for read in row:
            read.start()
    for s in range(slots):
        for read in reads[s]:
            read.wait()
        half = (beta_moment * mom[s]).astype(BF16)
        one, other = (left[s - 1], right[s - 1]) if s else (left_first[...], right_first[...])
        product = dot_nn(dot_tn(one, half).astype(BF16), other)
        if s:
            turned[s - 1] = product
            writes[s - 1].start()
        else:
            turned_first[...] = product
    for write in writes:
        write.wait()


def turn_moment(momentum, variance, left_basis, right_basis):
    slots, size, _ = momentum.shape
    square = (size, size)
    others = (slots - 1, size, size)
    return call(
        turn_kernel,
        "turn_moment",
        (),
        [(array, pltpu.HBM) for array in (momentum, variance, left_basis, right_basis)],
        [
            (square, F32, pltpu.VMEM),
            (square, F32, pltpu.VMEM),
            (square, BF16, pltpu.VMEM),
            (square, BF16, pltpu.VMEM),
            (others, F32, pltpu.HBM),
        ],
        [
            pltpu.VMEM(momentum.shape, F32),
            pltpu.VMEM(others, BF16),
            pltpu.VMEM(others, BF16),
            pltpu.VMEM(others, F32),
            DMA((slots, 4)),
            DMA((slots - 1,)),
        ],
        4 * slots * size**3,
        12 * slots * size**2,
    )


def step_kernel(
    load_ref,
    grad_ref,
    turned_ref,
    var_ref,
    left_ref,
    right_ref,
    turned_first,
    var_first,
    left_first,
    right_first,
    var_out,
    upd_out,
    grad,
    turned,
    var,
    left,
    right,
    kept,
    upd,
    into,
    out_of,
):
    slots, size, _ = kept.shape
    reads = [[pltpu.make_async_copy(grad_ref.at[:, 0], grad.at[0], into.at[0, 0])]]
    for s in range(1, slots):
        pairs = (
            (grad_ref.at[:, s], grad.at[s]),
            (left_ref.at[s], left.at[s - 1]),
            (right_ref.at[s], right.at[s - 1]),
            (var_ref.at[s], var.at[s - 1]),
            (turned_ref.at[s - 1], turned.at[s - 1]),
        )
        reads.append(
            [pltpu.make_async_copy(a, b, into.at[s, k]) for k, (a, b) in enumerate(pairs)]
        )
    writes = [
        (
            pltpu.make_async_copy(kept.at[s], var_out.at[s], out_of.at[s, 0]),
            pltpu.make_async_copy(upd.at[s], upd_out.at[:, s], out_of.at[s, 1]),
        )
        for s in range(slots)
    ]
    for row in reads:
        for read in row:
            read.start()
    for s in range(slots):
        for read in reads[s]:
            read.wait()
        at = (lambda ref, first: ref.at[s - 1]) if s else (lambda ref, first: first)
        old = at(var, var_first)

        @pl.when(s < load_ref[0])
        def _():
            one = at(left, left_first)[...]
            other = at(right, right_first)[...]
            block = grad[s].reshape(size, size)
            rotated = dot_nn(dot_tn(one, block).astype(BF16), other)
            second = beta_second * old[...] + (1.0 - beta_second) * rotated * rotated
            kept[s] = second
            rotated_moment = at(turned, turned_first)[...] + (1.0 - beta_moment) * rotated
            direction = (rotated_moment / (jnp.sqrt(second) + epsilon)).astype(BF16)
            back_half = dot_nn(one, direction).astype(BF16)
            update = dot_nt(back_half, other).astype(BF16)
            upd[s] = update.reshape(upd.shape[1:])

        @pl.when(s >= load_ref[0])
        def _():
            kept[s] = old[...]

        for write in writes[s]:
            write.start()
    for row in writes:
        for write in row:
            write.wait()


def owner_step(load, grad, prepared, variance, left_basis, right_basis):
    slots, size, _ = variance.shape
    owners, _, rows, _ = grad.shape
    slabs = pltpu.VMEM((slots, owners, rows, size), BF16)
    others = (slots - 1, size, size)
    *first, turned = prepared
    return call(
        step_kernel,
        "owner_step",
        (load,),
        [(array, pltpu.HBM) for array in (grad, turned, variance, left_basis, right_basis)]
        + [(array, pltpu.VMEM) for array in first],
        [(variance.shape, F32, pltpu.HBM), (grad.shape, BF16, pltpu.HBM)],
        [
            slabs,
            pltpu.VMEM(others, F32),
            pltpu.VMEM(others, F32),
            pltpu.VMEM(others, BF16),
            pltpu.VMEM(others, BF16),
            pltpu.VMEM(variance.shape, F32),
            slabs,
            DMA((slots, 5)),
            DMA((slots, 2)),
        ],
        8 * slots * size**3,
        8 * slots * size**2,
    )


def state_kernel(
    load_ref,
    grad_ref,
    mom_ref,
    left_ref,
    right_ref,
    mom_out,
    left_out,
    right_out,
    grad,
    mom,
    left,
    right,
    into,
    out_of,
):
    slots, size, _ = mom.shape
    pairs = ((mom_ref, mom), (left_ref, left), (right_ref, right))
    reads = [
        [pltpu.make_async_copy(grad_ref.at[:, s], grad.at[s], into.at[s, 3])]
        + [pltpu.make_async_copy(a.at[s], b.at[s], into.at[s, k]) for k, (a, b) in enumerate(pairs)]
        for s in range(slots)
    ]
    pairs = ((mom, mom_out), (left, left_out), (right, right_out))
    writes = [
        [pltpu.make_async_copy(a.at[s], b.at[s], out_of.at[s, k]) for k, (a, b) in enumerate(pairs)]
        for s in range(slots)
    ]
    for row in reads:
        for read in row:
            read.start()
    for s in range(slots):
        for read in reads[s]:
            read.wait()

        @pl.when(s < load_ref[0])
        def _():
            block = grad[s].reshape(size, size)
            mom[s] = beta_moment * mom[s] + (1.0 - beta_moment) * block.astype(F32)
            outer = dot_nt(block, block)
            left[s] = (beta_factor * left[s].astype(F32) + (1.0 - beta_factor) * outer).astype(BF16)
            outer = dot_tn(block, block)
            right[s] = (beta_factor * right[s].astype(F32) + (1.0 - beta_factor) * outer).astype(
                BF16
            )

        for write in writes[s]:
            write.start()
    for row in writes:
        for write in row:
            write.wait()


def rest_of_state(load, grad, momentum, left_factor, right_factor):
    slots, size, _ = momentum.shape
    owners, _, rows, _ = grad.shape
    shape = momentum.shape
    return call(
        state_kernel,
        "rest_of_state",
        (load,),
        [(array, pltpu.HBM) for array in (grad, momentum, left_factor, right_factor)],
        [(shape, F32, pltpu.HBM), (shape, BF16, pltpu.HBM), (shape, BF16, pltpu.HBM)],
        [
            pltpu.VMEM((slots, owners, rows, size), BF16),
            pltpu.VMEM(shape, F32),
            pltpu.VMEM(shape, BF16),
            pltpu.VMEM(shape, BF16),
            DMA((slots, 4)),
            DMA((slots, 3)),
        ],
        4 * slots * size**3,
        18 * slots * size**2,
    )


def exchange(slabs):
    return lax.all_to_all(slabs, "shard", split_axis=0, concat_axis=0, tiled=True)


def body(
    grads, owner_table, momentum, variance, left_factor, right_factor, left_basis, right_basis
):
    owner_count = lax.axis_size("shard")
    group = lax.axis_index("dp")
    own_index = lax.axis_index("shard")
    capacity = momentum.shape[0]
    local = grads[0]
    _, rows, width = local.shape
    up = lambda x: lax.ppermute(x, "dp", [(i, (i + 1) % REPLICAS) for i in range(REPLICAS)])
    down = lambda x: lax.ppermute(x, "dp", [((i + 1) % REPLICAS, i) for i in range(REPLICAS)])

    here = group.reshape(1)
    relay_up, relay_down, near_up, near_down = copy_halves(
        local, here, ((2, 0), (2, 1), (1, 1), (3, 0)), "copy_sends"
    )
    relay_up, relay_down = up(relay_up), down(relay_down)
    near_up, near_down = up(near_up), down(near_down)
    own_up, own_down, own_a, own_b = copy_halves(
        local, here, ((1, 0), (3, 1), (0, 0), (0, 1)), "copy_own"
    )
    prepared = turn_moment(momentum, variance, left_basis, right_basis)
    relay_up, relay_down, prepared = lax.optimization_barrier((relay_up, relay_down, prepared))
    ahead, behind = add_relayed(own_up, own_down, relay_up, relay_down)
    ahead, behind = up(ahead), down(behind)

    owners = lax.dynamic_index_in_dim(owner_table[:, :, 0], group, 0, keepdims=False)
    place = owners * capacity + owner_ranks(owners)
    load = jnp.sum((owners == own_index).astype(jnp.int32)).reshape(1)

    outgoing = sum_and_place(
        (own_a, own_b), (ahead, near_down), (near_up, behind), place, owner_count * capacity
    ).reshape(owner_count, capacity, rows, width)
    grad = exchange(outgoing)
    new_variance, update = owner_step(load, grad, prepared, variance, left_basis, right_basis)
    returned = exchange(update)
    new_momentum, new_left, new_right = rest_of_state(
        load, grad, momentum, left_factor, right_factor
    )
    update_rows = take_blocks(returned.reshape(owner_count * capacity, rows, width), place)
    return (update_rows, new_momentum, new_variance, new_left, new_right)


def solution(mesh):
    state = P(("dp", "shard"), None, None)
    return jax.shard_map(
        body,
        mesh=mesh,
        in_specs=(P("dp", None, "shard", None), P(), state, state, state, state, state, state),
        out_specs=(P("dp", "shard", None), state, state, state, state),
        check_vma=False,
    )
```

time: 171 us -> 103 us (0.60)
  local copies, waits for them, and re-layouts: 39.5 us -> 1.31 us
  waiting for transfers between devices: 63.5 us -> 29 us
  blocking collectives: 0 us -> 32.7 us
  Pallas kernels: 0 us -> 25.2 us
  matrix products: 24.5 us -> 0 us
  other arithmetic: 15.9 us -> 1.47 us
  between operations: 14.2 us -> 0.72 us
    reduce_scatter x1 -> x0, waiting for transfers between devices: 42.2 us -> none  [body(): lax.psum_scatter(local.astype(jnp.float32).astype(jnp.bfloat16), 'dp', sc...]
    all_to_all x0 -> x1, blocking collectives: none -> 32.7 us  [exchange(): lax.all_to_all(slabs, 'shard', split_axis=0, concat_axis=0, tiled=True)]
    pallas_call x0 -> x8, Pallas kernels: none -> 25.2 us  [call(): pl.pallas_call(kernel, out_shape=[pltpu.VMEM(shape, dtype) if where is pl...]
    dot_general x5 -> x0, matrix products: 24.5 us -> none  [the longest x1 8 us: owner_work(): jnp.einsum('cij,ckj->cik', back_half, right_basis, preferred_element_type...]
    unnamed x18 -> x2, local copies, waits for them, and re-layouts: 22.8 us -> 1.31 us
    select_n x6 -> x0, other arithmetic: 13.9 us -> none  [the longest x1 5.53 us: body(): new_variance = jnp.where(live, second, variance)]
    ppermute x0 -> x6, waiting for transfers between devices: none -> 12.2 us  [the longest x3 8.43 us: body(): lax.ppermute(x, 'dp', [(i, (i + 1) % REPLICAS) for i in range(REPLICAS)])]
    all_to_all x2 -> x1, starting transfers between devices: 12.9 us -> 4.89 us  [exchange(): lax.all_to_all(slabs, 'shard', split_axis=0, concat_axis=0, tiled=True)]
  transfers between devices with their start and end apart: 3 -> 7, of which waited for: 2 -> 3; matrix products, arithmetic and copies ran while one was open for 24% -> 1% of each run, Pallas kernels for 0% -> 12%
where the time goes in v2:
time: 103 us
  blocking collectives  32.7 us (32%)
  waiting for transfers between devices  29 us (28%)
  Pallas kernels  25.2 us (24%)
  starting transfers between devices  12.6 us (12%)
  other arithmetic  1.47 us (1%)
  local copies, waits for them, and re-layouts  1.31 us (1%)
    all_to_all x1, blocking collectives, exchange(): lax.all_to_all(slabs, 'shard', split_axis=0, concat_axis=0, tiled=True)  32.7 us
    pallas_call x8, Pallas kernels, call(): pl.pallas_call(kernel, out_shape=[pltpu.VMEM(shape, dtype) if where is pl...  25.2 us
    all_to_all x1, waiting for transfers between devices, exchange(): lax.all_to_all(slabs, 'shard', split_axis=0, concat_axis=0, tiled=True)  16.7 us
    ppermute x3, waiting for transfers between devices, body(): lax.ppermute(x, 'dp', [(i, (i + 1) % REPLICAS) for i in range(REPLICAS)])  8.43 us
    all_to_all x1, starting transfers between devices, exchange(): lax.all_to_all(slabs, 'shard', split_axis=0, concat_axis=0, tiled=True)  4.89 us
    ppermute x3, starting transfers between devices, body(): lax.ppermute(x, 'dp', [((i + 1) % REPLICAS, i) for i in range(REPLICAS)])  4.39 us
    ppermute x3, waiting for transfers between devices, body(): lax.ppermute(x, 'dp', [((i + 1) % REPLICAS, i) for i in range(REPLICAS)])  3.81 us
    ppermute x3, starting transfers between devices, body(): lax.ppermute(x, 'dp', [(i, (i + 1) % REPLICAS) for i in range(REPLICAS)])  3.28 us
  transfers between devices with their start and end apart: 7, of which 3 were waited for; matrix products, arithmetic and copies ran while one was open for 1% of the time, Pallas kernels for 12%

profile of v2, /device:TPU:1, one launch (start us, length us, event | category | flops | bytes accessed | tf_op | source)
XLA Modules:
  0.0 102.9 jit_solution(5749040097238117998)
XLA Ops:
  0.6 2.5 %copy_sends.1 = (bf16[24,16,512]{2,1,0:T(8,128)(2,1)}, bf16[24,16,512]{2,1,0:T(8,128)(2,1)}, bf16[24,16,512]{2,1,0:T(8,128)(2,1)S(1)}, bf16[24,16,512]{2,1,0:T(8,128)(2,1)}) custom-call(s32[1]{0:T(128)} %bitcast.2.group_ref, bf16[192,16,512]{2,1,0:T(8,128)(2,1)} %bitcast.10), custom_call_target="tpu_custom_call" | custom-call | bytes 1572864 | tf_op jit(solution)/shard_map/copy_sends/pallas_call | solution.py:52
  3.2 2.1 %collective-permute-start = (bf16[24,16,512]{2,1,0:T(8,128)(2,1)}, bf16[24,16,512]{2,1,0:T(8,128)(2,1)S(1)}, u32[]{:S(2)}, u32[]{:S(2)}) collective-permute-start(bf16[24,16,512]{2,1,0:T(8,128)(2,1)} %get-tuple-element.36), channel_id=1, source_target_pairs={{0,32},{32,64},{64,96},{96,0},{1,33},{33,65},{65,97},{97,1},{2,34}... | collective-permute-start | bytes 1179656 | tf_op jit(solution)/shard_map/ppermute | solution.py:479
  5.3 1.3 %collective-permute-start.1 = (bf16[24,16,512]{2,1,0:T(8,128)(2,1)}, bf16[24,16,512]{2,1,0:T(8,128)(2,1)S(1)}, u32[]{:S(2)}, u32[]{:S(2)}) collective-permute-start(bf16[24,16,512]{2,1,0:T(8,128)(2,1)} %get-tuple-element.37), channel_id=1, source_target_pairs={{32,0},{64,32},{96,64},{0,96},{33,1},{65,33},{97,65},{1,97},{34,2}... | collective-permute-start | bytes 1179656 | tf_op jit(solution)/shard_map/ppermute | solution.py:480
  6.6 1.4 %collective-permute-start.3 = (bf16[24,16,512]{2,1,0:T(8,128)(2,1)}, bf16[24,16,512]{2,1,0:T(8,128)(2,1)S(1)}, u32[]{:S(2)}, u32[]{:S(2)}) collective-permute-start(bf16[24,16,512]{2,1,0:T(8,128)(2,1)} %get-tuple-element.46), channel_id=1, source_target_pairs={{32,0},{64,32},{96,64},{0,96},{33,1},{65,33},{97,65},{1,97},{34,2}... | collective-permute-start | bytes 1179656 | tf_op jit(solution)/shard_map/ppermute | solution.py:480
  8.0 0.1 collective-permute-start.4
  8.1 1.5 %copy_own.1 = (bf16[24,16,512]{2,1,0:T(8,128)(2,1)S(1)}, bf16[24,16,512]{2,1,0:T(8,128)(2,1)S(1)}, bf16[24,16,512]{2,1,0:T(8,128)(2,1)S(1)}, bf16[24,16,512]{2,1,0:T(8,128)(2,1)S(1)}) custom-call(s32[1]{0:T(128)} %bitcast.2.group_ref, bf16[192,16,512]{2,1,0:T(8,128)(2,1)} %bitcast.11), custom_call_target="tpu_custom_call" | custom-call | bytes 1572864 | tf_op jit(solution)/shard_map/copy_own/pallas_call | solution.py:52
  9.6 4.4 %turn_moment.1 = (f32[512,512]{1,0:T(8,128)S(1)}, f32[512,512]{1,0:T(8,128)S(1)}, bf16[512,512]{1,0:T(8,128)(2,1)S(1)}, bf16[512,512]{1,0:T(8,128)(2,1)S(1)}, f32[2,512,512]{2,1,0:T(8,128)S(1)}) custom-call(f32[3,512,512]{2,1,0:T(8,128)} %mom_ref.3, f32[3,512,512]{2,1,0:T(8,128)} %var_ref.3, bf16[3,512,512]{2,1,0:T(8,128)(2,1)} %left_ref.4, ...), custom_call_target="tpu_custom_call" | custom-call | flops 1610612736 | bytes 9437184 | tf_op jit(solution)/shard_map/turn_moment/pallas_call | solution.py:52
  14.0 0.0 copy-start
  14.0 1.3 %copy-done = f32[2,512,512]{2,1,0:T(8,128)} copy-done((f32[2,512,512]{2,1,0:T(8,128)}, f32[2,512,512]{2,1,0:T(8,128)S(1)}, u32[]{:S(2)}) %copy-start) | copy-done | bytes 2097176
  15.3 0.0 collective-permute-done.a_ref
  15.3 0.0 collective-permute-done.1.b_ref
  15.3 0.2 add_relayed.1
  15.6 1.1 %collective-permute-start.2 = (bf16[24,16,512]{2,1,0:T(8,128)(2,1)S(1)}, bf16[24,16,512]{2,1,0:T(8,128)(2,1)S(1)}, u32[]{:S(2)}, u32[]{:S(2)}) collective-permute-start(bf16[24,16,512]{2,1,0:T(8,128)(2,1)S(1)} %get-tuple-element.45), channel_id=1, source_target_pairs={{0,32},{32,64},{64,96},{96,0},{1,33},{33,65},{65,97},{97,1},{2,34}... | collective-permute-start | bytes 1179656 | tf_op jit(solution)/shard_map/ppermute | solution.py:479
  16.7 1.7 %collective-permute-start.5 = (bf16[24,16,512]{2,1,0:T(8,128)(2,1)S(1)}, bf16[24,16,512]{2,1,0:T(8,128)(2,1)S(1)}, u32[]{:S(2)}, u32[]{:S(2)}) collective-permute-start(bf16[24,16,512]{2,1,0:T(8,128)(2,1)S(1)} %get-tuple-element.48), channel_id=1, source_target_pairs={{32,0},{64,32},{96,64},{0,96},{33,1},{65,33},{97,65},{1,97},{34,2}... | collective-permute-start | bytes 1179656 | tf_op jit(solution)/shard_map/ppermute | solution.py:480
  18.3 1.3 %fusion.1 = (s32[]{:T(128)}, s32[48]{0:T(128)S(1)}) fusion(s32[]{:T(128)S(6)} %axis_index.25, s32[4,48,1]{1,2,0:T(1,128)} %param.9, s32[]{:T(128)S(6)} %select_n.4), kind=kLoop, calls=%fused_computation.4 | loop fusion | flops 143 | bytes 396 | tf_op jit(solution)/shard_map/reduce_sum | solution.py:498
  19.6 0.2 convert_reduce_fusion
  19.8 3.8 %collective-permute-done.3.a2 = bf16[24,16,512]{2,1,0:T(8,128)(2,1)S(1)} collective-permute-done((bf16[24,16,512]{2,1,0:T(8,128)(2,1)}, bf16[24,16,512]{2,1,0:T(8,128)(2,1)S(1)}, u32[]{:S(2)}, u32[]{:S(2)}) %collective-permute-start.3) | collective-permute-done | bytes 393248 | tf_op jit(solution)/shard_map/ppermute | solution.py:480
  23.6 0.0 collective-permute-done.4.b1
  23.6 8.4 %collective-permute-done.2.a1 = bf16[24,16,512]{2,1,0:T(8,128)(2,1)S(1)} collective-permute-done((bf16[24,16,512]{2,1,0:T(8,128)(2,1)S(1)}, bf16[24,16,512]{2,1,0:T(8,128)(2,1)S(1)}, u32[]{:S(2)}, u32[]{:S(2)}) %collective-permute-start.2) | collective-permute-done | bytes 393248 | tf_op jit(solution)/shard_map/ppermute | solution.py:479
  32.0 0.0 collective-permute-done.5.b2
  32.0 2.0 %sum_and_place.1 = bf16[96,16,512]{2,1,0:T(8,128)(2,1)S(1)} custom-call(s32[48]{0:T(128)S(1)} %multiply_add_fusion.place_ref, bf16[24,16,512]{2,1,0:T(8,128)(2,1)S(1)} %get-tuple-element.32.own_a, bf16[24,16,512]{2,1,0:T(8,128)(2,1)S(1)} %get-tuple-element.33.own_b, bf16[24,16,512]{2,1,0:T(8,128)(2,1)S(1)} %collective-permute-done.2.a1, ...), custom_call_target="tpu_custom_call" | custom-call | flops 786432 | bytes 3145728 | tf_op jit(solution)/shard_map/sum_and_place/pallas_call | solution.py:52
  34.1 32.7 %all_to_all.10.grad_ref = bf16[32,3,16,512]{3,2,1,0:T(8,128)(2,1)} all-to-all(bf16[32,3,16,512]{3,2,1,0:T(8,128)(2,1)S(1)} %bitcast.9), channel_id=1, replica_groups=mesh['dp'=4,'shard'=32] {'shard'}, dimensions={0} | all-to-all | bytes 3145728 | tf_op jit(solution)/shard_map/all_to_all | solution.py:467
  66.8 5.8 %owner_step.1 = (f32[3,512,512]{2,1,0:T(8,128)}, bf16[32,3,16,512]{3,2,1,0:T(8,128)(2,1)}) custom-call(s32[1]{0:T(128)} %bitcast.1.load_ref, bf16[32,3,16,512]{3,2,1,0:T(8,128)(2,1)} %all_to_all.10.grad_ref, f32[2,512,512]{2,1,0:T(8,128)} %copy-done, f32[3,512,512]{2,1,0:T(8,128)} %var_ref.3, bf16[3,512,512]{2,1,0:T(8,128)(2,1)} %left_ref.4, ...), custom_call_target="tpu_custom_call" | custom-call | flops 3221225472 | bytes 6291456 | tf_op jit(solution)/shard_map/owner_step/pallas_call | solution.py:52
  72.6 4.9 %all-to-all-start.1 = ((bf16[32,3,16,512]{3,2,1,0:T(8,128)(2,1)}), bf16[32,3,16,512]{3,2,1,0:T(8,128)(2,1)S(1)}, u32[]{:S(2)}, u32[]{:S(2)}) async-start(bf16[32,3,16,512]{3,2,1,0:T(8,128)(2,1)} %get-tuple-element.54), calls=%async_computation.1 | async-start | bytes 3145728 | tf_op jit(solution)/shard_map/all_to_all | solution.py:467
  77.5 6.0 %rest_of_state.1 = (f32[3,512,512]{2,1,0:T(8,128)}, bf16[3,512,512]{2,1,0:T(8,128)(2,1)}, bf16[3,512,512]{2,1,0:T(8,128)(2,1)}) custom-call(s32[1]{0:T(128)} %bitcast.1.load_ref, bf16[32,3,16,512]{3,2,1,0:T(8,128)(2,1)} %all_to_all.10.grad_ref, f32[3,512,512]{2,1,0:T(8,128)} %mom_ref.3, bf16[3,512,512]{2,1,0:T(8,128)(2,1)} %left_ref.5, ...), custom_call_target="tpu_custom_call" | custom-call | flops 1610612736 | bytes 14155776 | tf_op jit(solution)/shard_map/rest_of_state/pallas_call | solution.py:52
  83.5 16.7 %all-to-all-done.1 = bf16[32,3,16,512]{3,2,1,0:T(8,128)(2,1)S(1)} async-done(((bf16[32,3,16,512]{3,2,1,0:T(8,128)(2,1)}), bf16[32,3,16,512]{3,2,1,0:T(8,128)(2,1)S(1)}, u32[]{:S(2)}, u32[]{:S(2)}) %all-to-all-start.1) | async-done | bytes 1572896 | tf_op jit(solution)/shard_map/all_to_all | solution.py:467
  100.2 2.7 %take_blocks.1 = bf16[48,16,512]{2,1,0:T(8,128)(2,1)} custom-call(s32[48]{0:T(128)S(1)} %multiply_add_fusion.place_ref, bf16[96,16,512]{2,1,0:T(8,128)(2,1)S(1)} %bitcast.8), custom_call_target="tpu_custom_call" | custom-call | bytes 1572864 | tf_op jit(solution)/shard_map/take_blocks/pallas_call | solution.py:52
  (1 shorter events, 0.0 us)
Async XLA Ops:
  3.2 12.2 %collective-permute-start = (bf16[24,16,512]{2,1,0:T(8,128)(2,1)}, bf16[24,16,512]{2,1,0:T(8,128)(2,1)S(1)}, u32[]{:S(2)}, u32[]{:S(2)}) collective-permute-start(bf16[24,16,512]{2,1,0:T(8,128)(2,1)} %get-tuple-element.36), channel_id=1, source_target_pairs={{0,32},{32,64},{64,96},{96,0},{1,33},{33,65},{65,97},{97,1},{2,34}... | collective-permute-start | bytes 1179656 | tf_op jit(solution)/shard_map/ppermute | solution.py:479
  5.3 10.1 %collective-permute-start.1 = (bf16[24,16,512]{2,1,0:T(8,128)(2,1)}, bf16[24,16,512]{2,1,0:T(8,128)(2,1)S(1)}, u32[]{:S(2)}, u32[]{:S(2)}) collective-permute-start(bf16[24,16,512]{2,1,0:T(8,128)(2,1)} %get-tuple-element.37), channel_id=1, source_target_pairs={{32,0},{64,32},{96,64},{0,96},{33,1},{65,33},{97,65},{1,97},{34,2}... | collective-permute-start | bytes 1179656 | tf_op jit(solution)/shard_map/ppermute | solution.py:480
  6.6 17.0 %collective-permute-start.3 = (bf16[24,16,512]{2,1,0:T(8,128)(2,1)}, bf16[24,16,512]{2,1,0:T(8,128)(2,1)S(1)}, u32[]{:S(2)}, u32[]{:S(2)}) collective-permute-start(bf16[24,16,512]{2,1,0:T(8,128)(2,1)} %get-tuple-element.46), channel_id=1, source_target_pairs={{32,0},{64,32},{96,64},{0,96},{33,1},{65,33},{97,65},{1,97},{34,2}... | collective-permute-start | bytes 1179656 | tf_op jit(solution)/shard_map/ppermute | solution.py:480
  8.0 15.6 %collective-permute-start.4 = (bf16[24,16,512]{2,1,0:T(8,128)(2,1)S(1)}, bf16[24,16,512]{2,1,0:T(8,128)(2,1)S(1)}, u32[]{:S(2)}, u32[]{:S(2)}) collective-permute-start(bf16[24,16,512]{2,1,0:T(8,128)(2,1)S(1)} %get-tuple-element.47), channel_id=1, source_target_pairs={{0,32},{32,64},{64,96},{96,0},{1,33},{33,65},{65,97},{97,1},{2,34}... | collective-permute-start | bytes 1179656 | tf_op jit(solution)/shard_map/ppermute | solution.py:479
  14.0 1.3 %copy-start = (f32[2,512,512]{2,1,0:T(8,128)}, f32[2,512,512]{2,1,0:T(8,128)S(1)}, u32[]{:S(2)}) copy-start(f32[2,512,512]{2,1,0:T(8,128)S(1)} %get-tuple-element.49.turned_ref) | copy-start | bytes 6291460
  15.6 16.5 %collective-permute-start.2 = (bf16[24,16,512]{2,1,0:T(8,128)(2,1)S(1)}, bf16[24,16,512]{2,1,0:T(8,128)(2,1)S(1)}, u32[]{:S(2)}, u32[]{:S(2)}) collective-permute-start(bf16[24,16,512]{2,1,0:T(8,128)(2,1)S(1)} %get-tuple-element.45), channel_id=1, source_target_pairs={{0,32},{32,64},{64,96},{96,0},{1,33},{33,65},{65,97},{97,1},{2,34}... | collective-permute-start | bytes 1179656 | tf_op jit(solution)/shard_map/ppermute | solution.py:479
  16.7 15.4 %collective-permute-start.5 = (bf16[24,16,512]{2,1,0:T(8,128)(2,1)S(1)}, bf16[24,16,512]{2,1,0:T(8,128)(2,1)S(1)}, u32[]{:S(2)}, u32[]{:S(2)}) collective-permute-start(bf16[24,16,512]{2,1,0:T(8,128)(2,1)S(1)} %get-tuple-element.48), channel_id=1, source_target_pairs={{32,0},{64,32},{96,64},{0,96},{33,1},{65,33},{97,65},{1,97},{34,2}... | collective-permute-start | bytes 1179656 | tf_op jit(solution)/shard_map/ppermute | solution.py:480
  72.6 27.6 %all-to-all-start.1 = ((bf16[32,3,16,512]{3,2,1,0:T(8,128)(2,1)}), bf16[32,3,16,512]{3,2,1,0:T(8,128)(2,1)S(1)}, u32[]{:S(2)}, u32[]{:S(2)}) async-start(bf16[32,3,16,512]{3,2,1,0:T(8,128)(2,1)} %get-tuple-element.54), calls=%async_computation.1 | async-start | bytes 3145728 | tf_op jit(solution)/shard_map/all_to_all | solution.py:467

commit v3 on v2

--- a/solution.py
+++ b/solution.py
@@ -29,15 +29,9 @@
     return lax.dot_general(a, b, (((1,), (1,)), ((), ())), preferred_element_type=F32)
 
 
-def owner_ranks(owners):
-    count = owners.shape[0]
-    places = jnp.arange(count, dtype=jnp.int32)
-    same = (owners[:, None] == owners[None, :]) & (places[None, :] < places[:, None])
-    return jnp.sum(same.astype(jnp.int32), axis=1)
-
-
 ANYWHERE = pl.BlockSpec(memory_space=pl.ANY)
 IN_VMEM = pl.BlockSpec(memory_space=pltpu.VMEM)
+IN_SMEM = pl.BlockSpec(memory_space=pltpu.SMEM)
 DMA = pltpu.SemaphoreType.DMA
 REPLICAS = 4
 CUTS = 2
@@ -45,16 +39,15 @@
 
 def call(kernel, name, scalars, operands, outs, scratch, flops, accessed):
     def place(array, where):
-        return array if where is pl.ANY else pltpu.with_memory_space_constraint(array, where)
+        free = where in (pl.ANY, pltpu.SMEM)
+        return array if free else pltpu.with_memory_space_constraint(array, where)
 
     spaces = [where for _, where in operands]
-    spec = lambda where: IN_VMEM if where is pltpu.VMEM else ANYWHERE
+    spec = lambda where: {pltpu.VMEM: IN_VMEM, pltpu.SMEM: IN_SMEM}.get(where, ANYWHERE)
     return pl.pallas_call(
         kernel,
         out_shape=[
-            pltpu.VMEM(shape, dtype)
-            if where is pltpu.VMEM
-            else jax.ShapeDtypeStruct(shape, dtype)
+            jax.ShapeDtypeStruct(shape, dtype) if where is pl.ANY else where(shape, dtype)
             for shape, dtype, where in outs
         ],
         grid_spec=pltpu.PrefetchScalarGridSpec(
@@ -133,20 +126,16 @@
     )
 
 
-def place_kernel(place_ref, own_a, own_b, a1, a2, b1, b2, out_ref, held, sem):
+def place_kernel(place_ref, own_a, own_b, a1, a2, b1, b2, out_ref):
     count = a1.shape[0]
     for own, left, right, base in ((own_a, a1, a2, 0), (own_b, b1, b2, count)):
 
         def step(j, carry, own=own, left=left, right=right, base=base):
             total = own[j].astype(F32) + (left[j].astype(F32) + right[j].astype(F32))
-            held[base + j] = total.astype(BF16)
-            pltpu.make_async_copy(
-                held.at[base + j], out_ref.at[place_ref[base + j]], sem
-            ).start()
+            out_ref[place_ref[base + j]] = total.astype(BF16)
             return carry
 
         lax.fori_loop(0, count, step, 0, unroll=4)
-    pltpu.make_async_copy(held, held, sem).wait()
 
 
 def sum_and_place(own, a, b, place, slots):
@@ -156,31 +145,20 @@
         "sum_and_place",
         (place,),
         [(array, pltpu.VMEM) for array in (*own, *a, *b)],
-        [((slots, rows, width), BF16, pltpu.HBM)],
-        [pltpu.VMEM((2 * count, rows, width), BF16), DMA(())],
+        [((slots, rows, width), BF16, pltpu.VMEM)],
+        [],
         4 * count * rows * width,
         16 * count * rows * width,
     )[0]
 
 
-def take_kernel(place_ref, source_ref, out_ref, held, into, out_of):
-    cuts = into.shape[0]
-    part = out_ref.shape[0] // cuts
-    for i in range(cuts):
-
-        def step(j, carry, i=i):
-            pltpu.make_async_copy(source_ref.at[place_ref[j]], held.at[j], into.at[i]).start()
-            return carry
-
-        lax.fori_loop(i * part, (i + 1) * part, step, 0, unroll=4)
-    writes = []
-    for i in range(cuts):
-        rows = pl.ds(i * part, part)
-        pltpu.make_async_copy(held.at[rows], held.at[rows], into.at[i]).wait()
-        writes.append(pltpu.make_async_copy(held.at[rows], out_ref.at[rows], out_of.at[i]))
-        writes[-1].start()
-    for write in writes:
-        write.wait()
+def take_kernel(place_ref, source_ref, out_ref, sem):
+    def step(j, carry):
+        pltpu.make_async_copy(source_ref.at[place_ref[j]], out_ref.at[j], sem).start()
+        return carry
+
+    lax.fori_loop(0, out_ref.shape[0], step, 0, unroll=4)
+    pltpu.make_async_copy(out_ref, out_ref, sem).wait()
 
 
 def take_blocks(source, place):
@@ -190,46 +168,46 @@
         take_kernel,
         "take_blocks",
         (place,),
-        [(source, pl.ANY)],
+        [(source, pltpu.VMEM)],
         [((count, rows, width), BF16, pltpu.HBM)],
-        [pltpu.VMEM((count, rows, width), BF16), DMA((3,)), DMA((3,))],
+        [DMA(())],
         0,
         4 * count * rows * width,
     )[0]
 
 
 def turn_kernel(
+    here_ref,
+    table_ref,
     mom_ref,
-    var_ref,
     left_ref,
     right_ref,
-    turned_first,
-    var_first,
+    place_out,
+    load_out,
     left_first,
     right_first,
+    turned_first,
+    left_second,
     turned_out,
     mom,
     left,
     right,
     turned,
+    counts,
     into,
     out_of,
 ):
     slots = mom.shape[0]
+    lefts = [left_first, left_second] + [left.at[s] for s in range(slots - 2)]
+    rights = [right_first] + [right.at[s] for s in range(slots - 1)]
     reads = [
         [
-            pltpu.make_async_copy(a.at[s], b, into.at[s, k])
-            for k, (a, b) in enumerate(
-                (
-                    (mom_ref, mom.at[s]),
-                    (left_ref, left.at[s - 1] if s else left_first),
-                    (right_ref, right.at[s - 1] if s else right_first),
-                )
-            )
+            pltpu.make_async_copy(mom_ref.at[s], mom.at[s], into.at[s, 0]),
+            pltpu.make_async_copy(left_ref.at[s], lefts[s], into.at[s, 1]),
+            pltpu.make_async_copy(right_ref.at[s], rights[s], into.at[s, 2]),
         ]
         for s in range(slots)
     ]
-    reads[0].append(pltpu.make_async_copy(var_ref.at[0], var_first, into.at[0, 3]))
     writes = [
         pltpu.make_async_copy(turned.at[s], turned_out.at[s], out_of.at[s])
         for s in range(slots - 1)
@@ -237,12 +215,30 @@
     for row in reads:
         for read in row:
             read.start()
+
+    owner_count = counts.shape[0]
+    group, own_index = here_ref[0], here_ref[1]
+
+    def clear(i, carry):
+        counts[i] = 0
+        return carry
+
+    def rank(j, carry):
+        owner = table_ref[group, j]
+        seen = counts[owner]
+        counts[owner] = seen + 1
+        place_out[j] = owner * slots + seen
+        return carry
+
+    lax.fori_loop(0, owner_count, clear, 0)
+    lax.fori_loop(0, place_out.shape[0], rank, 0)
+    load_out[0] = counts[own_index]
+
     for s in range(slots):
         for read in reads[s]:
             read.wait()
         half = (beta_moment * mom[s]).astype(BF16)
-        one, other = (left[s - 1], right[s - 1]) if s else (left_first[...], right_first[...])
-        product = dot_nn(dot_tn(one, half).astype(BF16), other)
+        product = dot_nn(dot_tn(lefts[s][...], half).astype(BF16), rights[s][...]).astype(BF16)
         if s:
             turned[s - 1] = product
             writes[s - 1].start()
@@ -252,28 +248,31 @@
         write.wait()
 
 
-def turn_moment(momentum, variance, left_basis, right_basis):
+def turn_moment(here, table, owner_count, momentum, left_basis, right_basis):
     slots, size, _ = momentum.shape
     square = (size, size)
-    others = (slots - 1, size, size)
     return call(
         turn_kernel,
         "turn_moment",
-        (),
-        [(array, pltpu.HBM) for array in (momentum, variance, left_basis, right_basis)],
+        (here,),
+        [(table, pltpu.SMEM)]
+        + [(array, pltpu.HBM) for array in (momentum, left_basis, right_basis)],
         [
-            (square, F32, pltpu.VMEM),
-            (square, F32, pltpu.VMEM),
+            ((table.shape[1],), jnp.int32, pltpu.SMEM),
+            ((1,), jnp.int32, pltpu.SMEM),
             (square, BF16, pltpu.VMEM),
             (square, BF16, pltpu.VMEM),
-            (others, F32, pltpu.HBM),
+            (square, BF16, pltpu.VMEM),
+            (square, BF16, pltpu.VMEM),
+            ((slots - 1, size, size), BF16, pltpu.HBM),
         ],
         [
             pltpu.VMEM(momentum.shape, F32),
-            pltpu.VMEM(others, BF16),
-            pltpu.VMEM(others, BF16),
-            pltpu.VMEM(others, F32),
-            DMA((slots, 4)),
+            pltpu.VMEM((slots - 2, size, size), BF16),
+            pltpu.VMEM((slots - 1, size, size), BF16),
+            pltpu.VMEM((slots - 1, size, size), BF16),
+            pltpu.SMEM((owner_count,), jnp.int32),
+            DMA((slots, 3)),
             DMA((slots - 1,)),
         ],
         4 * slots * size**3,
@@ -288,10 +287,10 @@
     var_ref,
     left_ref,
     right_ref,
-    turned_first,
-    var_first,
     left_first,
     right_first,
+    turned_first,
+    left_second,
     var_out,
     upd_out,
     grad,
@@ -305,65 +304,74 @@
     out_of,
 ):
     slots, size, _ = kept.shape
-    reads = [[pltpu.make_async_copy(grad_ref.at[:, 0], grad.at[0], into.at[0, 0])]]
-    for s in range(1, slots):
-        pairs = (
-            (grad_ref.at[:, s], grad.at[s]),
-            (left_ref.at[s], left.at[s - 1]),
-            (right_ref.at[s], right.at[s - 1]),
-            (var_ref.at[s], var.at[s - 1]),
-            (turned_ref.at[s - 1], turned.at[s - 1]),
-        )
-        reads.append(
-            [pltpu.make_async_copy(a, b, into.at[s, k]) for k, (a, b) in enumerate(pairs)]
-        )
+    lefts = [left_first, left_second] + [left.at[s] for s in range(slots - 2)]
+    rights = [right_first] + [right.at[s] for s in range(slots - 1)]
+    turns = [turned_first] + [turned.at[s] for s in range(slots - 1)]
+    reads = []
+    for s in range(slots):
+        pairs = [(grad_ref.at[:, s], grad.at[s])]
+        if s >= 2:
+            pairs.append((left_ref.at[s], lefts[s]))
+        if s >= 1:
+            pairs.append((right_ref.at[s], rights[s]))
+        early = len(pairs)
+        pairs.append((var_ref.at[s], var.at[s]))
+        if s >= 1:
+            pairs.append((turned_ref.at[s - 1], turns[s]))
+        row = [pltpu.make_async_copy(a, b, into.at[s, k]) for k, (a, b) in enumerate(pairs)]
+        reads += [row[:early], row[early:]]
+    reads.append([])
     writes = [
-        (
-            pltpu.make_async_copy(kept.at[s], var_out.at[s], out_of.at[s, 0]),
-            pltpu.make_async_copy(upd.at[s], upd_out.at[:, s], out_of.at[s, 1]),
-        )
+        [
+            pltpu.make_async_copy(upd.at[s], upd_out.at[:, s], out_of.at[s, 0]),
+            pltpu.make_async_copy(kept.at[s], var_out.at[s], out_of.at[s, 1]),
+        ]
         for s in range(slots)
     ]
-    for row in reads:
+
+    def start(row):
         for read in row:
             read.start()
+
+    def wait(row):
+        for read in row:
+            read.wait()
+
+    def rotate(s):
+        block = grad[s].reshape(size, size)
+        return dot_nn(dot_tn(lefts[s][...], block).astype(BF16), rights[s][...])
+
+    def finish(s, rotated):
+        second = beta_second * var[s] + (1.0 - beta_second) * rotated * rotated
+        rotated_moment = turns[s][...].astype(F32) + (1.0 - beta_moment) * rotated
+        direction = (rotated_moment / (jnp.sqrt(second) + epsilon)).astype(BF16)
+        back_half = dot_nn(lefts[s][...], direction).astype(BF16)
+        update = dot_nt(back_half, rights[s][...]).astype(BF16)
+        upd[s] = update.reshape(grad.shape[1:])
+        kept[s] = jnp.where(s < load_ref[0], second, var[s])
+
+    for row in reads[:3]:
+        start(row)
+    wait(reads[0])
+    start(reads[3])
+    start(reads[4])
+    rotated = rotate(0)
     for s in range(slots):
-        for read in reads[s]:
-            read.wait()
-        at = (lambda ref, first: ref.at[s - 1]) if s else (lambda ref, first: first)
-        old = at(var, var_first)
-
-        @pl.when(s < load_ref[0])
-        def _():
-            one = at(left, left_first)[...]
-            other = at(right, right_first)[...]
-            block = grad[s].reshape(size, size)
-            rotated = dot_nn(dot_tn(one, block).astype(BF16), other)
-            second = beta_second * old[...] + (1.0 - beta_second) * rotated * rotated
-            kept[s] = second
-            rotated_moment = at(turned, turned_first)[...] + (1.0 - beta_moment) * rotated
-            direction = (rotated_moment / (jnp.sqrt(second) + epsilon)).astype(BF16)
-            back_half = dot_nn(one, direction).astype(BF16)
-            update = dot_nt(back_half, other).astype(BF16)
-            upd[s] = update.reshape(upd.shape[1:])
-
-        @pl.when(s >= load_ref[0])
-        def _():
-            kept[s] = old[...]
-
-        for write in writes[s]:
-            write.start()
+        wait(reads[2 * s + 1])
+        wait(reads[2 * s + 2])
+        for row in reads[2 * s + 5 : 2 * s + 7]:
+            start(row)
+        ahead = rotate(s + 1) if s + 1 < slots else None
+        finish(s, rotated)
+        start(writes[s])
+        rotated = ahead
     for row in writes:
-        for write in row:
-            write.wait()
-
-
-def owner_step(load, grad, prepared, variance, left_basis, right_basis):
+        wait(row)
+
+
+def owner_step(load, grad, turned, variance, left_basis, right_basis, *first):
     slots, size, _ = variance.shape
     owners, _, rows, _ = grad.shape
-    slabs = pltpu.VMEM((slots, owners, rows, size), BF16)
-    others = (slots - 1, size, size)
-    *first, turned = prepared
     return call(
         step_kernel,
         "owner_step",
@@ -372,13 +380,13 @@
         + [(array, pltpu.VMEM) for array in first],
         [(variance.shape, F32, pltpu.HBM), (grad.shape, BF16, pltpu.HBM)],
         [
-            slabs,
-            pltpu.VMEM(others, F32),
-            pltpu.VMEM(others, F32),
-            pltpu.VMEM(others, BF16),
-            pltpu.VMEM(others, BF16),
+            pltpu.VMEM((slots, owners, rows, size), BF16),
+            pltpu.VMEM((slots - 1, size, size), BF16),
             pltpu.VMEM(variance.shape, F32),
-            slabs,
+            pltpu.VMEM((slots - 2, size, size), BF16),
+            pltpu.VMEM((slots - 1, size, size), BF16),
+            pltpu.VMEM(variance.shape, F32),
+            pltpu.VMEM((slots, owners, rows, size), BF16),
             DMA((slots, 5)),
             DMA((slots, 2)),
         ],
@@ -479,29 +487,28 @@
     up = lambda x: lax.ppermute(x, "dp", [(i, (i + 1) % REPLICAS) for i in range(REPLICAS)])
     down = lambda x: lax.ppermute(x, "dp", [((i + 1) % REPLICAS, i) for i in range(REPLICAS)])
 
-    here = group.reshape(1)
-    relay_up, relay_down, near_up, near_down = copy_halves(
-        local, here, ((2, 0), (2, 1), (1, 1), (3, 0)), "copy_sends"
-    )
+    here = jnp.stack([group, own_index])
+    relay_up, relay_down = copy_halves(local, here, ((2, 0), (2, 1)), "copy_relayed")
     relay_up, relay_down = up(relay_up), down(relay_down)
+    near_up, near_down, own_up, own_down, own_a, own_b = copy_halves(
+        local, here, ((1, 1), (3, 0), (1, 0), (3, 1), (0, 0), (0, 1)), "copy_rest"
+    )
     near_up, near_down = up(near_up), down(near_down)
-    own_up, own_down, own_a, own_b = copy_halves(
-        local, here, ((1, 0), (3, 1), (0, 0), (0, 1)), "copy_own"
-    )
-    prepared = turn_moment(momentum, variance, left_basis, right_basis)
-    relay_up, relay_down, prepared = lax.optimization_barrier((relay_up, relay_down, prepared))
     ahead, behind = add_relayed(own_up, own_down, relay_up, relay_down)
+    table = owner_table[:, :, 0]
+    ahead, behind, table = lax.optimization_barrier((ahead, behind, table))
     ahead, behind = up(ahead), down(behind)
-
-    owners = lax.dynamic_index_in_dim(owner_table[:, :, 0], group, 0, keepdims=False)
-    place = owners * capacity + owner_ranks(owners)
-    load = jnp.sum((owners == own_index).astype(jnp.int32)).reshape(1)
+    place, load, *first, turned = turn_moment(
+        here, table, owner_count, momentum, left_basis, right_basis
+    )
 
     outgoing = sum_and_place(
         (own_a, own_b), (ahead, near_down), (near_up, behind), place, owner_count * capacity
     ).reshape(owner_count, capacity, rows, width)
     grad = exchange(outgoing)
-    new_variance, update = owner_step(load, grad, prepared, variance, left_basis, right_basis)
+    new_variance, update = owner_step(
+        load, grad, turned, variance, left_basis, right_basis, *first
+    )
     returned = exchange(update)
     new_momentum, new_left, new_right = rest_of_state(
         load, grad, momentum, left_factor, right_factor

time: 103 us -> 99.3 us (0.964)
  other arithmetic: 1.47 us -> 0.08 us
  local copies, waits for them, and re-layouts: 1.31 us -> 0.01 us
  starting transfers between devices: 12.6 us -> 11.5 us
    ppermute x3, waiting for transfers between devices: 8.43 us -> 12.5 us  [body(): lax.ppermute(x, 'dp', [(i, (i + 1) % REPLICAS) for i in range(REPLICAS)])]
    ppermute x3, waiting for transfers between devices: 3.81 us -> 0.01 us  [body(): lax.ppermute(x, 'dp', [((i + 1) % REPLICAS, i) for i in range(REPLICAS)])]
    reduce_sum x2 -> x0, other arithmetic: 1.47 us -> none  [the longest x1 1.29 us: body(): load = jnp.sum((owners == own_index).astype(jnp.int32)).reshape(1)]
    unnamed x2, local copies, waits for them, and re-layouts: 1.31 us -> 0.01 us
    all_to_all x1, starting transfers between devices: 4.89 us -> 3.77 us  [exchange(): lax.all_to_all(slabs, 'shard', split_axis=0, concat_axis=0, tiled=True)]
  transfers between devices with their start and end apart: 7 -> 7, of which waited for: 3 -> 3; matrix products, arithmetic and copies ran while one was open for 1% -> 0% of each run, Pallas kernels for 12% -> 14%
where the time goes in v3:
time: 99.3 us; the launch traced here: 99 us
  blocking collectives  32.7 us (33%)
  waiting for transfers between devices  29.7 us (30%)
  Pallas kernels  24.2 us (24%)
  starting transfers between devices  11.5 us (12%)
    all_to_all x1, blocking collectives, exchange(): lax.all_to_all(slabs, 'shard', split_axis=0, concat_axis=0, tiled=True)  32.7 us
    pallas_call x8, Pallas kernels, call(): pl.pallas_call(kernel, out_shape=[jax.ShapeDtypeStruct(shape, dtype) if w...  24.2 us
    all_to_all x1, waiting for transfers between devices, exchange(): lax.all_to_all(slabs, 'shard', split_axis=0, concat_axis=0, tiled=True)  17.2 us
    ppermute x3, waiting for transfers between devices, body(): lax.ppermute(x, 'dp', [(i, (i + 1) % REPLICAS) for i in range(REPLICAS)])  12.5 us
    ppermute x3, starting transfers between devices, body(): lax.ppermute(x, 'dp', [((i + 1) % REPLICAS, i) for i in range(REPLICAS)])  4.27 us
    all_to_all x1, starting transfers between devices, exchange(): lax.all_to_all(slabs, 'shard', split_axis=0, concat_axis=0, tiled=True)  3.77 us
    ppermute x3, starting transfers between devices, body(): lax.ppermute(x, 'dp', [(i, (i + 1) % REPLICAS) for i in range(REPLICAS)])  3.47 us
  transfers between devices with their start and end apart: 7, of which 3 were waited for; matrix products, arithmetic and copies ran while one was open for 0% of the time, Pallas kernels for 14%

profile of v3, /device:TPU:1, one launch (start us, length us, event | category | flops | bytes accessed | tf_op | source)
XLA Modules:
  0.0 99.0 jit_solution(14952768538094864895)
XLA Ops:
  0.6 0.1 pad_add_fusion.group_ref.here_ref
  0.7 1.8 %copy_relayed.1 = (bf16[24,16,512]{2,1,0:T(8,128)(2,1)S(1)}, bf16[24,16,512]{2,1,0:T(8,128)(2,1)S(1)}) custom-call(s32[2]{0:T(128)S(1)} %pad_add_fusion.group_ref.here_ref, bf16[192,16,512]{2,1,0:T(8,128)(2,1)} %bitcast.9), custom_call_target="tpu_custom_call" | custom-call | bytes 786432 | tf_op jit(solution)/shard_map/copy_relayed/pallas_call | solution.py:47
  2.5 2.1 %collective-permute-start = (bf16[24,16,512]{2,1,0:T(8,128)(2,1)S(1)}, bf16[24,16,512]{2,1,0:T(8,128)(2,1)S(1)}, u32[]{:S(2)}, u32[]{:S(2)}) collective-permute-start(bf16[24,16,512]{2,1,0:T(8,128)(2,1)S(1)} %get-tuple-element.32), channel_id=1, source_target_pairs={{0,32},{32,64},{64,96},{96,0},{1,33},{33,65},{65,97},{97,1},{2,34}... | collective-permute-start | bytes 1179656 | tf_op jit(solution)/shard_map/ppermute | solution.py:487
  4.6 1.3 %collective-permute-start.1 = (bf16[24,16,512]{2,1,0:T(8,128)(2,1)S(1)}, bf16[24,16,512]{2,1,0:T(8,128)(2,1)S(1)}, u32[]{:S(2)}, u32[]{:S(2)}) collective-permute-start(bf16[24,16,512]{2,1,0:T(8,128)(2,1)S(1)} %get-tuple-element.33), channel_id=1, source_target_pairs={{32,0},{64,32},{96,64},{0,96},{33,1},{65,33},{97,65},{1,97},{34,2}... | collective-permute-start | bytes 1179656 | tf_op jit(solution)/shard_map/ppermute | solution.py:488
  6.0 2.3 %copy_rest.1 = (bf16[24,16,512]{2,1,0:T(8,128)(2,1)S(1)}, bf16[24,16,512]{2,1,0:T(8,128)(2,1)S(1)}, bf16[24,16,512]{2,1,0:T(8,128)(2,1)S(1)}, bf16[24,16,512]{2,...) custom-call(s32[2]{0:T(128)S(1)} %pad_add_fusion.group_ref.here_ref, ...), custom_call_target="tpu_custom_call" | custom-call | bytes 2359296 | tf_op jit(solution)/shard_map/copy_rest/pallas_call | solution.py:47
  8.3 0.0 copy-start
  8.3 1.5 %collective-permute-start.3 = (bf16[24,16,512]{2,1,0:T(8,128)(2,1)S(1)}, bf16[24,16,512]{2,1,0:T(8,128)(2,1)S(1)}, u32[]{:S(2)}, u32[]{:S(2)}) collective-permute-start(bf16[24,16,512]{2,1,0:T(8,128)(2,1)S(1)} %get-tuple-element.42), channel_id=1, source_target_pairs={{32,0},{64,32},{96,64},{0,96},{33,1},{65,33},{97,65},{1,97},{34,2}... | collective-permute-start | bytes 1179656 | tf_op jit(solution)/shard_map/ppermute | solution.py:488
  9.8 0.1 collective-permute-start.4
  9.9 4.4 %collective-permute-done.a_ref = bf16[24,16,512]{2,1,0:T(8,128)(2,1)S(1)} collective-permute-done((bf16[24,16,512]{2,1,0:T(8,128)(2,1)S(1)}, bf16[24,16,512]{2,1,0:T(8,128)(2,1)S(1)}, u32[]{:S(2)}, u32[]{:S(2)}) %collective-permute-start) | collective-permute-done | bytes 393248 | tf_op jit(solution)/shard_map/ppermute | solution.py:487
  14.3 0.0 collective-permute-done.1.b_ref
  14.3 0.2 add_relayed.1
  14.5 1.3 %collective-permute-start.2 = (bf16[24,16,512]{2,1,0:T(8,128)(2,1)S(1)}, bf16[24,16,512]{2,1,0:T(8,128)(2,1)S(1)}, u32[]{:S(2)}, u32[]{:S(2)}) collective-permute-start(bf16[24,16,512]{2,1,0:T(8,128)(2,1)S(1)} %get-tuple-element.41), channel_id=1, source_target_pairs={{0,32},{32,64},{64,96},{96,0},{1,33},{33,65},{65,97},{97,1},{2,34}... | collective-permute-start | bytes 1179656 | tf_op jit(solution)/shard_map/ppermute | solution.py:487
  15.8 1.5 %collective-permute-start.5 = (bf16[24,16,512]{2,1,0:T(8,128)(2,1)S(1)}, bf16[24,16,512]{2,1,0:T(8,128)(2,1)S(1)}, u32[]{:S(2)}, u32[]{:S(2)}) collective-permute-start(bf16[24,16,512]{2,1,0:T(8,128)(2,1)S(1)} %get-tuple-element.44), channel_id=1, source_target_pairs={{32,0},{64,32},{96,64},{0,96},{33,1},{65,33},{97,65},{1,97},{34,2}... | collective-permute-start | bytes 1179656 | tf_op jit(solution)/shard_map/ppermute | solution.py:488
  17.2 0.0 copy-done
  17.2 5.8 %turn_moment.1 = (s32[48]{0:T(128)S(4)}, s32[1]{0:T(128)S(4)}, bf16[512,512]{1,0:T(8,128)(2,1)S(1)}, bf16[512,512]{1,0:T(8,128)(2,1)S(1)}, bf16[512,512]{1,0:T(8...) custom-call(s32[2]{0:T(128)S(1)} %pad_add_fusion.group_ref.here_ref, s32[4,48]{1,0:T(4,128)S(1)} %bitcast.8, ...), custom_call_target="tpu_custom_call" | custom-call | flops 1610612736 | bytes 9437184 | tf_op jit(solution)/shard_map/turn_moment/pallas_call | solution.py:47
  23.0 0.0 collective-permute-done.3.a2
  23.0 0.0 collective-permute-done.4.b1
  23.1 8.1 %collective-permute-done.2.a1 = bf16[24,16,512]{2,1,0:T(8,128)(2,1)S(1)} collective-permute-done((bf16[24,16,512]{2,1,0:T(8,128)(2,1)S(1)}, bf16[24,16,512]{2,1,0:T(8,128)(2,1)S(1)}, u32[]{:S(2)}, u32[]{:S(2)}) %collective-permute-start.2) | collective-permute-done | bytes 393248 | tf_op jit(solution)/shard_map/ppermute | solution.py:487
  31.1 0.0 collective-permute-done.5.b2
  31.1 0.4 sum_and_place.1
  31.5 32.7 %all_to_all.10.grad_ref = bf16[32,3,16,512]{3,2,1,0:T(8,128)(2,1)} all-to-all(bf16[32,3,16,512]{3,2,1,0:T(8,128)(2,1)S(1)} %bitcast.7), channel_id=1, replica_groups=mesh['dp'=4,'shard'=32] {'shard'}, dimensions={0} | all-to-all | bytes 3145728 | tf_op jit(solution)/shard_map/all_to_all | solution.py:475
  64.2 7.6 %owner_step.1 = (f32[3,512,512]{2,1,0:T(8,128)}, bf16[32,3,16,512]{3,2,1,0:T(8,128)(2,1)}) custom-call(s32[1]{0:T(128)S(4)} %get-tuple-element.38.load_ref, bf16[32,3,16,512]{3,2,1,0:T(8,128)(2,1)} %all_to_all.10.grad_ref, bf16[2,512,512]{2,1,0:T(8,128)(2,1)} %get-tuple-element.45.turned_ref, f32[3,512,512]{2,1,0:T(8,128)} %var_ref.1, ...), custom_call_target="tpu_custom_call" | custom-call | flops 3221225472 | bytes 6291456 | tf_op jit(solution)/shard_map/owner_step/pallas_call | solution.py:47
  71.8 3.8 %all-to-all-start.1 = ((bf16[32,3,16,512]{3,2,1,0:T(8,128)(2,1)}), bf16[32,3,16,512]{3,2,1,0:T(8,128)(2,1)S(1)}, u32[]{:S(2)}, u32[]{:S(2)}) async-start(bf16[32,3,16,512]{3,2,1,0:T(8,128)(2,1)} %get-tuple-element.50), calls=%async_computation.1 | async-start | bytes 3145728 | tf_op jit(solution)/shard_map/all_to_all | solution.py:475
  75.6 5.3 %rest_of_state.1 = (f32[3,512,512]{2,1,0:T(8,128)}, bf16[3,512,512]{2,1,0:T(8,128)(2,1)}, bf16[3,512,512]{2,1,0:T(8,128)(2,1)}) custom-call(s32[1]{0:T(128)S(4)} %get-tuple-element.38.load_ref, bf16[32,3,16,512]{3,2,1,0:T(8,128)(2,1)} %all_to_all.10.grad_ref, f32[3,512,512]{2,1,0:T(8,128)} %mom_ref.3, bf16[3,512,512]{2,1,0:T(8,128)(2,1)} %left_ref.5, ...), custom_call_target="tpu_custom_call" | custom-call | flops 1610612736 | bytes 14155776 | tf_op jit(solution)/shard_map/rest_of_state/pallas_call | solution.py:47
  80.9 17.2 %all-to-all-done.1 = bf16[32,3,16,512]{3,2,1,0:T(8,128)(2,1)S(1)} async-done(((bf16[32,3,16,512]{3,2,1,0:T(8,128)(2,1)}), bf16[32,3,16,512]{3,2,1,0:T(8,128)(2,1)S(1)}, u32[]{:S(2)}, u32[]{:S(2)}) %all-to-all-start.1) | async-done | bytes 1572896 | tf_op jit(solution)/shard_map/all_to_all | solution.py:475
  98.2 0.9 take_blocks.1
Async XLA Ops:
  2.5 11.8 %collective-permute-start = (bf16[24,16,512]{2,1,0:T(8,128)(2,1)S(1)}, bf16[24,16,512]{2,1,0:T(8,128)(2,1)S(1)}, u32[]{:S(2)}, u32[]{:S(2)}) collective-permute-start(bf16[24,16,512]{2,1,0:T(8,128)(2,1)S(1)} %get-tuple-element.32), channel_id=1, source_target_pairs={{0,32},{32,64},{64,96},{96,0},{1,33},{33,65},{65,97},{97,1},{2,34}... | collective-permute-start | bytes 1179656 | tf_op jit(solution)/shard_map/ppermute | solution.py:487
  4.6 9.7 %collective-permute-start.1 = (bf16[24,16,512]{2,1,0:T(8,128)(2,1)S(1)}, bf16[24,16,512]{2,1,0:T(8,128)(2,1)S(1)}, u32[]{:S(2)}, u32[]{:S(2)}) collective-permute-start(bf16[24,16,512]{2,1,0:T(8,128)(2,1)S(1)} %get-tuple-element.33), channel_id=1, source_target_pairs={{32,0},{64,32},{96,64},{0,96},{33,1},{65,33},{97,65},{1,97},{34,2}... | collective-permute-start | bytes 1179656 | tf_op jit(solution)/shard_map/ppermute | solution.py:488
  8.3 8.9 %copy-start = (s32[4,48,1]{1,2,0:T(1,128)S(1)}, s32[4,48,1]{1,2,0:T(1,128)}, u32[]{:S(2)}) copy-start(s32[4,48,1]{1,2,0:T(1,128)} %param.9) | copy-start | bytes 2308
  8.3 14.7 %collective-permute-start.3 = (bf16[24,16,512]{2,1,0:T(8,128)(2,1)S(1)}, bf16[24,16,512]{2,1,0:T(8,128)(2,1)S(1)}, u32[]{:S(2)}, u32[]{:S(2)}) collective-permute-start(bf16[24,16,512]{2,1,0:T(8,128)(2,1)S(1)} %get-tuple-element.42), channel_id=1, source_target_pairs={{32,0},{64,32},{96,64},{0,96},{33,1},{65,33},{97,65},{1,97},{34,2}... | collective-permute-start | bytes 1179656 | tf_op jit(solution)/shard_map/ppermute | solution.py:488
  9.8 13.3 %collective-permute-start.4 = (bf16[24,16,512]{2,1,0:T(8,128)(2,1)S(1)}, bf16[24,16,512]{2,1,0:T(8,128)(2,1)S(1)}, u32[]{:S(2)}, u32[]{:S(2)}) collective-permute-start(bf16[24,16,512]{2,1,0:T(8,128)(2,1)S(1)} %get-tuple-element.43), channel_id=1, source_target_pairs={{0,32},{32,64},{64,96},{96,0},{1,33},{33,65},{65,97},{97,1},{2,34}... | collective-permute-start | bytes 1179656 | tf_op jit(solution)/shard_map/ppermute | solution.py:487
  14.5 16.6 %collective-permute-start.2 = (bf16[24,16,512]{2,1,0:T(8,128)(2,1)S(1)}, bf16[24,16,512]{2,1,0:T(8,128)(2,1)S(1)}, u32[]{:S(2)}, u32[]{:S(2)}) collective-permute-start(bf16[24,16,512]{2,1,0:T(8,128)(2,1)S(1)} %get-tuple-element.41), channel_id=1, source_target_pairs={{0,32},{32,64},{64,96},{96,0},{1,33},{33,65},{65,97},{97,1},{2,34}... | collective-permute-start | bytes 1179656 | tf_op jit(solution)/shard_map/ppermute | solution.py:487
  15.8 15.4 %collective-permute-start.5 = (bf16[24,16,512]{2,1,0:T(8,128)(2,1)S(1)}, bf16[24,16,512]{2,1,0:T(8,128)(2,1)S(1)}, u32[]{:S(2)}, u32[]{:S(2)}) collective-permute-start(bf16[24,16,512]{2,1,0:T(8,128)(2,1)S(1)} %get-tuple-element.44), channel_id=1, source_target_pairs={{32,0},{64,32},{96,64},{0,96},{33,1},{65,33},{97,65},{1,97},{34,2}... | collective-permute-start | bytes 1179656 | tf_op jit(solution)/shard_map/ppermute | solution.py:488
  71.8 26.3 %all-to-all-start.1 = ((bf16[32,3,16,512]{3,2,1,0:T(8,128)(2,1)}), bf16[32,3,16,512]{3,2,1,0:T(8,128)(2,1)S(1)}, u32[]{:S(2)}, u32[]{:S(2)}) async-start(bf16[32,3,16,512]{3,2,1,0:T(8,128)(2,1)} %get-tuple-element.50), calls=%async_computation.1 | async-start | bytes 3145728 | tf_op jit(solution)/shard_map/all_to_all | solution.py:475

commit v4 on v3

--- a/solution.py
+++ b/solution.py
@@ -67,9 +67,9 @@
     return lax.rem(group + hops, REPLICAS)
 
 
-def copy_kernel(halves, group_ref, local_ref, *refs):
+def copy_kernel(halves, local_ref, *refs):
     outs, sem = refs[:-1], refs[-1]
-    group = group_ref[0]
+    group = lax.axis_index("dp")
     count = outs[0].shape[0]
     step = count // CUTS
     reads = []
@@ -88,13 +88,13 @@
         read.wait()
 
 
-def copy_halves(local, group, halves, name):
+def copy_halves(local, halves, name):
     blocks, rows, width = local.shape
     count = blocks // REPLICAS // 2
     return call(
         functools.partial(copy_kernel, halves),
         name,
-        (group,),
+        (),
         [(local, pltpu.HBM)],
         [((count, rows, width), BF16, pltpu.VMEM)] * len(halves),
         [DMA((len(halves), CUTS))],
@@ -103,27 +103,25 @@
     )
 
 
-def add_kernel(up_ref, down_ref, a_ref, b_ref, up_out, down_out):
+def add_kernel(own_ref, got_ref, out_ref):
     def step(j, carry):
-        up_out[j] = (up_ref[j].astype(F32) + a_ref[j].astype(F32)).astype(BF16)
-        down_out[j] = (down_ref[j].astype(F32) + b_ref[j].astype(F32)).astype(BF16)
+        out_ref[j] = (own_ref[j].astype(F32) + got_ref[j].astype(F32)).astype(BF16)
         return carry
 
-    lax.fori_loop(0, up_ref.shape[0], step, 0, unroll=4)
-
-
-def add_relayed(own_up, own_down, up, down):
-    count, rows, width = up.shape
+    lax.fori_loop(0, own_ref.shape[0], step, 0, unroll=4)
+
+
+def add_relayed(own, got, name):
     return call(
         add_kernel,
-        "add_relayed",
+        name,
         (),
-        [(array, pltpu.VMEM) for array in (own_up, own_down, up, down)],
-        [((count, rows, width), BF16, pltpu.VMEM)] * 2,
+        [(own, pltpu.VMEM), (got, pltpu.VMEM)],
+        [(own.shape, BF16, pltpu.VMEM)],
         [],
-        2 * count * rows * width,
-        12 * count * rows * width,
-    )
+        own.size,
+        6 * own.size,
+    )[0]
 
 
 def place_kernel(place_ref, own_a, own_b, a1, a2, b1, b2, out_ref):
@@ -177,7 +175,6 @@
 
 
 def turn_kernel(
-    here_ref,
     table_ref,
     mom_ref,
     left_ref,
@@ -217,7 +214,7 @@
             read.start()
 
     owner_count = counts.shape[0]
-    group, own_index = here_ref[0], here_ref[1]
+    group, own_index = lax.axis_index("dp"), lax.axis_index("shard")
 
     def clear(i, carry):
         counts[i] = 0
@@ -248,13 +245,13 @@
         write.wait()
 
 
-def turn_moment(here, table, owner_count, momentum, left_basis, right_basis):
+def turn_moment(table, owner_count, momentum, left_basis, right_basis):
     slots, size, _ = momentum.shape
     square = (size, size)
     return call(
         turn_kernel,
         "turn_moment",
-        (here,),
+        (),
         [(table, pltpu.SMEM)]
         + [(array, pltpu.HBM) for array in (momentum, left_basis, right_basis)],
         [
@@ -329,10 +326,6 @@
         for s in range(slots)
     ]
 
-    def start(row):
-        for read in row:
-            read.start()
-
     def wait(row):
         for read in row:
             read.wait()
@@ -343,27 +336,25 @@
 
     def finish(s, rotated):
         second = beta_second * var[s] + (1.0 - beta_second) * rotated * rotated
+        kept[s] = jnp.where(s < load_ref[0], second, var[s])
+        writes[s][1].start()
         rotated_moment = turns[s][...].astype(F32) + (1.0 - beta_moment) * rotated
         direction = (rotated_moment / (jnp.sqrt(second) + epsilon)).astype(BF16)
         back_half = dot_nn(lefts[s][...], direction).astype(BF16)
         update = dot_nt(back_half, rights[s][...]).astype(BF16)
         upd[s] = update.reshape(grad.shape[1:])
-        kept[s] = jnp.where(s < load_ref[0], second, var[s])
-
-    for row in reads[:3]:
-        start(row)
+        writes[s][0].start()
+
+    for row in reads:
+        for read in row:
+            read.start()
     wait(reads[0])
-    start(reads[3])
-    start(reads[4])
     rotated = rotate(0)
     for s in range(slots):
         wait(reads[2 * s + 1])
         wait(reads[2 * s + 2])
-        for row in reads[2 * s + 5 : 2 * s + 7]:
-            start(row)
         ahead = rotate(s + 1) if s + 1 < slots else None
         finish(s, rotated)
-        start(writes[s])
         rotated = ahead
     for row in writes:
         wait(row)
@@ -479,27 +470,25 @@
     grads, owner_table, momentum, variance, left_factor, right_factor, left_basis, right_basis
 ):
     owner_count = lax.axis_size("shard")
-    group = lax.axis_index("dp")
-    own_index = lax.axis_index("shard")
     capacity = momentum.shape[0]
     local = grads[0]
     _, rows, width = local.shape
     up = lambda x: lax.ppermute(x, "dp", [(i, (i + 1) % REPLICAS) for i in range(REPLICAS)])
     down = lambda x: lax.ppermute(x, "dp", [((i + 1) % REPLICAS, i) for i in range(REPLICAS)])
 
-    here = jnp.stack([group, own_index])
-    relay_up, relay_down = copy_halves(local, here, ((2, 0), (2, 1)), "copy_relayed")
+    relay_up, relay_down = copy_halves(local, ((2, 0), (2, 1)), "copy_relayed")
     relay_up, relay_down = up(relay_up), down(relay_down)
     near_up, near_down, own_up, own_down, own_a, own_b = copy_halves(
-        local, here, ((1, 1), (3, 0), (1, 0), (3, 1), (0, 0), (0, 1)), "copy_rest"
+        local, ((1, 1), (3, 0), (1, 0), (3, 1), (0, 0), (0, 1)), "copy_rest"
     )
     near_up, near_down = up(near_up), down(near_down)
-    ahead, behind = add_relayed(own_up, own_down, relay_up, relay_down)
+    ahead = add_relayed(own_up, relay_up, "add_up")
+    behind = add_relayed(own_down, relay_down, "add_down")
     table = owner_table[:, :, 0]
     ahead, behind, table = lax.optimization_barrier((ahead, behind, table))
     ahead, behind = up(ahead), down(behind)
     place, load, *first, turned = turn_moment(
-        here, table, owner_count, momentum, left_basis, right_basis
+        table, owner_count, momentum, left_basis, right_basis
     )
 
     outgoing = sum_and_place(

time: 99.3 us -> 98.3 us (0.990)
  Pallas kernels: 24.2 us -> 22.4 us
  waiting for transfers between devices: 29.7 us -> 30.7 us
    pallas_call x8 -> x9, Pallas kernels: 24.2 us -> 22.4 us  [call(): pl.pallas_call(kernel, out_shape=[jax.ShapeDtypeStruct(shape, dtype) if w...]
  transfers between devices with their start and end apart: 7 -> 7, of which waited for: 3 -> 4; matrix products, arithmetic and copies ran while one was open for 0% -> 0% of each run, Pallas kernels for 14% -> 13%
where the time goes in v4:
time: 98.3 us; the launch traced here: 98 us
  blocking collectives  32.7 us (33%)
  waiting for transfers between devices  30.7 us (31%)
  Pallas kernels  22.4 us (23%)
  starting transfers between devices  11.5 us (12%)
    all_to_all x1, blocking collectives, exchange(): lax.all_to_all(slabs, 'shard', split_axis=0, concat_axis=0, tiled=True)  32.7 us
    pallas_call x9, Pallas kernels, call(): pl.pallas_call(kernel, out_shape=[jax.ShapeDtypeStruct(shape, dtype) if w...  22.4 us
    all_to_all x1, waiting for transfers between devices, exchange(): lax.all_to_all(slabs, 'shard', split_axis=0, concat_axis=0, tiled=True)  17.1 us
    ppermute x3, waiting for transfers between devices, body(): lax.ppermute(x, 'dp', [(i, (i + 1) % REPLICAS) for i in range(REPLICAS)])  13.4 us
    ppermute x3, starting transfers between devices, body(): lax.ppermute(x, 'dp', [((i + 1) % REPLICAS, i) for i in range(REPLICAS)])  4.4 us
    all_to_all x1, starting transfers between devices, exchange(): lax.all_to_all(slabs, 'shard', split_axis=0, concat_axis=0, tiled=True)  3.77 us
    ppermute x3, starting transfers between devices, body(): lax.ppermute(x, 'dp', [(i, (i + 1) % REPLICAS) for i in range(REPLICAS)])  3.34 us
  transfers between devices with their start and end apart: 7, of which 4 were waited for; matrix products, arithmetic and copies ran while one was open for 0% of the time, Pallas kernels for 13%

profile of v4, /device:TPU:1, one launch (start us, length us, event | category | flops | bytes accessed | tf_op | source)
XLA Modules:
  0.0 98.0 jit_solution(18188579400869076219)
XLA Ops:
  0.6 1.3 %copy_relayed.1 = (bf16[24,16,512]{2,1,0:T(8,128)(2,1)S(1)}, bf16[24,16,512]{2,1,0:T(8,128)(2,1)S(1)}) custom-call(bf16[192,16,512]{2,1,0:T(8,128)(2,1)} %bitcast.7), custom_call_target="tpu_custom_call" | custom-call | bytes 786432 | tf_op jit(solution)/shard_map/copy_relayed/pallas_call | solution.py:47
  1.9 2.1 %collective-permute-start = (bf16[24,16,512]{2,1,0:T(8,128)(2,1)S(1)}, bf16[24,16,512]{2,1,0:T(8,128)(2,1)S(1)}, u32[]{:S(2)}, u32[]{:S(2)}) collective-permute-start(bf16[24,16,512]{2,1,0:T(8,128)(2,1)S(1)} %get-tuple-element.29), channel_id=1, source_target_pairs={{0,32},{32,64},{64,96},{96,0},{1,33},{33,65},{65,97},{97,1},{2,34}... | collective-permute-start | bytes 1179656 | tf_op jit(solution)/shard_map/ppermute | solution.py:476
  4.0 1.3 %collective-permute-start.1 = (bf16[24,16,512]{2,1,0:T(8,128)(2,1)S(1)}, bf16[24,16,512]{2,1,0:T(8,128)(2,1)S(1)}, u32[]{:S(2)}, u32[]{:S(2)}) collective-permute-start(bf16[24,16,512]{2,1,0:T(8,128)(2,1)S(1)} %get-tuple-element.31), channel_id=1, source_target_pairs={{32,0},{64,32},{96,64},{0,96},{33,1},{65,33},{97,65},{1,97},{34,2}... | collective-permute-start | bytes 1179656 | tf_op jit(solution)/shard_map/ppermute | solution.py:477
  5.4 1.8 %copy_rest.1 = (bf16[24,16,512]{2,1,0:T(8,128)(2,1)S(1)}, bf16[24,16,512]{2,1,0:T(8,128)(2,1)S(1)}, bf16[24,16,512]{2,1,0:T(8,128)(2,1)S(1)}, bf16[24,16,512]{2,...) custom-call(bf16[192,16,512]{2,1,0:T(8,128)(2,1)} %bitcast.8), custom_call_target="tpu_custom_call" | custom-call | bytes 2359296 | tf_op jit(solution)/shard_map/copy_rest/pallas_call | solution.py:47
  7.2 0.0 copy-start
  7.2 1.5 %collective-permute-start.3 = (bf16[24,16,512]{2,1,0:T(8,128)(2,1)S(1)}, bf16[24,16,512]{2,1,0:T(8,128)(2,1)S(1)}, u32[]{:S(2)}, u32[]{:S(2)}) collective-permute-start(bf16[24,16,512]{2,1,0:T(8,128)(2,1)S(1)} %get-tuple-element.38), channel_id=1, source_target_pairs={{32,0},{64,32},{96,64},{0,96},{33,1},{65,33},{97,65},{1,97},{34,2}... | collective-permute-start | bytes 1179656 | tf_op jit(solution)/shard_map/ppermute | solution.py:477
  8.6 0.1 collective-permute-start.4
  8.7 5.0 %collective-permute-done.got_ref = bf16[24,16,512]{2,1,0:T(8,128)(2,1)S(1)} collective-permute-done((bf16[24,16,512]{2,1,0:T(8,128)(2,1)S(1)}, bf16[24,16,512]{2,1,0:T(8,128)(2,1)S(1)}, u32[]{:S(2)}, u32[]{:S(2)}) %collective-permute-start) | collective-permute-done | bytes 393248 | tf_op jit(solution)/shard_map/ppermute | solution.py:476
  13.7 0.1 add_up.1
  13.8 0.0 collective-permute-done.1.got_ref
  13.8 0.1 add_down.1
  13.9 1.1 %collective-permute-start.2 = (bf16[24,16,512]{2,1,0:T(8,128)(2,1)S(1)}, bf16[24,16,512]{2,1,0:T(8,128)(2,1)S(1)}, u32[]{:S(2)}, u32[]{:S(2)}) collective-permute-start(bf16[24,16,512]{2,1,0:T(8,128)(2,1)S(1)} %add_up.1), channel_id=1, source_target_pairs={{0,32},{32,64},{64,96},{96,0},{1,33},{33,65},{65,97},{97,1},{2,34}... | collective-permute-start | bytes 1179656 | tf_op jit(solution)/shard_map/ppermute | solution.py:476
  15.1 1.6 %collective-permute-start.5 = (bf16[24,16,512]{2,1,0:T(8,128)(2,1)S(1)}, bf16[24,16,512]{2,1,0:T(8,128)(2,1)S(1)}, u32[]{:S(2)}, u32[]{:S(2)}) collective-permute-start(bf16[24,16,512]{2,1,0:T(8,128)(2,1)S(1)} %add_down.1), channel_id=1, source_target_pairs={{32,0},{64,32},{96,64},{0,96},{33,1},{65,33},{97,65},{1,97},{34,2}... | collective-permute-start | bytes 1179656 | tf_op jit(solution)/shard_map/ppermute | solution.py:477
  16.7 0.0 copy-done
  16.7 5.2 %turn_moment.1 = (s32[48]{0:T(128)S(4)}, s32[1]{0:T(128)S(4)}, bf16[512,512]{1,0:T(8,128)(2,1)S(1)}, bf16[512,512]{1,0:T(8,128)(2,1)S(1)}, bf16[512,512]{1,0:T(8...) custom-call(s32[4,48]{1,0:T(4,128)S(1)} %bitcast.6, f32[3,512,512]{2,1,0:T(8,128)} %mom_ref.3, ...), custom_call_target="tpu_custom_call" | custom-call | flops 1610612736 | bytes 9437184 | tf_op jit(solution)/shard_map/turn_moment/pallas_call | solution.py:47
  21.9 0.2 collective-permute-done.3.a2
  22.1 0.0 collective-permute-done.4.b1
  22.1 8.4 %collective-permute-done.2.a1 = bf16[24,16,512]{2,1,0:T(8,128)(2,1)S(1)} collective-permute-done((bf16[24,16,512]{2,1,0:T(8,128)(2,1)S(1)}, bf16[24,16,512]{2,1,0:T(8,128)(2,1)S(1)}, u32[]{:S(2)}, u32[]{:S(2)}) %collective-permute-start.2) | collective-permute-done | bytes 393248 | tf_op jit(solution)/shard_map/ppermute | solution.py:476
  30.5 0.0 collective-permute-done.5.b2
  30.5 0.3 sum_and_place.1
  30.9 32.7 %all_to_all.10.grad_ref = bf16[32,3,16,512]{3,2,1,0:T(8,128)(2,1)} all-to-all(bf16[32,3,16,512]{3,2,1,0:T(8,128)(2,1)S(1)} %bitcast.5), channel_id=1, replica_groups=mesh['dp'=4,'shard'=32] {'shard'}, dimensions={0} | all-to-all | bytes 3145728 | tf_op jit(solution)/shard_map/all_to_all | solution.py:466
  63.6 7.2 %owner_step.1 = (f32[3,512,512]{2,1,0:T(8,128)}, bf16[32,3,16,512]{3,2,1,0:T(8,128)(2,1)}) custom-call(s32[1]{0:T(128)S(4)} %get-tuple-element.34.load_ref, bf16[32,3,16,512]{3,2,1,0:T(8,128)(2,1)} %all_to_all.10.grad_ref, bf16[2,512,512]{2,1,0:T(8,128)(2,1)} %get-tuple-element.41.turned_ref, f32[3,512,512]{2,1,0:T(8,128)} %var_ref.1, ...), custom_call_target="tpu_custom_call" | custom-call | flops 3221225472 | bytes 6291456 | tf_op jit(solution)/shard_map/owner_step/pallas_call | solution.py:47
  70.9 3.8 %all-to-all-start.1 = ((bf16[32,3,16,512]{3,2,1,0:T(8,128)(2,1)}), bf16[32,3,16,512]{3,2,1,0:T(8,128)(2,1)S(1)}, u32[]{:S(2)}, u32[]{:S(2)}) async-start(bf16[32,3,16,512]{3,2,1,0:T(8,128)(2,1)} %get-tuple-element.46), calls=%async_computation.1 | async-start | bytes 3145728 | tf_op jit(solution)/shard_map/all_to_all | solution.py:466
  74.6 5.4 %rest_of_state.1 = (f32[3,512,512]{2,1,0:T(8,128)}, bf16[3,512,512]{2,1,0:T(8,128)(2,1)}, bf16[3,512,512]{2,1,0:T(8,128)(2,1)}) custom-call(s32[1]{0:T(128)S(4)} %get-tuple-element.34.load_ref, bf16[32,3,16,512]{3,2,1,0:T(8,128)(2,1)} %all_to_all.10.grad_ref, f32[3,512,512]{2,1,0:T(8,128)} %mom_ref.3, bf16[3,512,512]{2,1,0:T(8,128)(2,1)} %left_ref.5, ...), custom_call_target="tpu_custom_call" | custom-call | flops 1610612736 | bytes 14155776 | tf_op jit(solution)/shard_map/rest_of_state/pallas_call | solution.py:47
  80.1 17.1 %all-to-all-done.1 = bf16[32,3,16,512]{3,2,1,0:T(8,128)(2,1)S(1)} async-done(((bf16[32,3,16,512]{3,2,1,0:T(8,128)(2,1)}), bf16[32,3,16,512]{3,2,1,0:T(8,128)(2,1)S(1)}, u32[]{:S(2)}, u32[]{:S(2)}) %all-to-all-start.1) | async-done | bytes 1572896 | tf_op jit(solution)/shard_map/all_to_all | solution.py:466
  97.2 0.9 take_blocks.1
Async XLA Ops:
  1.9 11.8 %collective-permute-start = (bf16[24,16,512]{2,1,0:T(8,128)(2,1)S(1)}, bf16[24,16,512]{2,1,0:T(8,128)(2,1)S(1)}, u32[]{:S(2)}, u32[]{:S(2)}) collective-permute-start(bf16[24,16,512]{2,1,0:T(8,128)(2,1)S(1)} %get-tuple-element.29), channel_id=1, source_target_pairs={{0,32},{32,64},{64,96},{96,0},{1,33},{33,65},{65,97},{97,1},{2,34}... | collective-permute-start | bytes 1179656 | tf_op jit(solution)/shard_map/ppermute | solution.py:476
  4.0 9.8 %collective-permute-start.1 = (bf16[24,16,512]{2,1,0:T(8,128)(2,1)S(1)}, bf16[24,16,512]{2,1,0:T(8,128)(2,1)S(1)}, u32[]{:S(2)}, u32[]{:S(2)}) collective-permute-start(bf16[24,16,512]{2,1,0:T(8,128)(2,1)S(1)} %get-tuple-element.31), channel_id=1, source_target_pairs={{32,0},{64,32},{96,64},{0,96},{33,1},{65,33},{97,65},{1,97},{34,2}... | collective-permute-start | bytes 1179656 | tf_op jit(solution)/shard_map/ppermute | solution.py:477
  7.2 9.5 %copy-start = (s32[4,48,1]{1,2,0:T(1,128)S(1)}, s32[4,48,1]{1,2,0:T(1,128)}, u32[]{:S(2)}) copy-start(s32[4,48,1]{1,2,0:T(1,128)} %param.9) | copy-start | bytes 2308
  7.2 14.9 %collective-permute-start.3 = (bf16[24,16,512]{2,1,0:T(8,128)(2,1)S(1)}, bf16[24,16,512]{2,1,0:T(8,128)(2,1)S(1)}, u32[]{:S(2)}, u32[]{:S(2)}) collective-permute-start(bf16[24,16,512]{2,1,0:T(8,128)(2,1)S(1)} %get-tuple-element.38), channel_id=1, source_target_pairs={{32,0},{64,32},{96,64},{0,96},{33,1},{65,33},{97,65},{1,97},{34,2}... | collective-permute-start | bytes 1179656 | tf_op jit(solution)/shard_map/ppermute | solution.py:477
  8.6 13.5 %collective-permute-start.4 = (bf16[24,16,512]{2,1,0:T(8,128)(2,1)S(1)}, bf16[24,16,512]{2,1,0:T(8,128)(2,1)S(1)}, u32[]{:S(2)}, u32[]{:S(2)}) collective-permute-start(bf16[24,16,512]{2,1,0:T(8,128)(2,1)S(1)} %get-tuple-element.39), channel_id=1, source_target_pairs={{0,32},{32,64},{64,96},{96,0},{1,33},{33,65},{65,97},{97,1},{2,34}... | collective-permute-start | bytes 1179656 | tf_op jit(solution)/shard_map/ppermute | solution.py:476
  13.9 16.6 %collective-permute-start.2 = (bf16[24,16,512]{2,1,0:T(8,128)(2,1)S(1)}, bf16[24,16,512]{2,1,0:T(8,128)(2,1)S(1)}, u32[]{:S(2)}, u32[]{:S(2)}) collective-permute-start(bf16[24,16,512]{2,1,0:T(8,128)(2,1)S(1)} %add_up.1), channel_id=1, source_target_pairs={{0,32},{32,64},{64,96},{96,0},{1,33},{33,65},{65,97},{97,1},{2,34}... | collective-permute-start | bytes 1179656 | tf_op jit(solution)/shard_map/ppermute | solution.py:476
  15.1 15.5 %collective-permute-start.5 = (bf16[24,16,512]{2,1,0:T(8,128)(2,1)S(1)}, bf16[24,16,512]{2,1,0:T(8,128)(2,1)S(1)}, u32[]{:S(2)}, u32[]{:S(2)}) collective-permute-start(bf16[24,16,512]{2,1,0:T(8,128)(2,1)S(1)} %add_down.1), channel_id=1, source_target_pairs={{32,0},{64,32},{96,64},{0,96},{33,1},{65,33},{97,65},{1,97},{34,2}... | collective-permute-start | bytes 1179656 | tf_op jit(solution)/shard_map/ppermute | solution.py:477
  70.9 26.3 %all-to-all-start.1 = ((bf16[32,3,16,512]{3,2,1,0:T(8,128)(2,1)}), bf16[32,3,16,512]{3,2,1,0:T(8,128)(2,1)S(1)}, u32[]{:S(2)}, u32[]{:S(2)}) async-start(bf16[32,3,16,512]{3,2,1,0:T(8,128)(2,1)} %get-tuple-element.46), calls=%async_computation.1 | async-start | bytes 3145728 | tf_op jit(solution)/shard_map/all_to_all | solution.py:466

commit v5 on v4

--- a/solution.py
+++ b/solution.py
@@ -177,37 +177,24 @@
 def turn_kernel(
     table_ref,
     mom_ref,
+    var_ref,
     left_ref,
     right_ref,
     place_out,
     load_out,
-    left_first,
-    right_first,
-    turned_first,
-    left_second,
-    turned_out,
-    mom,
+    turned,
+    var,
     left,
     right,
-    turned,
+    mom,
     counts,
     into,
-    out_of,
 ):
     slots = mom.shape[0]
-    lefts = [left_first, left_second] + [left.at[s] for s in range(slots - 2)]
-    rights = [right_first] + [right.at[s] for s in range(slots - 1)]
+    pairs = ((mom_ref, mom), (left_ref, left), (right_ref, right), (var_ref, var))
     reads = [
-        [
-            pltpu.make_async_copy(mom_ref.at[s], mom.at[s], into.at[s, 0]),
-            pltpu.make_async_copy(left_ref.at[s], lefts[s], into.at[s, 1]),
-            pltpu.make_async_copy(right_ref.at[s], rights[s], into.at[s, 2]),
-        ]
+        [pltpu.make_async_copy(a.at[s], b.at[s], into.at[s, k]) for k, (a, b) in enumerate(pairs)]
         for s in range(slots)
-    ]
-    writes = [
-        pltpu.make_async_copy(turned.at[s], turned_out.at[s], out_of.at[s])
-        for s in range(slots - 1)
     ]
     for row in reads:
         for read in row:
@@ -235,42 +222,30 @@
         for read in reads[s]:
             read.wait()
         half = (beta_moment * mom[s]).astype(BF16)
-        product = dot_nn(dot_tn(lefts[s][...], half).astype(BF16), rights[s][...]).astype(BF16)
-        if s:
-            turned[s - 1] = product
-            writes[s - 1].start()
-        else:
-            turned_first[...] = product
-    for write in writes:
-        write.wait()
-
-
-def turn_moment(table, owner_count, momentum, left_basis, right_basis):
+        turned[s] = dot_nn(dot_tn(left[s], half).astype(BF16), right[s])
+
+
+def turn_moment(table, owner_count, momentum, variance, left_basis, right_basis):
     slots, size, _ = momentum.shape
-    square = (size, size)
+    shape = momentum.shape
     return call(
         turn_kernel,
         "turn_moment",
         (),
         [(table, pltpu.SMEM)]
-        + [(array, pltpu.HBM) for array in (momentum, left_basis, right_basis)],
+        + [(array, pltpu.HBM) for array in (momentum, variance, left_basis, right_basis)],
         [
             ((table.shape[1],), jnp.int32, pltpu.SMEM),
             ((1,), jnp.int32, pltpu.SMEM),
-            (square, BF16, pltpu.VMEM),
-            (square, BF16, pltpu.VMEM),
-            (square, BF16, pltpu.VMEM),
-            (square, BF16, pltpu.VMEM),
-            ((slots - 1, size, size), BF16, pltpu.HBM),
+            (shape, F32, pltpu.VMEM),
+            (shape, F32, pltpu.VMEM),
+            (shape, BF16, pltpu.VMEM),
+            (shape, BF16, pltpu.VMEM),
         ],
         [
-            pltpu.VMEM(momentum.shape, F32),
-            pltpu.VMEM((slots - 2, size, size), BF16),
-            pltpu.VMEM((slots - 1, size, size), BF16),
-            pltpu.VMEM((slots - 1, size, size), BF16),
+            pltpu.VMEM(shape, F32),
             pltpu.SMEM((owner_count,), jnp.int32),
-            DMA((slots, 3)),
-            DMA((slots - 1,)),
+            DMA((slots, 4)),
         ],
         4 * slots * size**3,
         12 * slots * size**2,
@@ -278,46 +253,9 @@
 
 
 def step_kernel(
-    load_ref,
-    grad_ref,
-    turned_ref,
-    var_ref,
-    left_ref,
-    right_ref,
-    left_first,
-    right_first,
-    turned_first,
-    left_second,
-    var_out,
-    upd_out,
-    grad,
-    turned,
-    var,
-    left,
-    right,
-    kept,
-    upd,
-    into,
-    out_of,
+    load_ref, grad, turned, var, left, right, var_out, upd_out, kept, upd, out_of
 ):
     slots, size, _ = kept.shape
-    lefts = [left_first, left_second] + [left.at[s] for s in range(slots - 2)]
-    rights = [right_first] + [right.at[s] for s in range(slots - 1)]
-    turns = [turned_first] + [turned.at[s] for s in range(slots - 1)]
-    reads = []
-    for s in range(slots):
-        pairs = [(grad_ref.at[:, s], grad.at[s])]
-        if s >= 2:
-            pairs.append((left_ref.at[s], lefts[s]))
-        if s >= 1:
-            pairs.append((right_ref.at[s], rights[s]))
-        early = len(pairs)
-        pairs.append((var_ref.at[s], var.at[s]))
-        if s >= 1:
-            pairs.append((turned_ref.at[s - 1], turns[s]))
-        row = [pltpu.make_async_copy(a, b, into.at[s, k]) for k, (a, b) in enumerate(pairs)]
-        reads += [row[:early], row[early:]]
-    reads.append([])
     writes = [
         [
             pltpu.make_async_copy(upd.at[s], upd_out.at[:, s], out_of.at[s, 0]),
@@ -326,61 +264,42 @@
         for s in range(slots)
     ]
 
-    def wait(row):
-        for read in row:
-            read.wait()
-
     def rotate(s):
-        block = grad[s].reshape(size, size)
-        return dot_nn(dot_tn(lefts[s][...], block).astype(BF16), rights[s][...])
+        block = grad[:, s].reshape(size, size)
+        return dot_nn(dot_tn(left[s], block).astype(BF16), right[s])
 
     def finish(s, rotated):
         second = beta_second * var[s] + (1.0 - beta_second) * rotated * rotated
         kept[s] = jnp.where(s < load_ref[0], second, var[s])
         writes[s][1].start()
-        rotated_moment = turns[s][...].astype(F32) + (1.0 - beta_moment) * rotated
+        rotated_moment = turned[s] + (1.0 - beta_moment) * rotated
         direction = (rotated_moment / (jnp.sqrt(second) + epsilon)).astype(BF16)
-        back_half = dot_nn(lefts[s][...], direction).astype(BF16)
-        update = dot_nt(back_half, rights[s][...]).astype(BF16)
-        upd[s] = update.reshape(grad.shape[1:])
+        back_half = dot_nn(left[s], direction).astype(BF16)
+        update = dot_nt(back_half, right[s]).astype(BF16)
+        upd[s] = update.reshape(upd.shape[1:])
         writes[s][0].start()
 
-    for row in reads:
-        for read in row:
-            read.start()
-    wait(reads[0])
     rotated = rotate(0)
     for s in range(slots):
-        wait(reads[2 * s + 1])
-        wait(reads[2 * s + 2])
         ahead = rotate(s + 1) if s + 1 < slots else None
         finish(s, rotated)
         rotated = ahead
     for row in writes:
-        wait(row)
-
-
-def owner_step(load, grad, turned, variance, left_basis, right_basis, *first):
+        for write in row:
+            write.wait()
+
+
+def owner_step(load, grad, turned, variance, left_basis, right_basis):
     slots, size, _ = variance.shape
     owners, _, rows, _ = grad.shape
+    slabs = pltpu.VMEM((slots, owners, rows, size), BF16)
     return call(
         step_kernel,
         "owner_step",
         (load,),
-        [(array, pltpu.HBM) for array in (grad, turned, variance, left_basis, right_basis)]
-        + [(array, pltpu.VMEM) for array in first],
+        [(array, pltpu.VMEM) for array in (grad, turned, variance, left_basis, right_basis)],
         [(variance.shape, F32, pltpu.HBM), (grad.shape, BF16, pltpu.HBM)],
-        [
-            pltpu.VMEM((slots, owners, rows, size), BF16),
-            pltpu.VMEM((slots - 1, size, size), BF16),
-            pltpu.VMEM(variance.shape, F32),
-            pltpu.VMEM((slots - 2, size, size), BF16),
-            pltpu.VMEM((slots - 1, size, size), BF16),
-            pltpu.VMEM(variance.shape, F32),
-            pltpu.VMEM((slots, owners, rows, size), BF16),
-            DMA((slots, 5)),
-            DMA((slots, 2)),
-        ],
+        [pltpu.VMEM(variance.shape, F32), slabs, DMA((slots, 2))],
         8 * slots * size**3,
         8 * slots * size**2,
     )
@@ -447,7 +366,8 @@
         state_kernel,
         "rest_of_state",
         (load,),
-        [(array, pltpu.HBM) for array in (grad, momentum, left_factor, right_factor)],
+        [(grad, pl.ANY)]
+        + [(array, pltpu.HBM) for array in (momentum, left_factor, right_factor)],
         [(shape, F32, pltpu.HBM), (shape, BF16, pltpu.HBM), (shape, BF16, pltpu.HBM)],
         [
             pltpu.VMEM((slots, owners, rows, size), BF16),
@@ -487,17 +407,15 @@
     table = owner_table[:, :, 0]
     ahead, behind, table = lax.optimization_barrier((ahead, behind, table))
     ahead, behind = up(ahead), down(behind)
-    place, load, *first, turned = turn_moment(
-        table, owner_count, momentum, left_basis, right_basis
+    place, load, *prepared = turn_moment(
+        table, owner_count, momentum, variance, left_basis, right_basis
     )
 
     outgoing = sum_and_place(
         (own_a, own_b), (ahead, near_down), (near_up, behind), place, owner_count * capacity
     ).reshape(owner_count, capacity, rows, width)
     grad = exchange(outgoing)
-    new_variance, update = owner_step(
-        load, grad, turned, variance, left_basis, right_basis, *first
-    )
+    new_variance, update = owner_step(load, grad, *prepared)
     returned = exchange(update)
     new_momentum, new_left, new_right = rest_of_state(
         load, grad, momentum, left_factor, right_factor

time: 98.3 us -> 96 us (0.977)
  Pallas kernels: 22.4 us -> 19.9 us
    pallas_call x9, Pallas kernels: 22.4 us -> 19.9 us  [call(): pl.pallas_call(kernel, out_shape=[jax.ShapeDtypeStruct(shape, dtype) if w...]
where the time goes in v5:
time: 96 us; the launch traced here: 95.7 us
  blocking collectives  32.6 us (34%)
  waiting for transfers between devices  30.9 us (32%)
  Pallas kernels  19.9 us (21%)
  starting transfers between devices  11.5 us (12%)
    all_to_all x1, blocking collectives, exchange(): lax.all_to_all(slabs, 'shard', split_axis=0, concat_axis=0, tiled=True)  32.6 us
    pallas_call x9, Pallas kernels, call(): pl.pallas_call(kernel, out_shape=[jax.ShapeDtypeStruct(shape, dtype) if w...  19.9 us
    all_to_all x1, waiting for transfers between devices, exchange(): lax.all_to_all(slabs, 'shard', split_axis=0, concat_axis=0, tiled=True)  17.2 us
    ppermute x3, waiting for transfers between devices, body(): lax.ppermute(x, 'dp', [(i, (i + 1) % REPLICAS) for i in range(REPLICAS)])  13.4 us
    ppermute x3, starting transfers between devices, body(): lax.ppermute(x, 'dp', [((i + 1) % REPLICAS, i) for i in range(REPLICAS)])  4.4 us
    all_to_all x1, starting transfers between devices, exchange(): lax.all_to_all(slabs, 'shard', split_axis=0, concat_axis=0, tiled=True)  3.77 us
    ppermute x3, starting transfers between devices, body(): lax.ppermute(x, 'dp', [(i, (i + 1) % REPLICAS) for i in range(REPLICAS)])  3.34 us
  transfers between devices with their start and end apart: 7, of which 4 were waited for; matrix products, arithmetic and copies ran while one was open for 0% of the time, Pallas kernels for 13%

profile of v5, /device:TPU:1, one launch (start us, length us, event | category | flops | bytes accessed | tf_op | source)
XLA Modules:
  0.0 95.7 jit_solution(17701680711605760596)
XLA Ops:
  0.6 1.3 %copy_relayed.1 = (bf16[24,16,512]{2,1,0:T(8,128)(2,1)S(1)}, bf16[24,16,512]{2,1,0:T(8,128)(2,1)S(1)}) custom-call(bf16[192,16,512]{2,1,0:T(8,128)(2,1)} %bitcast.7), custom_call_target="tpu_custom_call" | custom-call | bytes 786432 | tf_op jit(solution)/shard_map/copy_relayed/pallas_call | solution.py:47
  1.9 2.1 %collective-permute-start = (bf16[24,16,512]{2,1,0:T(8,128)(2,1)S(1)}, bf16[24,16,512]{2,1,0:T(8,128)(2,1)S(1)}, u32[]{:S(2)}, u32[]{:S(2)}) collective-permute-start(bf16[24,16,512]{2,1,0:T(8,128)(2,1)S(1)} %get-tuple-element.28), channel_id=1, source_target_pairs={{0,32},{32,64},{64,96},{96,0},{1,33},{33,65},{65,97},{97,1},{2,34}... | collective-permute-start | bytes 1179656 | tf_op jit(solution)/shard_map/ppermute | solution.py:396
  4.0 1.3 %collective-permute-start.1 = (bf16[24,16,512]{2,1,0:T(8,128)(2,1)S(1)}, bf16[24,16,512]{2,1,0:T(8,128)(2,1)S(1)}, u32[]{:S(2)}, u32[]{:S(2)}) collective-permute-start(bf16[24,16,512]{2,1,0:T(8,128)(2,1)S(1)} %get-tuple-element.30), channel_id=1, source_target_pairs={{32,0},{64,32},{96,64},{0,96},{33,1},{65,33},{97,65},{1,97},{34,2}... | collective-permute-start | bytes 1179656 | tf_op jit(solution)/shard_map/ppermute | solution.py:397
  5.4 1.8 %copy_rest.1 = (bf16[24,16,512]{2,1,0:T(8,128)(2,1)S(1)}, bf16[24,16,512]{2,1,0:T(8,128)(2,1)S(1)}, bf16[24,16,512]{2,1,0:T(8,128)(2,1)S(1)}, bf16[24,16,512]{2,...) custom-call(bf16[192,16,512]{2,1,0:T(8,128)(2,1)} %bitcast.8), custom_call_target="tpu_custom_call" | custom-call | bytes 2359296 | tf_op jit(solution)/shard_map/copy_rest/pallas_call | solution.py:47
  7.2 0.0 copy-start
  7.2 1.5 %collective-permute-start.3 = (bf16[24,16,512]{2,1,0:T(8,128)(2,1)S(1)}, bf16[24,16,512]{2,1,0:T(8,128)(2,1)S(1)}, u32[]{:S(2)}, u32[]{:S(2)}) collective-permute-start(bf16[24,16,512]{2,1,0:T(8,128)(2,1)S(1)} %get-tuple-element.37), channel_id=1, source_target_pairs={{32,0},{64,32},{96,64},{0,96},{33,1},{65,33},{97,65},{1,97},{34,2}... | collective-permute-start | bytes 1179656 | tf_op jit(solution)/shard_map/ppermute | solution.py:397
  8.6 0.1 collective-permute-start.4
  8.7 5.0 %collective-permute-done.got_ref = bf16[24,16,512]{2,1,0:T(8,128)(2,1)S(1)} collective-permute-done((bf16[24,16,512]{2,1,0:T(8,128)(2,1)S(1)}, bf16[24,16,512]{2,1,0:T(8,128)(2,1)S(1)}, u32[]{:S(2)}, u32[]{:S(2)}) %collective-permute-start) | collective-permute-done | bytes 393248 | tf_op jit(solution)/shard_map/ppermute | solution.py:396
  13.7 0.1 add_up.1
  13.8 0.0 collective-permute-done.1.got_ref
  13.8 0.1 add_down.1
  13.9 1.1 %collective-permute-start.2 = (bf16[24,16,512]{2,1,0:T(8,128)(2,1)S(1)}, bf16[24,16,512]{2,1,0:T(8,128)(2,1)S(1)}, u32[]{:S(2)}, u32[]{:S(2)}) collective-permute-start(bf16[24,16,512]{2,1,0:T(8,128)(2,1)S(1)} %add_up.1), channel_id=1, source_target_pairs={{0,32},{32,64},{64,96},{96,0},{1,33},{33,65},{65,97},{97,1},{2,34}... | collective-permute-start | bytes 1179656 | tf_op jit(solution)/shard_map/ppermute | solution.py:396
  15.1 1.6 %collective-permute-start.5 = (bf16[24,16,512]{2,1,0:T(8,128)(2,1)S(1)}, bf16[24,16,512]{2,1,0:T(8,128)(2,1)S(1)}, u32[]{:S(2)}, u32[]{:S(2)}) collective-permute-start(bf16[24,16,512]{2,1,0:T(8,128)(2,1)S(1)} %add_down.1), channel_id=1, source_target_pairs={{32,0},{64,32},{96,64},{0,96},{33,1},{65,33},{97,65},{1,97},{34,2}... | collective-permute-start | bytes 1179656 | tf_op jit(solution)/shard_map/ppermute | solution.py:397
  16.7 0.0 copy-done
  16.7 5.1 %turn_moment.1 = (s32[48]{0:T(128)S(4)}, s32[1]{0:T(128)S(4)}, f32[3,512,512]{2,1,0:T(8,128)S(1)}, f32[3,512,512]{2,1,0:T(8,128)S(1)}, bf16[3,512,512]{2,1,0:T(8...) custom-call(s32[4,48]{1,0:T(4,128)S(1)} %bitcast.6, f32[3,512,512]{2,1,0:T(8,128)} %mom_ref.3, f32[3,512,512]{2,1,0:T(8,128)} %var_ref.1, ...), custom_call_target="tpu_custom_call" | custom-call | flops 1610612736 | bytes 9437184 | tf_op jit(solution)/shard_map/turn_moment/pallas_call | solution.py:47
  21.8 0.3 collective-permute-done.3.a2
  22.1 0.0 collective-permute-done.4.b1
  22.1 8.4 %collective-permute-done.2.a1 = bf16[24,16,512]{2,1,0:T(8,128)(2,1)S(1)} collective-permute-done((bf16[24,16,512]{2,1,0:T(8,128)(2,1)S(1)}, bf16[24,16,512]{2,1,0:T(8,128)(2,1)S(1)}, u32[]{:S(2)}, u32[]{:S(2)}) %collective-permute-start.2) | collective-permute-done | bytes 393248 | tf_op jit(solution)/shard_map/ppermute | solution.py:396
  30.5 0.0 collective-permute-done.5.b2
  30.5 0.3 sum_and_place.1
  30.9 32.6 %all_to_all.10.grad.grad_ref = bf16[32,3,16,512]{3,2,1,0:T(8,128)(2,1)S(1)} all-to-all(bf16[32,3,16,512]{3,2,1,0:T(8,128)(2,1)S(1)} %bitcast.5), channel_id=1, replica_groups=mesh['dp'=4,'shard'=32] {'shard'}, dimensions={0} | all-to-all | bytes 3145728 | tf_op jit(solution)/shard_map/all_to_all | solution.py:386
  63.5 5.0 %owner_step.1 = (f32[3,512,512]{2,1,0:T(8,128)}, bf16[32,3,16,512]{3,2,1,0:T(8,128)(2,1)}) custom-call(s32[1]{0:T(128)S(4)} %get-tuple-element.33.load_ref, bf16[32,3,16,512]{3,2,1,0:T(8,128)(2,1)S(1)} %all_to_all.10.grad.grad_ref, f32[3,512,512]{2,1,0:T(8,128)S(1)} %get-tuple-element.40.turned, f32[3,512,512]{2,1,0:T(8,128)S(1)} %get-tuple-element.41.var, ...), custom_call_target="tpu_custom_call" | custom-call | flops 3221225472 | bytes 6291456 | tf_op jit(solution)/shard_map/owner_step/pallas_call | solution.py:47
  68.5 3.8 %all-to-all-start.1 = ((bf16[32,3,16,512]{3,2,1,0:T(8,128)(2,1)}), bf16[32,3,16,512]{3,2,1,0:T(8,128)(2,1)S(1)}, u32[]{:S(2)}, u32[]{:S(2)}) async-start(bf16[32,3,16,512]{3,2,1,0:T(8,128)(2,1)} %get-tuple-element.44), calls=%async_computation.1 | async-start | bytes 3145728 | tf_op jit(solution)/shard_map/all_to_all | solution.py:386
  72.3 5.3 %rest_of_state.1 = (f32[3,512,512]{2,1,0:T(8,128)}, bf16[3,512,512]{2,1,0:T(8,128)(2,1)}, bf16[3,512,512]{2,1,0:T(8,128)(2,1)}) custom-call(s32[1]{0:T(128)S(4)} %get-tuple-element.33.load_ref, bf16[32,3,16,512]{3,2,1,0:T(8,128)(2,1)S(1)} %all_to_all.10.grad.grad_ref, f32[3,512,512]{2,1,0:T(8,128)} %mom_ref.3, bf16[3,512,512]{2,1,0:T(8,128)(2,1)} %left_ref.3, ...), custom_call_target="tpu_custom_call" | custom-call | flops 1610612736 | bytes 14155776 | tf_op jit(solution)/shard_map/rest_of_state/pallas_call | solution.py:47
  77.6 17.2 %all-to-all-done.1 = bf16[32,3,16,512]{3,2,1,0:T(8,128)(2,1)S(1)} async-done(((bf16[32,3,16,512]{3,2,1,0:T(8,128)(2,1)}), bf16[32,3,16,512]{3,2,1,0:T(8,128)(2,1)S(1)}, u32[]{:S(2)}, u32[]{:S(2)}) %all-to-all-start.1) | async-done | bytes 1572896 | tf_op jit(solution)/shard_map/all_to_all | solution.py:386
  94.8 0.9 take_blocks.1
Async XLA Ops:
  1.9 11.8 %collective-permute-start = (bf16[24,16,512]{2,1,0:T(8,128)(2,1)S(1)}, bf16[24,16,512]{2,1,0:T(8,128)(2,1)S(1)}, u32[]{:S(2)}, u32[]{:S(2)}) collective-permute-start(bf16[24,16,512]{2,1,0:T(8,128)(2,1)S(1)} %get-tuple-element.28), channel_id=1, source_target_pairs={{0,32},{32,64},{64,96},{96,0},{1,33},{33,65},{65,97},{97,1},{2,34}... | collective-permute-start | bytes 1179656 | tf_op jit(solution)/shard_map/ppermute | solution.py:396
  4.0 9.8 %collective-permute-start.1 = (bf16[24,16,512]{2,1,0:T(8,128)(2,1)S(1)}, bf16[24,16,512]{2,1,0:T(8,128)(2,1)S(1)}, u32[]{:S(2)}, u32[]{:S(2)}) collective-permute-start(bf16[24,16,512]{2,1,0:T(8,128)(2,1)S(1)} %get-tuple-element.30), channel_id=1, source_target_pairs={{32,0},{64,32},{96,64},{0,96},{33,1},{65,33},{97,65},{1,97},{34,2}... | collective-permute-start | bytes 1179656 | tf_op jit(solution)/shard_map/ppermute | solution.py:397
  7.2 9.5 %copy-start = (s32[4,48,1]{1,2,0:T(1,128)S(1)}, s32[4,48,1]{1,2,0:T(1,128)}, u32[]{:S(2)}) copy-start(s32[4,48,1]{1,2,0:T(1,128)} %param.9) | copy-start | bytes 2308
  7.2 14.9 %collective-permute-start.3 = (bf16[24,16,512]{2,1,0:T(8,128)(2,1)S(1)}, bf16[24,16,512]{2,1,0:T(8,128)(2,1)S(1)}, u32[]{:S(2)}, u32[]{:S(2)}) collective-permute-start(bf16[24,16,512]{2,1,0:T(8,128)(2,1)S(1)} %get-tuple-element.37), channel_id=1, source_target_pairs={{32,0},{64,32},{96,64},{0,96},{33,1},{65,33},{97,65},{1,97},{34,2}... | collective-permute-start | bytes 1179656 | tf_op jit(solution)/shard_map/ppermute | solution.py:397
  8.6 13.5 %collective-permute-start.4 = (bf16[24,16,512]{2,1,0:T(8,128)(2,1)S(1)}, bf16[24,16,512]{2,1,0:T(8,128)(2,1)S(1)}, u32[]{:S(2)}, u32[]{:S(2)}) collective-permute-start(bf16[24,16,512]{2,1,0:T(8,128)(2,1)S(1)} %get-tuple-element.38), channel_id=1, source_target_pairs={{0,32},{32,64},{64,96},{96,0},{1,33},{33,65},{65,97},{97,1},{2,34}... | collective-permute-start | bytes 1179656 | tf_op jit(solution)/shard_map/ppermute | solution.py:396
  13.9 16.6 %collective-permute-start.2 = (bf16[24,16,512]{2,1,0:T(8,128)(2,1)S(1)}, bf16[24,16,512]{2,1,0:T(8,128)(2,1)S(1)}, u32[]{:S(2)}, u32[]{:S(2)}) collective-permute-start(bf16[24,16,512]{2,1,0:T(8,128)(2,1)S(1)} %add_up.1), channel_id=1, source_target_pairs={{0,32},{32,64},{64,96},{96,0},{1,33},{33,65},{65,97},{97,1},{2,34}... | collective-permute-start | bytes 1179656 | tf_op jit(solution)/shard_map/ppermute | solution.py:396
  15.1 15.5 %collective-permute-start.5 = (bf16[24,16,512]{2,1,0:T(8,128)(2,1)S(1)}, bf16[24,16,512]{2,1,0:T(8,128)(2,1)S(1)}, u32[]{:S(2)}, u32[]{:S(2)}) collective-permute-start(bf16[24,16,512]{2,1,0:T(8,128)(2,1)S(1)} %add_down.1), channel_id=1, source_target_pairs={{32,0},{64,32},{96,64},{0,96},{33,1},{65,33},{97,65},{1,97},{34,2}... | collective-permute-start | bytes 1179656 | tf_op jit(solution)/shard_map/ppermute | solution.py:397
  68.5 26.3 %all-to-all-start.1 = ((bf16[32,3,16,512]{3,2,1,0:T(8,128)(2,1)}), bf16[32,3,16,512]{3,2,1,0:T(8,128)(2,1)S(1)}, u32[]{:S(2)}, u32[]{:S(2)}) async-start(bf16[32,3,16,512]{3,2,1,0:T(8,128)(2,1)} %get-tuple-element.44), calls=%async_computation.1 | async-start | bytes 3145728 | tf_op jit(solution)/shard_map/all_to_all | solution.py:386

commit v6 on v5

--- a/solution.py
+++ b/solution.py
@@ -253,15 +253,11 @@
 
 
 def step_kernel(
-    load_ref, grad, turned, var, left, right, var_out, upd_out, kept, upd, out_of
+    grad, turned, var, left, right, upd_out, upd, out_of
 ):
-    slots, size, _ = kept.shape
+    slots, size, _ = var.shape
     writes = [
-        [
-            pltpu.make_async_copy(upd.at[s], upd_out.at[:, s], out_of.at[s, 0]),
-            pltpu.make_async_copy(kept.at[s], var_out.at[s], out_of.at[s, 1]),
-        ]
-        for s in range(slots)
+        pltpu.make_async_copy(upd.at[s], upd_out.at[:, s], out_of.at[s]) for s in range(slots)
     ]
 
     def rotate(s):
@@ -270,39 +266,36 @@
 
     def finish(s, rotated):
         second = beta_second * var[s] + (1.0 - beta_second) * rotated * rotated
-        kept[s] = jnp.where(s < load_ref[0], second, var[s])
-        writes[s][1].start()
         rotated_moment = turned[s] + (1.0 - beta_moment) * rotated
         direction = (rotated_moment / (jnp.sqrt(second) + epsilon)).astype(BF16)
         back_half = dot_nn(left[s], direction).astype(BF16)
         update = dot_nt(back_half, right[s]).astype(BF16)
         upd[s] = update.reshape(upd.shape[1:])
-        writes[s][0].start()
+        writes[s].start()
 
     rotated = rotate(0)
     for s in range(slots):
         ahead = rotate(s + 1) if s + 1 < slots else None
         finish(s, rotated)
         rotated = ahead
-    for row in writes:
-        for write in row:
-            write.wait()
-
-
-def owner_step(load, grad, turned, variance, left_basis, right_basis):
+    for write in writes:
+        write.wait()
+
+
+def owner_step(grad, turned, variance, left_basis, right_basis):
     slots, size, _ = variance.shape
     owners, _, rows, _ = grad.shape
     slabs = pltpu.VMEM((slots, owners, rows, size), BF16)
     return call(
         step_kernel,
         "owner_step",
-        (load,),
+        (),
         [(array, pltpu.VMEM) for array in (grad, turned, variance, left_basis, right_basis)],
-        [(variance.shape, F32, pltpu.HBM), (grad.shape, BF16, pltpu.HBM)],
-        [pltpu.VMEM(variance.shape, F32), slabs, DMA((slots, 2))],
+        [(grad.shape, BF16, pltpu.HBM)],
+        [slabs, DMA((slots,))],
         8 * slots * size**3,
         8 * slots * size**2,
-    )
+    )[0]
 
 
 def state_kernel(
@@ -311,24 +304,38 @@
     mom_ref,
     left_ref,
     right_ref,
+    var_ref,
+    left_basis_ref,
+    right_basis_ref,
     mom_out,
     left_out,
     right_out,
+    var_out,
     grad,
     mom,
     left,
     right,
+    var,
+    left_basis,
+    right_basis,
     into,
     out_of,
 ):
     slots, size, _ = mom.shape
-    pairs = ((mom_ref, mom), (left_ref, left), (right_ref, right))
+    pairs = (
+        (mom_ref, mom),
+        (left_ref, left),
+        (right_ref, right),
+        (var_ref, var),
+        (left_basis_ref, left_basis),
+        (right_basis_ref, right_basis),
+    )
     reads = [
-        [pltpu.make_async_copy(grad_ref.at[:, s], grad.at[s], into.at[s, 3])]
+        [pltpu.make_async_copy(grad_ref.at[:, s], grad.at[s], into.at[s, len(pairs)])]
         + [pltpu.make_async_copy(a.at[s], b.at[s], into.at[s, k]) for k, (a, b) in enumerate(pairs)]
         for s in range(slots)
     ]
-    pairs = ((mom, mom_out), (left, left_out), (right, right_out))
+    pairs = ((mom, mom_out), (left, left_out), (right, right_out), (var, var_out))
     writes = [
         [pltpu.make_async_copy(a.at[s], b.at[s], out_of.at[s, k]) for k, (a, b) in enumerate(pairs)]
         for s in range(slots)
@@ -350,6 +357,8 @@
             right[s] = (beta_factor * right[s].astype(F32) + (1.0 - beta_factor) * outer).astype(
                 BF16
             )
+            rotated = dot_nn(dot_tn(left_basis[s], block).astype(BF16), right_basis[s])
+            var[s] = beta_second * var[s] + (1.0 - beta_second) * rotated * rotated
 
         for write in writes[s]:
             write.start()
@@ -358,7 +367,8 @@
             write.wait()
 
 
-def rest_of_state(load, grad, momentum, left_factor, right_factor):
+def rest_of_state(load, grad, *state):
+    momentum = state[0]
     slots, size, _ = momentum.shape
     owners, _, rows, _ = grad.shape
     shape = momentum.shape
@@ -366,18 +376,20 @@
         state_kernel,
         "rest_of_state",
         (load,),
-        [(grad, pl.ANY)]
-        + [(array, pltpu.HBM) for array in (momentum, left_factor, right_factor)],
-        [(shape, F32, pltpu.HBM), (shape, BF16, pltpu.HBM), (shape, BF16, pltpu.HBM)],
+        [(grad, pl.ANY)] + [(array, pltpu.HBM) for array in state],
+        [(shape, dtype, pltpu.HBM) for dtype in (F32, BF16, BF16, F32)],
         [
             pltpu.VMEM((slots, owners, rows, size), BF16),
             pltpu.VMEM(shape, F32),
             pltpu.VMEM(shape, BF16),
             pltpu.VMEM(shape, BF16),
+            pltpu.VMEM(shape, F32),
+            pltpu.VMEM(shape, BF16),
+            pltpu.VMEM(shape, BF16),
+            DMA((slots, 7)),
             DMA((slots, 4)),
-            DMA((slots, 3)),
         ],
-        4 * slots * size**3,
+        8 * slots * size**3,
         18 * slots * size**2,
     )
 
@@ -415,10 +427,10 @@
         (own_a, own_b), (ahead, near_down), (near_up, behind), place, owner_count * capacity
     ).reshape(owner_count, capacity, rows, width)
     grad = exchange(outgoing)
-    new_variance, update = owner_step(load, grad, *prepared)
+    update = owner_step(grad, *prepared)
     returned = exchange(update)
-    new_momentum, new_left, new_right = rest_of_state(
-        load, grad, momentum, left_factor, right_factor
+    new_momentum, new_left, new_right, new_variance = rest_of_state(
+        load, grad, momentum, left_factor, right_factor, variance, left_basis, right_basis
     )
     update_rows = take_blocks(returned.reshape(owner_count * capacity, rows, width), place)
     return (update_rows, new_momentum, new_variance, new_left, new_right)

time: 96 us -> 95.9 us (level)
  waiting for transfers between devices: 30.9 us -> 28.4 us
  Pallas kernels: 19.9 us -> 22.3 us
    all_to_all x1, waiting for transfers between devices: 17.2 us -> 14.7 us  [exchange(): lax.all_to_all(slabs, 'shard', split_axis=0, concat_axis=0, tiled=True)]
    pallas_call x9, Pallas kernels: 19.9 us -> 22.3 us  [call(): pl.pallas_call(kernel, out_shape=[jax.ShapeDtypeStruct(shape, dtype) if w...]
  transfers between devices with their start and end apart: 7 -> 7, of which waited for: 4 -> 4; matrix products, arithmetic and copies ran while one was open for 0% -> 0% of each run, Pallas kernels for 13% -> 16%
where the time goes in v6:
time: 95.9 us; the launch traced here: 95.6 us
  blocking collectives  32.6 us (34%)
  waiting for transfers between devices  28.4 us (30%)
  Pallas kernels  22.3 us (23%)
  starting transfers between devices  11.5 us (12%)
    all_to_all x1, blocking collectives, exchange(): lax.all_to_all(slabs, 'shard', split_axis=0, concat_axis=0, tiled=True)  32.6 us
    pallas_call x9, Pallas kernels, call(): pl.pallas_call(kernel, out_shape=[jax.ShapeDtypeStruct(shape, dtype) if w...  22.3 us
    all_to_all x1, waiting for transfers between devices, exchange(): lax.all_to_all(slabs, 'shard', split_axis=0, concat_axis=0, tiled=True)  14.7 us
    ppermute x3, waiting for transfers between devices, body(): lax.ppermute(x, 'dp', [(i, (i + 1) % REPLICAS) for i in range(REPLICAS)])  13.4 us
    ppermute x3, starting transfers between devices, body(): lax.ppermute(x, 'dp', [((i + 1) % REPLICAS, i) for i in range(REPLICAS)])  4.4 us
    all_to_all x1, starting transfers between devices, exchange(): lax.all_to_all(slabs, 'shard', split_axis=0, concat_axis=0, tiled=True)  3.77 us
    ppermute x3, starting transfers between devices, body(): lax.ppermute(x, 'dp', [(i, (i + 1) % REPLICAS) for i in range(REPLICAS)])  3.34 us
  transfers between devices with their start and end apart: 7, of which 4 were waited for; matrix products, arithmetic and copies ran while one was open for 0% of the time, Pallas kernels for 16%

profile of v6, /device:TPU:1, one launch (start us, length us, event | category | flops | bytes accessed | tf_op | source)
XLA Modules:
  0.0 95.6 jit_solution(14429158622310838386)
XLA Ops:
  0.6 1.3 %copy_relayed.1 = (bf16[24,16,512]{2,1,0:T(8,128)(2,1)S(1)}, bf16[24,16,512]{2,1,0:T(8,128)(2,1)S(1)}) custom-call(bf16[192,16,512]{2,1,0:T(8,128)(2,1)} %bitcast.7), custom_call_target="tpu_custom_call" | custom-call | bytes 786432 | tf_op jit(solution)/shard_map/copy_relayed/pallas_call | solution.py:47
  1.9 2.1 %collective-permute-start = (bf16[24,16,512]{2,1,0:T(8,128)(2,1)S(1)}, bf16[24,16,512]{2,1,0:T(8,128)(2,1)S(1)}, u32[]{:S(2)}, u32[]{:S(2)}) collective-permute-start(bf16[24,16,512]{2,1,0:T(8,128)(2,1)S(1)} %get-tuple-element.27), channel_id=1, source_target_pairs={{0,32},{32,64},{64,96},{96,0},{1,33},{33,65},{65,97},{97,1},{2,34}... | collective-permute-start | bytes 1179656 | tf_op jit(solution)/shard_map/ppermute | solution.py:408
  4.0 1.3 %collective-permute-start.1 = (bf16[24,16,512]{2,1,0:T(8,128)(2,1)S(1)}, bf16[24,16,512]{2,1,0:T(8,128)(2,1)S(1)}, u32[]{:S(2)}, u32[]{:S(2)}) collective-permute-start(bf16[24,16,512]{2,1,0:T(8,128)(2,1)S(1)} %get-tuple-element.29), channel_id=1, source_target_pairs={{32,0},{64,32},{96,64},{0,96},{33,1},{65,33},{97,65},{1,97},{34,2}... | collective-permute-start | bytes 1179656 | tf_op jit(solution)/shard_map/ppermute | solution.py:409
  5.4 1.8 %copy_rest.1 = (bf16[24,16,512]{2,1,0:T(8,128)(2,1)S(1)}, bf16[24,16,512]{2,1,0:T(8,128)(2,1)S(1)}, bf16[24,16,512]{2,1,0:T(8,128)(2,1)S(1)}, bf16[24,16,512]{2,...) custom-call(bf16[192,16,512]{2,1,0:T(8,128)(2,1)} %bitcast.8), custom_call_target="tpu_custom_call" | custom-call | bytes 2359296 | tf_op jit(solution)/shard_map/copy_rest/pallas_call | solution.py:47
  7.2 0.0 copy-start
  7.2 1.5 %collective-permute-start.3 = (bf16[24,16,512]{2,1,0:T(8,128)(2,1)S(1)}, bf16[24,16,512]{2,1,0:T(8,128)(2,1)S(1)}, u32[]{:S(2)}, u32[]{:S(2)}) collective-permute-start(bf16[24,16,512]{2,1,0:T(8,128)(2,1)S(1)} %get-tuple-element.35), channel_id=1, source_target_pairs={{32,0},{64,32},{96,64},{0,96},{33,1},{65,33},{97,65},{1,97},{34,2}... | collective-permute-start | bytes 1179656 | tf_op jit(solution)/shard_map/ppermute | solution.py:409
  8.6 0.1 collective-permute-start.4
  8.7 5.0 %collective-permute-done.got_ref = bf16[24,16,512]{2,1,0:T(8,128)(2,1)S(1)} collective-permute-done((bf16[24,16,512]{2,1,0:T(8,128)(2,1)S(1)}, bf16[24,16,512]{2,1,0:T(8,128)(2,1)S(1)}, u32[]{:S(2)}, u32[]{:S(2)}) %collective-permute-start) | collective-permute-done | bytes 393248 | tf_op jit(solution)/shard_map/ppermute | solution.py:408
  13.7 0.1 add_up.1
  13.8 0.0 collective-permute-done.1.got_ref
  13.8 0.1 add_down.1
  13.9 1.1 %collective-permute-start.2 = (bf16[24,16,512]{2,1,0:T(8,128)(2,1)S(1)}, bf16[24,16,512]{2,1,0:T(8,128)(2,1)S(1)}, u32[]{:S(2)}, u32[]{:S(2)}) collective-permute-start(bf16[24,16,512]{2,1,0:T(8,128)(2,1)S(1)} %add_up.1), channel_id=1, source_target_pairs={{0,32},{32,64},{64,96},{96,0},{1,33},{33,65},{65,97},{97,1},{2,34}... | collective-permute-start | bytes 1179656 | tf_op jit(solution)/shard_map/ppermute | solution.py:408
  15.1 1.6 %collective-permute-start.5 = (bf16[24,16,512]{2,1,0:T(8,128)(2,1)S(1)}, bf16[24,16,512]{2,1,0:T(8,128)(2,1)S(1)}, u32[]{:S(2)}, u32[]{:S(2)}) collective-permute-start(bf16[24,16,512]{2,1,0:T(8,128)(2,1)S(1)} %add_down.1), channel_id=1, source_target_pairs={{32,0},{64,32},{96,64},{0,96},{33,1},{65,33},{97,65},{1,97},{34,2}... | collective-permute-start | bytes 1179656 | tf_op jit(solution)/shard_map/ppermute | solution.py:409
  16.7 0.0 copy-done
  16.7 5.1 %turn_moment.1 = (s32[48]{0:T(128)S(4)}, s32[1]{0:T(128)S(4)}, f32[3,512,512]{2,1,0:T(8,128)S(1)}, f32[3,512,512]{2,1,0:T(8,128)S(1)}, bf16[3,512,512]{2,1,0:T(8...) custom-call(s32[4,48]{1,0:T(4,128)S(1)} %bitcast.6, f32[3,512,512]{2,1,0:T(8,128)} %mom_ref.3, f32[3,512,512]{2,1,0:T(8,128)} %var_ref.3, ...), custom_call_target="tpu_custom_call" | custom-call | flops 1610612736 | bytes 9437184 | tf_op jit(solution)/shard_map/turn_moment/pallas_call | solution.py:47
  21.8 0.3 collective-permute-done.3.a2
  22.1 0.0 collective-permute-done.4.b1
  22.1 8.4 %collective-permute-done.2.a1 = bf16[24,16,512]{2,1,0:T(8,128)(2,1)S(1)} collective-permute-done((bf16[24,16,512]{2,1,0:T(8,128)(2,1)S(1)}, bf16[24,16,512]{2,1,0:T(8,128)(2,1)S(1)}, u32[]{:S(2)}, u32[]{:S(2)}) %collective-permute-start.2) | collective-permute-done | bytes 393248 | tf_op jit(solution)/shard_map/ppermute | solution.py:408
  30.5 0.0 collective-permute-done.5.b2
  30.5 0.3 sum_and_place.1
  30.9 32.6 %all_to_all.10.grad.grad_ref = bf16[32,3,16,512]{3,2,1,0:T(8,128)(2,1)S(1)} all-to-all(bf16[32,3,16,512]{3,2,1,0:T(8,128)(2,1)S(1)} %bitcast.5), channel_id=1, replica_groups=mesh['dp'=4,'shard'=32] {'shard'}, dimensions={0} | all-to-all | bytes 3145728 | tf_op jit(solution)/shard_map/all_to_all | solution.py:398
  63.5 4.8 %owner_step.1 = bf16[32,3,16,512]{3,2,1,0:T(8,128)(2,1)} custom-call(bf16[32,3,16,512]{3,2,1,0:T(8,128)(2,1)S(1)} %all_to_all.10.grad.grad_ref, f32[3,512,512]{2,1,0:T(8,128)S(1)} %get-tuple-element.38.turned, f32[3,512,512]{2,1,0:T(8,128)S(1)} %get-tuple-element.39.var, bf16[3,512,512]{2,1,0:T(8,128)(2,1)S(1)} %get-tuple-element.40.left, ...), custom_call_target="tpu_custom_call" | custom-call | flops 3221225472 | bytes 6291456 | tf_op jit(solution)/shard_map/owner_step/pallas_call | solution.py:47
  68.4 3.8 %all-to-all-start.1 = ((bf16[32,3,16,512]{3,2,1,0:T(8,128)(2,1)}), bf16[32,3,16,512]{3,2,1,0:T(8,128)(2,1)S(1)}, u32[]{:S(2)}, u32[]{:S(2)}) async-start(bf16[32,3,16,512]{3,2,1,0:T(8,128)(2,1)} %owner_step.1), calls=%async_computation.1 | async-start | bytes 3145728 | tf_op jit(solution)/shard_map/all_to_all | solution.py:398
  72.1 7.8 %rest_of_state.1 = (f32[3,512,512]{2,1,0:T(8,128)}, bf16[3,512,512]{2,1,0:T(8,128)(2,1)}, bf16[3,512,512]{2,1,0:T(8,128)(2,1)}, f32[3,512,512]{2,1,0:T(8,128)}) custom-call(s32[1]{0:T(128)S(4)} %get-tuple-element.42.load_ref, bf16[32,3,16,512]{3,2,1,0:T(8,128)(2,1)S(1)} %all_to_all.10.grad.grad_ref, f32[3,512,512]{2,1,0:T(8,128)} %mom_ref.3, ...), custom_call_target="tpu_custom_call" | custom-call | flops 3221225472 | bytes 14155776 | tf_op jit(solution)/shard_map/rest_of_state/pallas_call | solution.py:47
  80.0 14.7 %all-to-all-done.1 = bf16[32,3,16,512]{3,2,1,0:T(8,128)(2,1)S(1)} async-done(((bf16[32,3,16,512]{3,2,1,0:T(8,128)(2,1)}), bf16[32,3,16,512]{3,2,1,0:T(8,128)(2,1)S(1)}, u32[]{:S(2)}, u32[]{:S(2)}) %all-to-all-start.1) | async-done | bytes 1572896 | tf_op jit(solution)/shard_map/all_to_all | solution.py:398
  94.7 0.9 take_blocks.1
Async XLA Ops:
  1.9 11.8 %collective-permute-start = (bf16[24,16,512]{2,1,0:T(8,128)(2,1)S(1)}, bf16[24,16,512]{2,1,0:T(8,128)(2,1)S(1)}, u32[]{:S(2)}, u32[]{:S(2)}) collective-permute-start(bf16[24,16,512]{2,1,0:T(8,128)(2,1)S(1)} %get-tuple-element.27), channel_id=1, source_target_pairs={{0,32},{32,64},{64,96},{96,0},{1,33},{33,65},{65,97},{97,1},{2,34}... | collective-permute-start | bytes 1179656 | tf_op jit(solution)/shard_map/ppermute | solution.py:408
  4.0 9.8 %collective-permute-start.1 = (bf16[24,16,512]{2,1,0:T(8,128)(2,1)S(1)}, bf16[24,16,512]{2,1,0:T(8,128)(2,1)S(1)}, u32[]{:S(2)}, u32[]{:S(2)}) collective-permute-start(bf16[24,16,512]{2,1,0:T(8,128)(2,1)S(1)} %get-tuple-element.29), channel_id=1, source_target_pairs={{32,0},{64,32},{96,64},{0,96},{33,1},{65,33},{97,65},{1,97},{34,2}... | collective-permute-start | bytes 1179656 | tf_op jit(solution)/shard_map/ppermute | solution.py:409
  7.2 9.5 %copy-start = (s32[4,48,1]{1,2,0:T(1,128)S(1)}, s32[4,48,1]{1,2,0:T(1,128)}, u32[]{:S(2)}) copy-start(s32[4,48,1]{1,2,0:T(1,128)} %param.9) | copy-start | bytes 2308
  7.2 14.9 %collective-permute-start.3 = (bf16[24,16,512]{2,1,0:T(8,128)(2,1)S(1)}, bf16[24,16,512]{2,1,0:T(8,128)(2,1)S(1)}, u32[]{:S(2)}, u32[]{:S(2)}) collective-permute-start(bf16[24,16,512]{2,1,0:T(8,128)(2,1)S(1)} %get-tuple-element.35), channel_id=1, source_target_pairs={{32,0},{64,32},{96,64},{0,96},{33,1},{65,33},{97,65},{1,97},{34,2}... | collective-permute-start | bytes 1179656 | tf_op jit(solution)/shard_map/ppermute | solution.py:409
  8.6 13.5 %collective-permute-start.4 = (bf16[24,16,512]{2,1,0:T(8,128)(2,1)S(1)}, bf16[24,16,512]{2,1,0:T(8,128)(2,1)S(1)}, u32[]{:S(2)}, u32[]{:S(2)}) collective-permute-start(bf16[24,16,512]{2,1,0:T(8,128)(2,1)S(1)} %get-tuple-element.36), channel_id=1, source_target_pairs={{0,32},{32,64},{64,96},{96,0},{1,33},{33,65},{65,97},{97,1},{2,34}... | collective-permute-start | bytes 1179656 | tf_op jit(solution)/shard_map/ppermute | solution.py:408
  13.9 16.6 %collective-permute-start.2 = (bf16[24,16,512]{2,1,0:T(8,128)(2,1)S(1)}, bf16[24,16,512]{2,1,0:T(8,128)(2,1)S(1)}, u32[]{:S(2)}, u32[]{:S(2)}) collective-permute-start(bf16[24,16,512]{2,1,0:T(8,128)(2,1)S(1)} %add_up.1), channel_id=1, source_target_pairs={{0,32},{32,64},{64,96},{96,0},{1,33},{33,65},{65,97},{97,1},{2,34}... | collective-permute-start | bytes 1179656 | tf_op jit(solution)/shard_map/ppermute | solution.py:408
  15.1 15.5 %collective-permute-start.5 = (bf16[24,16,512]{2,1,0:T(8,128)(2,1)S(1)}, bf16[24,16,512]{2,1,0:T(8,128)(2,1)S(1)}, u32[]{:S(2)}, u32[]{:S(2)}) collective-permute-start(bf16[24,16,512]{2,1,0:T(8,128)(2,1)S(1)} %add_down.1), channel_id=1, source_target_pairs={{32,0},{64,32},{96,64},{0,96},{33,1},{65,33},{97,65},{1,97},{34,2}... | collective-permute-start | bytes 1179656 | tf_op jit(solution)/shard_map/ppermute | solution.py:409
  68.4 26.4 %all-to-all-start.1 = ((bf16[32,3,16,512]{3,2,1,0:T(8,128)(2,1)}), bf16[32,3,16,512]{3,2,1,0:T(8,128)(2,1)S(1)}, u32[]{:S(2)}, u32[]{:S(2)}) async-start(bf16[32,3,16,512]{3,2,1,0:T(8,128)(2,1)} %owner_step.1), calls=%async_computation.1 | async-start | bytes 3145728 | tf_op jit(solution)/shard_map/all_to_all | solution.py:398

commit v7 on v6

--- a/solution.py
+++ b/solution.py
@@ -267,7 +267,7 @@
     def finish(s, rotated):
         second = beta_second * var[s] + (1.0 - beta_second) * rotated * rotated
         rotated_moment = turned[s] + (1.0 - beta_moment) * rotated
-        direction = (rotated_moment / (jnp.sqrt(second) + epsilon)).astype(BF16)
+        direction = (rotated_moment / (second * lax.rsqrt(second) + epsilon)).astype(BF16)
         back_half = dot_nn(left[s], direction).astype(BF16)
         update = dot_nt(back_half, right[s]).astype(BF16)
         upd[s] = update.reshape(upd.shape[1:])
@@ -405,20 +405,21 @@
     capacity = momentum.shape[0]
     local = grads[0]
     _, rows, width = local.shape
-    up = lambda x: lax.ppermute(x, "dp", [(i, (i + 1) % REPLICAS) for i in range(REPLICAS)])
-    down = lambda x: lax.ppermute(x, "dp", [((i + 1) % REPLICAS, i) for i in range(REPLICAS)])
+    down = lambda x: lax.ppermute(x, "dp", [(i, (i + 1) % REPLICAS) for i in range(REPLICAS)])
+    up = lambda x: lax.ppermute(x, "dp", [((i + 1) % REPLICAS, i) for i in range(REPLICAS)])
 
     relay_up, relay_down = copy_halves(local, ((2, 0), (2, 1)), "copy_relayed")
     relay_up, relay_down = up(relay_up), down(relay_down)
     near_up, near_down, own_up, own_down, own_a, own_b = copy_halves(
-        local, ((1, 1), (3, 0), (1, 0), (3, 1), (0, 0), (0, 1)), "copy_rest"
+        local, ((3, 1), (1, 0), (3, 0), (1, 1), (0, 0), (0, 1)), "copy_rest"
     )
     near_up, near_down = up(near_up), down(near_down)
     ahead = add_relayed(own_up, relay_up, "add_up")
     behind = add_relayed(own_down, relay_down, "add_down")
     table = owner_table[:, :, 0]
-    ahead, behind, table = lax.optimization_barrier((ahead, behind, table))
-    ahead, behind = up(ahead), down(behind)
+    ahead = up(ahead)
+    behind, table = lax.optimization_barrier((behind, table))
+    behind = down(behind)
     place, load, *prepared = turn_moment(
         table, owner_count, momentum, variance, left_basis, right_basis
     )

time: 95.9 us -> 95.9 us (level)
  starting transfers between devices: 11.5 us -> 12.8 us
  waiting for transfers between devices: 28.4 us -> 27.2 us
    ppermute x3, starting transfers between devices: 4.4 us -> 6.34 us  [body(): lax.ppermute(x, 'dp', [((i + 1) % REPLICAS, i) for i in range(REPLICAS)])]
    ppermute x3, waiting for transfers between devices: 13.4 us -> 12.4 us  [body(): lax.ppermute(x, 'dp', [(i, (i + 1) % REPLICAS) for i in range(REPLICAS)])]
where the time goes in v7:
time: 95.9 us; the launch traced here: 95.6 us
  blocking collectives  32.6 us (34%)
  waiting for transfers between devices  27.2 us (28%)
  Pallas kernels  22.4 us (23%)
  starting transfers between devices  12.8 us (13%)
    all_to_all x1, blocking collectives, exchange(): lax.all_to_all(slabs, 'shard', split_axis=0, concat_axis=0, tiled=True)  32.6 us
    pallas_call x9, Pallas kernels, call(): pl.pallas_call(kernel, out_shape=[jax.ShapeDtypeStruct(shape, dtype) if w...  22.4 us
    all_to_all x1, waiting for transfers between devices, exchange(): lax.all_to_all(slabs, 'shard', split_axis=0, concat_axis=0, tiled=True)  14.7 us
    ppermute x3, waiting for transfers between devices, body(): lax.ppermute(x, 'dp', [(i, (i + 1) % REPLICAS) for i in range(REPLICAS)])  12.4 us
    ppermute x3, starting transfers between devices, body(): lax.ppermute(x, 'dp', [((i + 1) % REPLICAS, i) for i in range(REPLICAS)])  6.34 us
    all_to_all x1, starting transfers between devices, exchange(): lax.all_to_all(slabs, 'shard', split_axis=0, concat_axis=0, tiled=True)  3.77 us
    ppermute x3, starting transfers between devices, body(): lax.ppermute(x, 'dp', [(i, (i + 1) % REPLICAS) for i in range(REPLICAS)])  2.68 us
  transfers between devices with their start and end apart: 7, of which 4 were waited for; matrix products, arithmetic and copies ran while one was open for 0% of the time, Pallas kernels for 16%

profile of v7, /device:TPU:1, one launch (start us, length us, event | category | flops | bytes accessed | tf_op | source)
XLA Modules:
  0.0 95.6 jit_solution(16316100865212553580)
XLA Ops:
  0.6 1.3 %copy_relayed.1 = (bf16[24,16,512]{2,1,0:T(8,128)(2,1)S(1)}, bf16[24,16,512]{2,1,0:T(8,128)(2,1)S(1)}) custom-call(bf16[192,16,512]{2,1,0:T(8,128)(2,1)} %bitcast.7), custom_call_target="tpu_custom_call" | custom-call | bytes 786432 | tf_op jit(solution)/shard_map/copy_relayed/pallas_call | solution.py:47
  1.9 2.1 %collective-permute-start = (bf16[24,16,512]{2,1,0:T(8,128)(2,1)S(1)}, bf16[24,16,512]{2,1,0:T(8,128)(2,1)S(1)}, u32[]{:S(2)}, u32[]{:S(2)}) collective-permute-start(bf16[24,16,512]{2,1,0:T(8,128)(2,1)S(1)} %get-tuple-element.26), channel_id=1, source_target_pairs={{0,32},{32,64},{64,96},{96,0},{1,33},{33,65},{65,97},{97,1},{2,34}... | collective-permute-start | bytes 1179656 | tf_op jit(solution)/shard_map/ppermute | solution.py:408
  4.0 1.3 %collective-permute-start.1 = (bf16[24,16,512]{2,1,0:T(8,128)(2,1)S(1)}, bf16[24,16,512]{2,1,0:T(8,128)(2,1)S(1)}, u32[]{:S(2)}, u32[]{:S(2)}) collective-permute-start(bf16[24,16,512]{2,1,0:T(8,128)(2,1)S(1)} %get-tuple-element.32), channel_id=1, source_target_pairs={{32,0},{64,32},{96,64},{0,96},{33,1},{65,33},{97,65},{1,97},{34,2}... | collective-permute-start | bytes 1179656 | tf_op jit(solution)/shard_map/ppermute | solution.py:409
  5.4 1.8 %copy_rest.1 = (bf16[24,16,512]{2,1,0:T(8,128)(2,1)S(1)}, bf16[24,16,512]{2,1,0:T(8,128)(2,1)S(1)}, bf16[24,16,512]{2,1,0:T(8,128)(2,1)S(1)}, bf16[24,16,512]{2,...) custom-call(bf16[192,16,512]{2,1,0:T(8,128)(2,1)} %bitcast.8), custom_call_target="tpu_custom_call" | custom-call | bytes 2359296 | tf_op jit(solution)/shard_map/copy_rest/pallas_call | solution.py:47
  7.2 0.0 copy-start
  7.2 0.2 collective-permute-start.3
  7.4 2.6 %collective-permute-start.4 = (bf16[24,16,512]{2,1,0:T(8,128)(2,1)S(1)}, bf16[24,16,512]{2,1,0:T(8,128)(2,1)S(1)}, u32[]{:S(2)}, u32[]{:S(2)}) collective-permute-start(bf16[24,16,512]{2,1,0:T(8,128)(2,1)S(1)} %get-tuple-element.34), channel_id=1, source_target_pairs={{32,0},{64,32},{96,64},{0,96},{33,1},{65,33},{97,65},{1,97},{34,2}... | collective-permute-start | bytes 1179656 | tf_op jit(solution)/shard_map/ppermute | solution.py:409
  9.9 3.8 %collective-permute-done.got_ref = bf16[24,16,512]{2,1,0:T(8,128)(2,1)S(1)} collective-permute-done((bf16[24,16,512]{2,1,0:T(8,128)(2,1)S(1)}, bf16[24,16,512]{2,1,0:T(8,128)(2,1)S(1)}, u32[]{:S(2)}, u32[]{:S(2)}) %collective-permute-start) | collective-permute-done | bytes 393248 | tf_op jit(solution)/shard_map/ppermute | solution.py:408
  13.7 0.1 add_down.1
  13.8 0.4 collective-permute-start.5
  14.2 0.0 collective-permute-done.1.got_ref
  14.2 0.1 add_up.1
  14.3 2.4 %collective-permute-start.2 = (bf16[24,16,512]{2,1,0:T(8,128)(2,1)S(1)}, bf16[24,16,512]{2,1,0:T(8,128)(2,1)S(1)}, u32[]{:S(2)}, u32[]{:S(2)}) collective-permute-start(bf16[24,16,512]{2,1,0:T(8,128)(2,1)S(1)} %add_up.1), channel_id=1, source_target_pairs={{32,0},{64,32},{96,64},{0,96},{33,1},{65,33},{97,65},{1,97},{34,2}... | collective-permute-start | bytes 1179656 | tf_op jit(solution)/shard_map/ppermute | solution.py:409
  16.7 0.0 copy-done
  16.7 5.1 %turn_moment.1 = (s32[48]{0:T(128)S(4)}, s32[1]{0:T(128)S(4)}, f32[3,512,512]{2,1,0:T(8,128)S(1)}, f32[3,512,512]{2,1,0:T(8,128)S(1)}, bf16[3,512,512]{2,1,0:T(8...) custom-call(s32[4,48]{1,0:T(4,128)S(1)} %bitcast.6, f32[3,512,512]{2,1,0:T(8,128)} %mom_ref.3, f32[3,512,512]{2,1,0:T(8,128)} %var_ref.3, ...), custom_call_target="tpu_custom_call" | custom-call | flops 1610612736 | bytes 9437184 | tf_op jit(solution)/shard_map/turn_moment/pallas_call | solution.py:47
  21.9 0.2 collective-permute-done.3.a2
  22.1 0.0 collective-permute-done.4.b1
  22.1 8.4 %collective-permute-done.5.b2 = bf16[24,16,512]{2,1,0:T(8,128)(2,1)S(1)} collective-permute-done((bf16[24,16,512]{2,1,0:T(8,128)(2,1)S(1)}, bf16[24,16,512]{2,1,0:T(8,128)(2,1)S(1)}, u32[]{:S(2)}, u32[]{:S(2)}) %collective-permute-start.5) | collective-permute-done | bytes 393248 | tf_op jit(solution)/shard_map/ppermute | solution.py:408
  30.5 0.0 collective-permute-done.2.a1
  30.5 0.3 sum_and_place.1
  30.9 32.6 %all_to_all.10.grad.grad_ref = bf16[32,3,16,512]{3,2,1,0:T(8,128)(2,1)S(1)} all-to-all(bf16[32,3,16,512]{3,2,1,0:T(8,128)(2,1)S(1)} %bitcast.5), channel_id=1, replica_groups=mesh['dp'=4,'shard'=32] {'shard'}, dimensions={0} | all-to-all | bytes 3145728 | tf_op jit(solution)/shard_map/all_to_all | solution.py:398
  63.5 4.9 %owner_step.1 = bf16[32,3,16,512]{3,2,1,0:T(8,128)(2,1)} custom-call(bf16[32,3,16,512]{3,2,1,0:T(8,128)(2,1)S(1)} %all_to_all.10.grad.grad_ref, f32[3,512,512]{2,1,0:T(8,128)S(1)} %get-tuple-element.36.turned, f32[3,512,512]{2,1,0:T(8,128)S(1)} %get-tuple-element.37.var, bf16[3,512,512]{2,1,0:T(8,128)(2,1)S(1)} %get-tuple-element.38.left, ...), custom_call_target="tpu_custom_call" | custom-call | flops 3221225472 | bytes 6291456 | tf_op jit(solution)/shard_map/owner_step/pallas_call | solution.py:47
  68.4 3.8 %all-to-all-start.1 = ((bf16[32,3,16,512]{3,2,1,0:T(8,128)(2,1)}), bf16[32,3,16,512]{3,2,1,0:T(8,128)(2,1)S(1)}, u32[]{:S(2)}, u32[]{:S(2)}) async-start(bf16[32,3,16,512]{3,2,1,0:T(8,128)(2,1)} %owner_step.1), calls=%async_computation.1 | async-start | bytes 3145728 | tf_op jit(solution)/shard_map/all_to_all | solution.py:398
  72.2 7.8 %rest_of_state.1 = (f32[3,512,512]{2,1,0:T(8,128)}, bf16[3,512,512]{2,1,0:T(8,128)(2,1)}, bf16[3,512,512]{2,1,0:T(8,128)(2,1)}, f32[3,512,512]{2,1,0:T(8,128)}) custom-call(s32[1]{0:T(128)S(4)} %get-tuple-element.40.load_ref, bf16[32,3,16,512]{3,2,1,0:T(8,128)(2,1)S(1)} %all_to_all.10.grad.grad_ref, f32[3,512,512]{2,1,0:T(8,128)} %mom_ref.3, ...), custom_call_target="tpu_custom_call" | custom-call | flops 3221225472 | bytes 14155776 | tf_op jit(solution)/shard_map/rest_of_state/pallas_call | solution.py:47
  80.0 14.7 %all-to-all-done.1 = bf16[32,3,16,512]{3,2,1,0:T(8,128)(2,1)S(1)} async-done(((bf16[32,3,16,512]{3,2,1,0:T(8,128)(2,1)}), bf16[32,3,16,512]{3,2,1,0:T(8,128)(2,1)S(1)}, u32[]{:S(2)}, u32[]{:S(2)}) %all-to-all-start.1) | async-done | bytes 1572896 | tf_op jit(solution)/shard_map/all_to_all | solution.py:398
  94.8 0.9 take_blocks.1
Async XLA Ops:
  1.9 11.8 %collective-permute-start = (bf16[24,16,512]{2,1,0:T(8,128)(2,1)S(1)}, bf16[24,16,512]{2,1,0:T(8,128)(2,1)S(1)}, u32[]{:S(2)}, u32[]{:S(2)}) collective-permute-start(bf16[24,16,512]{2,1,0:T(8,128)(2,1)S(1)} %get-tuple-element.26), channel_id=1, source_target_pairs={{0,32},{32,64},{64,96},{96,0},{1,33},{33,65},{65,97},{97,1},{2,34}... | collective-permute-start | bytes 1179656 | tf_op jit(solution)/shard_map/ppermute | solution.py:408
  4.0 10.2 %collective-permute-start.1 = (bf16[24,16,512]{2,1,0:T(8,128)(2,1)S(1)}, bf16[24,16,512]{2,1,0:T(8,128)(2,1)S(1)}, u32[]{:S(2)}, u32[]{:S(2)}) collective-permute-start(bf16[24,16,512]{2,1,0:T(8,128)(2,1)S(1)} %get-tuple-element.32), channel_id=1, source_target_pairs={{32,0},{64,32},{96,64},{0,96},{33,1},{65,33},{97,65},{1,97},{34,2}... | collective-permute-start | bytes 1179656 | tf_op jit(solution)/shard_map/ppermute | solution.py:409
  7.2 9.6 %copy-start = (s32[4,48,1]{1,2,0:T(1,128)S(1)}, s32[4,48,1]{1,2,0:T(1,128)}, u32[]{:S(2)}) copy-start(s32[4,48,1]{1,2,0:T(1,128)} %param.9) | copy-start | bytes 2308
  7.2 14.9 %collective-permute-start.3 = (bf16[24,16,512]{2,1,0:T(8,128)(2,1)S(1)}, bf16[24,16,512]{2,1,0:T(8,128)(2,1)S(1)}, u32[]{:S(2)}, u32[]{:S(2)}) collective-permute-start(bf16[24,16,512]{2,1,0:T(8,128)(2,1)S(1)} %get-tuple-element.33), channel_id=1, source_target_pairs={{0,32},{32,64},{64,96},{96,0},{1,33},{33,65},{65,97},{97,1},{2,34}... | collective-permute-start | bytes 1179656 | tf_op jit(solution)/shard_map/ppermute | solution.py:408
  7.4 14.7 %collective-permute-start.4 = (bf16[24,16,512]{2,1,0:T(8,128)(2,1)S(1)}, bf16[24,16,512]{2,1,0:T(8,128)(2,1)S(1)}, u32[]{:S(2)}, u32[]{:S(2)}) collective-permute-start(bf16[24,16,512]{2,1,0:T(8,128)(2,1)S(1)} %get-tuple-element.34), channel_id=1, source_target_pairs={{32,0},{64,32},{96,64},{0,96},{33,1},{65,33},{97,65},{1,97},{34,2}... | collective-permute-start | bytes 1179656 | tf_op jit(solution)/shard_map/ppermute | solution.py:409
  13.8 16.7 %collective-permute-start.5 = (bf16[24,16,512]{2,1,0:T(8,128)(2,1)S(1)}, bf16[24,16,512]{2,1,0:T(8,128)(2,1)S(1)}, u32[]{:S(2)}, u32[]{:S(2)}) collective-permute-start(bf16[24,16,512]{2,1,0:T(8,128)(2,1)S(1)} %add_down.1), channel_id=1, source_target_pairs={{0,32},{32,64},{64,96},{96,0},{1,33},{33,65},{65,97},{97,1},{2,34}... | collective-permute-start | bytes 1179656 | tf_op jit(solution)/shard_map/ppermute | solution.py:408
  14.3 16.2 %collective-permute-start.2 = (bf16[24,16,512]{2,1,0:T(8,128)(2,1)S(1)}, bf16[24,16,512]{2,1,0:T(8,128)(2,1)S(1)}, u32[]{:S(2)}, u32[]{:S(2)}) collective-permute-start(bf16[24,16,512]{2,1,0:T(8,128)(2,1)S(1)} %add_up.1), channel_id=1, source_target_pairs={{32,0},{64,32},{96,64},{0,96},{33,1},{65,33},{97,65},{1,97},{34,2}... | collective-permute-start | bytes 1179656 | tf_op jit(solution)/shard_map/ppermute | solution.py:409
  68.4 26.3 %all-to-all-start.1 = ((bf16[32,3,16,512]{3,2,1,0:T(8,128)(2,1)}), bf16[32,3,16,512]{3,2,1,0:T(8,128)(2,1)S(1)}, u32[]{:S(2)}, u32[]{:S(2)}) async-start(bf16[32,3,16,512]{3,2,1,0:T(8,128)(2,1)} %owner_step.1), calls=%async_computation.1 | async-start | bytes 3145728 | tf_op jit(solution)/shard_map/all_to_all | solution.py:398
